TPU v7x, 32 devices: a whole 2x2x4 slice. The times are simulated.
32 devices in a mesh: mem: 4 (over z), lat: 8 (over y, x, core).
Axes of the slice: x: 2, y: 2, z: 4, core: 2. Of those that a mesh axis runs over, the one named last changes fastest.
Arguments:
- perturbations: bfloat16 [128, 3, 192, 1280], P('mem', None, 'lat'), may hold values from -0.5 to 0.5
- control: float32 [128, 48, 320], P('mem', 'lat'), may hold values from -6 to 6
- innovations: float32 [3, 192, 1280], P(None, 'lat'), may hold values from -6 to 6
- thresholds: float32 [3], replicated, may hold values from 0.4 to 1.5
Outputs:
- weights: float32 [128, 48, 320], P('mem', 'lat')
- increment: float32 [3, 192, 1280], P(None, 'lat', 'mem')
All inputs are finite; a program needn't handle non-finite values.
Results may differ from a plain program's by a relative error of at most 0.0003.
Values sent between devices are 32-bit elements; how exact they have to be, the bound alone decides.
No kernel may reach another device: no remote copies, remote signals or barrier semaphores. Data moves between devices by JAX's collectives and lax.ppermute only.
A program may use at most 64 MiB of HBM per device.

v0:
```python
import functools

import jax
import jax.numpy as jnp
import ml_dtypes
import numpy as np
from jax import lax
from jax.experimental import pallas as pl
from jax.experimental.pallas import tpu as pltpu
from jax.sharding import PartitionSpec as P

RATIO = 4
HALF = 5
STEPS = 2
REACH = HALF + 1
LANES = 128
WIN = 64
MARGIN = 32
FINE = RATIO * WIN
CHUNK = 8
F32 = jnp.float32
BF16 = jnp.bfloat16


def tent(distance):
    return max(0.0, 1.0 - abs(distance) / RATIO)


def smooth(distance):
    return (1.0 - abs(distance) / REACH) / 2 if abs(distance) <= HALF else 0.0


def window_table():
    fine = np.arange(FINE, dtype=np.float64)[None, :]
    coarse = np.arange(LANES, dtype=np.float64)[:, None] - MARGIN
    table = np.maximum(0.0, 1.0 - np.abs(fine + 0.5 - RATIO * coarse - RATIO / 2) / RATIO)
    return table.astype(ml_dtypes.bfloat16)


class Sizes:
    def __init__(self, mesh, perturbations, control):
        self.n_mem = mesh.shape["mem"]
        self.n_lat = mesh.shape["lat"]
        self.members = control.shape[0]
        self.rows = control.shape[1]
        self.cols = control.shape[2]
        self.vars = perturbations.shape[1]
        self.fine_rows = perturbations.shape[2]
        self.fine_cols = perturbations.shape[3]
        assert self.rows == REACH and self.cols % LANES == WIN
        assert self.fine_rows == RATIO * self.rows and self.fine_cols == RATIO * self.cols
        self.windows = self.cols // WIN
        self.ext = self.cols + 2 * MARGIN
        self.slab = self.rows * self.members
        self.full = self.cols // LANES
        self.packed = self.full * self.slab + self.slab // 2
        self.field_rows = self.vars * self.fine_rows
        self.share = self.fine_cols // self.n_mem
        self.share_full = self.share // LANES
        self.share_rem = self.share % LANES
        self.groups = LANES // self.share_rem if self.share_rem else 1
        self.rem_rows = -(-self.field_rows // 8 // self.groups) * 8 if self.share_rem else 0
        self.part_rows = self.share_full * self.field_rows + self.rem_rows


def lane(shape):
    return lax.broadcasted_iota(jnp.int32, shape, 1)


def half_turn(x):
    return pltpu.roll(x, WIN, 1)


def pack_slab(size, first, last, middle):
    rows = size.slab
    at = lane((rows, LANES))
    pieces = list(middle)
    pieces.append(jnp.where(at < LANES - MARGIN, last, first))
    half = rows // 2
    at = lane((half, LANES))
    inner = (at >= MARGIN) & (at < LANES - MARGIN)
    pieces.append(jnp.where(inner, first[:half], half_turn(first[half:])))
    return pieces


def unpack_slab(size, packed):
    rows = size.slab
    middle = [packed[i * rows : (i + 1) * rows] for i in range(size.full - 1)]
    mixed = packed[(size.full - 1) * rows : size.full * rows]
    rest = packed[size.full * rows :]
    rest = jnp.concatenate([rest, half_turn(rest)], axis=0)
    at = lane((rows, LANES))
    first = jnp.where(at < MARGIN, half_turn(mixed), jnp.where(at < LANES - MARGIN, rest, mixed))
    last = jnp.where(at < LANES - MARGIN, mixed, half_turn(rest))
    return [first] + middle + [last]


def tiles_of(ref, count):
    return [ref[:, i * LANES : (i + 1) * LANES] for i in range(count)]


def put_packed(out, pieces):
    at = 0
    for piece in pieces:
        out[at : at + piece.shape[0], :] = piece
        at += piece.shape[0]


def pack_ref(size, out, tiles):
    put_packed(out, pack_slab(size, tiles[0], tiles[-1], tiles[1:-1]))


def place():
    lat = lax.axis_index("lat")
    odd = lax.rem(lat, 2) == 1
    low = (lat > 0).astype(F32)
    high = (lat < lax.axis_size("lat") - 1).astype(F32)
    return odd, low, high


def sides(a, b):
    odd, low, high = place()
    lower = jnp.where(odd, a, b) * low
    upper = jnp.where(odd, b, a) * high
    return lower, upper


def step_length(scal_ref):
    total = jnp.sum(scal_ref[...].reshape(-1, 8, LANES), axis=0)
    grad_sq = total[0:1, 0:1]
    image_sq = total[1:2, 0:1]
    return grad_sq / (grad_sq + image_sq)


def enter_kernel(size, control_ref, own_ref, packed_ref):
    slabs = [control_ref[:, r, :] for r in range(size.rows)]
    x = jnp.concatenate(slabs, axis=0)
    x = jnp.concatenate([x[:, size.cols - MARGIN :], x, x[:, :MARGIN]], axis=1)
    own_ref[...] = x
    pack_ref(size, packed_ref, tiles_of(own_ref, size.ext // LANES))


def forward_kernel(size, own_ref, a_ref, b_ref, pert_ref, table_ref, *rest):
    outs = rest[: size.n_mem]
    ext_ref, coarse_ref, rows_ref, acc_ref, parts_ref = rest[size.n_mem :]
    step = pl.program_id(0)
    members = size.members
    n_tiles = size.ext // LANES
    fine_rows = size.fine_rows

    @pl.when(step == 0)
    def _():
        unused, low, high = place()
        lower, upper = sides(a_ref[...], b_ref[...])
        lower = unpack_slab(size, lower)
        upper = unpack_slab(size, upper)
        n = size.slab
        for e in range(n_tiles):
            cut = slice(e * LANES, (e + 1) * LANES)
            ext_ref[0:n, cut] = lower[e]
            ext_ref[n : 2 * n, cut] = own_ref[:, cut]
            ext_ref[2 * n : 3 * n, cut] = upper[e]
        for e in range(n_tiles):
            cut = slice(e * LANES, (e + 1) * LANES)
            for g in range(0, members, 8):
                held = [
                    ext_ref[k * members + g : k * members + g + 8, cut] for k in range(3 * REACH)
                ]
                for j in range(size.rows + 2):
                    total = None
                    for k in range(3 * REACH):
                        weight = smooth(j - 1 - (k - REACH))
                        if weight:
                            term = held[k] * weight
                            total = term if total is None else total + term
                    if j == 0:
                        total = total * low
                    if j == size.rows + 1:
                        total = total * high
                    coarse_ref[j * members + g : j * members + g + 8, cut] = total
        for t in range(size.windows):
            e = t // 2
            held = []
            for j in range(size.rows + 2):
                at = slice(j * members, (j + 1) * members)
                value = coarse_ref[at, e * LANES : (e + 1) * LANES]
                if t % 2:
                    other = coarse_ref[at, (e + 1) * LANES : (e + 2) * LANES]
                    value = half_turn(jnp.where(lane(value.shape) < WIN, other, value))
                held.append(value)
            for i in range(fine_rows):
                total = None
                for j in range(size.rows + 2):
                    weight = tent(i + 0.5 - RATIO * (j - 1) - RATIO / 2)
                    if weight:
                        term = held[j] * weight
                        total = term if total is None else total + term
                rows_ref[t, pl.ds(i, members, stride=fine_rows), :] = total
        acc_ref[...] = jnp.zeros_like(acc_ref)

    block = CHUNK * fine_rows
    first = pl.multiple_of(step * block, 8)
    for t in range(size.windows):
        x = rows_ref[t, pl.ds(first, block), :]
        head = x.astype(BF16)
        tail = (x - head.astype(F32)).astype(BF16)
        refined = jnp.dot(
            jnp.concatenate([head, tail], axis=1), table_ref[...], preferred_element_type=F32
        )
        cut = slice(t * FINE, (t + 1) * FINE)
        for v in range(size.vars):
            at = slice(v * fine_rows, (v + 1) * fine_rows)
            total = acc_ref[at, cut]
            for m in range(CHUNK):
                total = total + pert_ref[m, v, :, cut].astype(F32) * refined[
                    m * fine_rows : (m + 1) * fine_rows
                ]
            acc_ref[at, cut] = total

    @pl.when(step == pl.num_programs(0) - 1)
    def _():
        for q in range(size.n_mem):
            put_part(size, parts_ref.at[q], acc_ref, q * size.share)
        mine = lax.axis_index("mem")
        for d in range(size.n_mem):
            outs[d][...] = parts_ref[mine ^ d]


def field_tile(acc_ref, start):
    e, shift = start // LANES, start % LANES
    tile = acc_ref[:, e * LANES : (e + 1) * LANES]
    if shift == 0:
        return tile
    if (e + 1) * LANES < acc_ref.shape[1]:
        other = acc_ref[:, (e + 1) * LANES : (e + 2) * LANES]
        tile = jnp.where(lane(tile.shape) < shift, other, tile)
    return pltpu.roll(tile, LANES - shift, 1)


def put_part(size, out, acc_ref, start):
    rows = size.field_rows
    for j in range(size.share_full):
        out[j * rows : (j + 1) * rows, :] = field_tile(acc_ref, start + j * LANES)
    if size.share_rem:
        tile = field_tile(acc_ref, start + size.share_full * LANES)
        tile = jnp.where(lane(tile.shape) < size.share_rem, tile, 0.0)
        missing = size.rem_rows * size.groups - rows
        if missing:
            tile = jnp.concatenate([tile, jnp.zeros((missing, LANES), F32)], axis=0)
        total = None
        for g in range(size.groups):
            term = tile[g * size.rem_rows : (g + 1) * size.rem_rows]
            if g:
                term = pltpu.roll(term, g * size.share_rem, 1)
            total = term if total is None else total + term
        out[size.share_full * rows :, :] = total


def part_tiles(size, part):
    rows = size.field_rows
    tiles = [(part[j * rows : (j + 1) * rows], LANES) for j in range(size.share_full)]
    if size.share_rem:
        rest = part[size.share_full * rows :]
        stack = [rest]
        for g in range(1, size.groups):
            stack.append(pltpu.roll(rest, LANES - g * size.share_rem, 1))
        tiles.append((jnp.concatenate(stack, axis=0)[:rows], size.share_rem))
    return tiles


def total_kernel(count, *refs):
    parts, out_ref = refs[:count], refs[count]
    total = parts[0][...]
    for part in parts[1:]:
        total = total + part[...]
    out_ref[...] = total


def squares_kernel(count, *refs):
    parts, grad_ref, out_ref, scal_ref = refs[:count], refs[count], refs[count + 1], refs[count + 2]
    total = parts[0][...]
    for part in parts[1:]:
        total = total + part[...]
    out_ref[...] = total
    image_sq = jnp.sum(total * total)
    grad = grad_ref[...]
    grad_sq = jnp.sum(grad * grad)
    row = lax.broadcasted_iota(jnp.int32, (8, LANES), 0)
    tile = jnp.where(row == 0, grad_sq, jnp.where(row == 1, image_sq, 0.0))
    for i in range(scal_ref.shape[0] // 8):
        scal_ref[i * 8 : (i + 1) * 8, :] = tile


def adjoint_kernel(size, later, *refs):
    refs = list(refs)
    parts = [refs.pop(0) for i in range(size.n_mem)]
    if later:
        scal_ref = refs.pop(0)
        before_ref = refs.pop(0)
    innov_ref, limit_ref, pert_ref, table_ref = refs[:4]
    refs = refs[4:]
    a_ref, b_ref, own_ref = refs[:3]
    refs = refs[3:]
    if not later:
        field_ref = refs.pop(0)
    misfit_ref, parts_ref, cols_ref, coarse_ref, spread_ref = refs
    step = pl.program_id(0)
    members = size.members
    n_tiles = size.ext // LANES
    fine_rows = size.fine_rows

    @pl.when(step == 0)
    def _():
        mine = lax.axis_index("mem")
        for d in range(size.n_mem):
            parts_ref[mine ^ d] = parts[d][...]
        for q in range(size.n_mem):
            start = q * size.share
            for tile, width in part_tiles(size, parts_ref[q]):
                e, shift = start // LANES, start % LANES
                turned = pltpu.roll(tile, shift, 1) if shift else tile
                at = lane(turned.shape)
                cut = slice(e * LANES, (e + 1) * LANES)
                if shift == 0 and width == LANES:
                    misfit_ref[:, cut] = turned
                else:
                    inside = (at >= shift) & (at < shift + width)
                    misfit_ref[:, cut] = jnp.where(inside, turned, misfit_ref[:, cut])
                if shift + width > LANES:
                    cut = slice((e + 1) * LANES, (e + 2) * LANES)
                    inside = at < shift + width - LANES
                    misfit_ref[:, cut] = jnp.where(inside, turned, misfit_ref[:, cut])
                start += width
        value = misfit_ref[...]
        if later:
            value = before_ref[...] - step_length(scal_ref) * value
        else:
            field_ref[...] = value
        for v in range(size.vars):
            at = slice(v * fine_rows, (v + 1) * fine_rows)
            limit = limit_ref[v]
            misfit_ref[at, :] = jnp.clip(value[at] - innov_ref[v], -limit, limit)

    block = CHUNK * fine_rows
    first = pl.multiple_of(step * block, 8)
    tops = [None] * n_tiles
    for t in range(size.windows):
        cut = slice(t * FINE, (t + 1) * FINE)
        mis = [misfit_ref[v * fine_rows : (v + 1) * fine_rows, cut] for v in range(size.vars)]
        weighted = []
        for m in range(CHUNK):
            total = pert_ref[m, 0, :, cut].astype(F32) * mis[0]
            for v in range(1, size.vars):
                total = total + pert_ref[m, v, :, cut].astype(F32) * mis[v]
            weighted.append(total)
        x = jnp.concatenate(weighted, axis=0)
        head = x.astype(BF16)
        tail = (x - head.astype(F32)).astype(BF16)
        columns = jnp.dot(
            jnp.concatenate([head, tail], axis=1), table_ref[...], preferred_element_type=F32
        )
        e = t // 2
        if t % 2 == 0:
            tops[e] = columns if tops[e] is None else tops[e] + columns
        else:
            turned = half_turn(columns)
            at = lane(turned.shape)
            tops[e] = tops[e] + jnp.where(at >= WIN, turned, 0.0)
            tops[e + 1] = jnp.where(at < WIN, turned, 0.0)
    for e in range(n_tiles):
        cols_ref[e, pl.ds(first, block), :] = tops[e]

    @pl.when(step == pl.num_programs(0) - 1)
    def _():
        odd, low, high = place()
        for e in range(n_tiles):
            cut = slice(e * LANES, (e + 1) * LANES)
            sums = [None] * (size.rows + 2)
            for i in range(fine_rows):
                value = cols_ref[e, pl.ds(i, members, stride=fine_rows), :]
                for j in range(size.rows + 2):
                    weight = tent(i + 0.5 - RATIO * (j - 1) - RATIO / 2)
                    if weight:
                        term = value * weight
                        sums[j] = term if sums[j] is None else sums[j] + term
            sums[0] = sums[0] * low
            sums[-1] = sums[-1] * high
            for j in range(size.rows + 2):
                coarse_ref[j * members : (j + 1) * members, cut] = sums[j]
        head = coarse_ref[:, 0:LANES]
        tail = coarse_ref[:, (n_tiles - 1) * LANES :]
        at = lane(head.shape)
        turned_head, turned_tail = half_turn(head), half_turn(tail)
        coarse_ref[:, 0:LANES] = head + jnp.where(at < WIN, turned_tail, 0.0)
        coarse_ref[:, (n_tiles - 1) * LANES :] = tail + jnp.where(at >= WIN, turned_head, 0.0)
        for e in range(n_tiles):
            cut = slice(e * LANES, (e + 1) * LANES)
            for g in range(0, members, 8):
                held = [
                    coarse_ref[j * members + g : j * members + g + 8, cut]
                    for j in range(size.rows + 2)
                ]
                for k in range(3 * REACH):
                    total = None
                    for j in range(size.rows + 2):
                        weight = smooth(j - 1 - (k - REACH))
                        if weight:
                            term = held[j] * weight
                            total = term if total is None else total + term
                    spread_ref[k * members + g : k * members + g + 8, cut] = total
        n = size.slab

        def packed_of(part):
            tiles = [
                spread_ref[part * n : (part + 1) * n, e * LANES : (e + 1) * LANES]
                for e in range(n_tiles)
            ]
            return pack_slab(size, tiles[0], tiles[-1], tiles[1:-1])

        lower, upper = packed_of(0), packed_of(2)
        own_ref[...] = spread_ref[n : 2 * n, :]
        put_packed(a_ref, [jnp.where(odd, x, y) for x, y in zip(lower, upper)])
        put_packed(b_ref, [jnp.where(odd, y, x) for x, y in zip(lower, upper)])


def gradient_kernel(size, later, *refs):
    refs = list(refs)
    own_ref, a_ref, b_ref, weights_ref = refs[:4]
    refs = refs[4:]
    weights = weights_ref[...]
    if later:
        scal_ref, before_ref = refs.pop(0), refs.pop(0)
        weights = weights - step_length(scal_ref) * before_ref[...]
    grad_ref, packed_ref = refs[:2]
    if later:
        refs[2][...] = weights
    lower, upper = sides(a_ref[...], b_ref[...])
    arrived = unpack_slab(size, lower + upper)
    for e in range(size.ext // LANES):
        cut = slice(e * LANES, (e + 1) * LANES)
        grad_ref[:, cut] = weights[:, cut] + own_ref[:, cut] + arrived[e]
    pack_ref(size, packed_ref, tiles_of(grad_ref, size.ext // LANES))


def leave_kernel(size, weights_ref, grad_ref, field_ref, image0_ref, scal0_ref, image1_ref,
                 scal1_ref, out_weights_ref, out_field_ref):
    second = step_length(scal1_ref)
    weights = weights_ref[...] - second * grad_ref[...]
    n_tiles = size.ext // LANES
    tiles = [weights[:, e * LANES : (e + 1) * LANES] for e in range(n_tiles)]
    for e in range(n_tiles):
        tile = tiles[e]
        if e + 1 < n_tiles:
            tile = jnp.where(lane(tile.shape) < MARGIN, tiles[e + 1], tile)
        tile = pltpu.roll(tile, LANES - MARGIN, 1)
        start = e * LANES
        width = min(LANES, size.cols - start)
        for r in range(size.rows):
            rows = slice(r * size.members, (r + 1) * size.members)
            out_weights_ref[:, r, start : start + width] = tile[rows, :width]
    field = field_ref[...] - step_length(scal0_ref) * image0_ref[...] - second * image1_ref[...]
    start = 0
    for tile, width in part_tiles(size, field):
        for v in range(size.vars):
            rows = slice(v * size.fine_rows, (v + 1) * size.fine_rows)
            out_field_ref[v, :, start : start + width] = tile[rows, :width]
        start += width


def whole():
    return pl.BlockSpec(memory_space=pltpu.VMEM)


def params():
    return pltpu.CompilerParams(vmem_limit_bytes=24 * 1024 * 1024)


def array(*shape):
    return jax.ShapeDtypeStruct(shape, F32)


def call(kernel, outs, *args):
    return pl.pallas_call(
        kernel,
        out_shape=outs,
        in_specs=[whole()] * len(args),
        out_specs=jax.tree.map(lambda unused: whole(), outs),
        compiler_params=params(),
    )(*args)


def per_device(mesh, perturbations, control, innovations, thresholds):
    size = Sizes(mesh, perturbations, control)
    n_mem, n_lat, members = size.n_mem, size.n_lat, size.members
    devices = n_mem * n_lat
    table = window_table()
    up_table = jnp.asarray(np.concatenate([table, table], axis=0))
    down_table = jnp.asarray(np.concatenate([table.T, table.T], axis=0))
    pairs = [(i, i ^ 1) for i in range(n_lat)]
    cross = [(i, (i - 1 if i % 2 == 0 else i + 1) % n_lat) for i in range(n_lat)]
    steps = members // CHUNK
    slab = array(size.slab, size.ext)
    packed = array(size.packed, LANES)
    part = array(size.part_rows, LANES)
    scal = array(devices * 8, LANES)

    def same(*shape):
        return pl.BlockSpec(shape, lambda i: (0,) * len(shape))

    pert_spec = pl.BlockSpec(
        (CHUNK, size.vars, size.fine_rows, size.fine_cols), lambda i: (i, 0, 0, 0)
    )

    def swap(to_a, to_b):
        return lax.ppermute(to_a, "lat", pairs), lax.ppermute(to_b, "lat", cross)

    def between(parts, d):
        return lax.ppermute(parts, "mem", [(i, i ^ d) for i in range(n_mem)])

    far_first = sorted(range(1, n_mem), key=lambda d: -d)

    def reduced(outs):
        moved = {d: between(outs[d], d) for d in far_first}
        return [outs[0]] + [moved[d] for d in range(1, n_mem)]

    def gathered(own):
        moved = {d: between(own, d) for d in far_first}
        return [own] + [moved[d] for d in range(1, n_mem)]

    def forward(own, a, b):
        return pl.pallas_call(
            functools.partial(forward_kernel, size),
            grid=(steps,),
            out_shape=[part] * n_mem,
            in_specs=[
                same(size.slab, size.ext),
                same(size.packed, LANES),
                same(size.packed, LANES),
                pert_spec,
                same(2 * LANES, FINE),
            ],
            out_specs=[same(size.part_rows, LANES)] * n_mem,
            scratch_shapes=[
                pltpu.VMEM((3 * size.slab, size.ext), F32),
                pltpu.VMEM(((size.rows + 2) * members, size.ext), F32),
                pltpu.VMEM((size.windows, members * size.fine_rows, LANES), F32),
                pltpu.VMEM((size.field_rows, size.fine_cols), F32),
                pltpu.VMEM((n_mem, size.part_rows, LANES), F32),
            ],
            compiler_params=params(),
        )(own, a, b, perturbations, up_table)

    def adjoint(parts, scal_all=None, before=None):
        later = scal_all is not None
        field = array(size.field_rows, size.fine_cols)
        outs = [packed, packed, slab] + ([] if later else [field])
        out_specs = [
            same(size.packed, LANES),
            same(size.packed, LANES),
            same(size.slab, size.ext),
        ] + ([] if later else [same(size.field_rows, size.fine_cols)])
        args = list(parts)
        in_specs = [same(size.part_rows, LANES)] * n_mem
        if later:
            args += [scal_all, before]
            in_specs += [same(devices * 8, LANES), same(size.field_rows, size.fine_cols)]
        args += [innovations, thresholds, perturbations, down_table]
        in_specs += [
            same(size.vars, size.fine_rows, size.fine_cols),
            pl.BlockSpec(memory_space=pltpu.SMEM),
            pert_spec,
            same(2 * FINE, LANES),
        ]
        n_tiles = size.ext // LANES
        return pl.pallas_call(
            functools.partial(adjoint_kernel, size, later),
            grid=(steps,),
            out_shape=outs,
            in_specs=in_specs,
            out_specs=out_specs,
            scratch_shapes=[
                pltpu.VMEM((size.field_rows, size.fine_cols), F32),
                pltpu.VMEM((n_mem, size.part_rows, LANES), F32),
                pltpu.VMEM((n_tiles, members * size.fine_rows, LANES), F32),
                pltpu.VMEM(((size.rows + 2) * members, size.ext), F32),
                pltpu.VMEM((3 * size.slab, size.ext), F32),
            ],
            compiler_params=params(),
        )(*args)

    def everywhere(tile):
        moved = lax.all_to_all(tile.reshape(devices, 8, LANES), ("mem", "lat"), 0, 0)
        return moved.reshape(devices * 8, LANES)

    own, sent = call(functools.partial(enter_kernel, size), [slab, packed], control)
    parts = reduced(forward(own, *swap(sent, sent)))
    field0 = call(functools.partial(total_kernel, n_mem), part, *parts)
    to_a, to_b, spread, field_all = adjoint(gathered(field0))
    grad0, sent = call(
        functools.partial(gradient_kernel, size, False),
        [slab, packed],
        spread,
        *swap(to_a, to_b),
        own,
    )
    parts = reduced(forward(grad0, *swap(sent, sent)))
    image0, scal0 = call(
        functools.partial(squares_kernel, n_mem), [part, scal], *parts, sent
    )
    images = gathered(image0)
    scal0 = everywhere(scal0)
    to_a, to_b, spread = adjoint(images, scal0, field_all)
    grad1, sent, weights1 = call(
        functools.partial(gradient_kernel, size, True),
        [slab, packed, slab],
        spread,
        *swap(to_a, to_b),
        own,
        scal0,
        grad0,
    )
    parts = reduced(forward(grad1, *swap(sent, sent)))
    image1, scal1 = call(
        functools.partial(squares_kernel, n_mem), [part, scal], *parts, sent
    )
    scal1 = everywhere(scal1)
    return tuple(
        call(
            functools.partial(leave_kernel, size),
            [
                array(members, size.rows, size.cols),
                array(size.vars, size.fine_rows, size.share),
            ],
            weights1,
            grad1,
            field0,
            image0,
            scal0,
            image1,
            scal1,
        )
    )


def solution(mesh):
    return jax.shard_map(
        functools.partial(per_device, mesh),
        mesh=mesh,
        in_specs=(P("mem", None, "lat", None), P("mem", "lat", None), P(None, "lat", None), P()),
        out_specs=(P("mem", "lat", None), P(None, "lat", "mem")),
        check_vma=False,
    )
```

profile of v0, /device:TPU:0, one launch (start us, length us, event | category | flops | bytes accessed | tf_op | source)
XLA Modules:
  0.0 144.9 jit_solution(11824165708740770198)
XLA Ops:
  2.1 3.4 %collective-permute-start.1 = (f32[480,128]{1,0:T(8,128)S(1)}, f32[480,128]{1,0:T(8,128)S(1)}, u32[]{:S(2)}, u32[]{:S(2)}) collective-permute-start(f32[480,128]{1,0:T(8,128)S(1)} %get-tuple-element.33), channel_id=1, source_target_pairs={{0,7},{1,2},{2,1},{3,4},{4,3},{5,6},{6,5},{7,0},{8,15},{9,10},{10,... | collective-permute-start | bytes 737288 | tf_op jit(solution)/shard_map/ppermute | solution.py:515
  5.5 5.7 %collective-permute-done.1.b_ref = f32[480,128]{1,0:T(8,128)S(1)} collective-permute-done((f32[480,128]{1,0:T(8,128)S(1)}, f32[480,128]{1,0:T(8,128)S(1)}, u32[]{:S(2)}, u32[]{:S(2)}) %collective-permute-start.1) | collective-permute-done | bytes 245792 | tf_op jit(solution)/shard_map/ppermute | solution.py:515
  11.2 2.7 %copy-done = bf16[32,3,24,1280]{3,2,1,0:T(8,128)(2,1)S(1)} copy-done((bf16[32,3,24,1280]{3,2,1,0:T(8,128)(2,1)S(1)}, bf16[32,3,24,1280]{3,2,1,0:T(8,128)(2,1)}, u32[]{:S(2)}) %copy-start) | copy-done | bytes 5898264
  14.8 2.9 %shard_map.78 = (f32[184,128]{1,0:T(8,128)S(1)}, f32[184,128]{1,0:T(8,128)S(1)}, f32[184,128]{1,0:T(8,128)S(1)}, f32[184,128]{1,0:T(8,128)S(1)}) custom-call(f32[192,384]{1,0:T(8,128)S(1)} %get-tuple-element.32.own_ref.refs_3_, f32[480,128]{1,0:T(8,128)S(1)} %collective-permute-done.a_ref, f32[480,128]{1,0:T(8,128)S(1)} %collective-permute-done.1.b_ref, ...), custom_call_target="tpu_custom_call" | custom-call | tf_op jit(solution)/shard_map/pallas_call | solution.py:531
  17.7 3.1 %collective-permute-start.2 = (f32[184,128]{1,0:T(8,128)S(1)}, f32[184,128]{1,0:T(8,128)S(1)}, u32[]{:S(2)}, u32[]{:S(2)}) collective-permute-start(f32[184,128]{1,0:T(8,128)S(1)} %get-tuple-element.35), channel_id=1, source_target_pairs={{0,8},{8,0},{16,24},{24,16},{1,9},{9,1},{17,25},{25,17},{2,10},{10... | collective-permute-start | bytes 282632 | tf_op jit(solution)/shard_map/ppermute | solution.py:518
  20.8 2.6 %collective-permute-start.3 = (f32[184,128]{1,0:T(8,128)S(1)}, f32[184,128]{1,0:T(8,128)S(1)}, u32[]{:S(2)}, u32[]{:S(2)}) collective-permute-start(f32[184,128]{1,0:T(8,128)S(1)} %get-tuple-element.36), channel_id=1, source_target_pairs={{0,16},{8,24},{16,0},{24,8},{1,17},{9,25},{17,1},{25,9},{2,18},{10... | collective-permute-start | bytes 282632 | tf_op jit(solution)/shard_map/ppermute | solution.py:518
  24.3 4.2 %collective-permute-done.3.refs_2_ = f32[184,128]{1,0:T(8,128)S(1)} collective-permute-done((f32[184,128]{1,0:T(8,128)S(1)}, f32[184,128]{1,0:T(8,128)S(1)}, u32[]{:S(2)}, u32[]{:S(2)}) %collective-permute-start.3) | collective-permute-done | bytes 94240 | tf_op jit(solution)/shard_map/ppermute | solution.py:518
  29.9 2.2 %collective-permute-start.7 = (f32[184,128]{1,0:T(8,128)S(1)}, f32[184,128]{1,0:T(8,128)S(1)}, u32[]{:S(2)}, u32[]{:S(2)}) collective-permute-start(f32[184,128]{1,0:T(8,128)S(1)} %shard_map.79.refs_0_.field_ref), channel_id=1, source_target_pairs={{0,24},{8,16},{16,8},{24,0},{1,25},{9,17},{17,9},{25,1},{2,26},{10... | collective-permute-start | bytes 282632 | tf_op jit(solution)/shard_map/ppermute | solution.py:518
  32.7 1.7 %collective-permute-start.5 = (f32[184,128]{1,0:T(8,128)S(1)}, f32[184,128]{1,0:T(8,128)S(1)}, u32[]{:S(2)}, u32[]{:S(2)}) collective-permute-start(f32[184,128]{1,0:T(8,128)S(1)} %shard_map.79.refs_0_.field_ref), channel_id=1, source_target_pairs={{0,8},{8,0},{16,24},{24,16},{1,9},{9,1},{17,25},{25,17},{2,10},{10... | collective-permute-start | bytes 282632 | tf_op jit(solution)/shard_map/ppermute | solution.py:518
  34.3 2.2 %collective-permute-done.7.refs_3_ = f32[184,128]{1,0:T(8,128)S(1)} collective-permute-done((f32[184,128]{1,0:T(8,128)S(1)}, f32[184,128]{1,0:T(8,128)S(1)}, u32[]{:S(2)}, u32[]{:S(2)}) %collective-permute-start.7) | collective-permute-done | bytes 94240 | tf_op jit(solution)/shard_map/ppermute | solution.py:518
  36.5 2.6 %collective-permute-done.6.refs_2_ = f32[184,128]{1,0:T(8,128)S(1)} collective-permute-done((f32[184,128]{1,0:T(8,128)S(1)}, f32[184,128]{1,0:T(8,128)S(1)}, u32[]{:S(2)}, u32[]{:S(2)}) %collective-permute-start.6) | collective-permute-done | bytes 94240 | tf_op jit(solution)/shard_map/ppermute | solution.py:518
  39.1 3.7 %shard_map.80 = (f32[480,128]{1,0:T(8,128)S(1)}, f32[480,128]{1,0:T(8,128)S(1)}, f32[192,384]{1,0:T(8,128)S(1)}, f32[72,1280]{1,0:T(8,128)S(1)}) custom-call(f32[184,128]{1,0:T(8,128)S(1)} %shard_map.79.refs_0_.field_ref, f32[184,128]{1,0:T(8,128)S(1)} %collective-permute-done.5.refs_1_, f32[184,128]{1,0:T(8,128)S(1)} %collective-permute-done.6.refs_2_, ...), custom_call_target="tpu_custom_call" | custom-call | tf_op jit(solution)/shard_map/pallas_call | solution.py:575
  42.9 3.7 %collective-permute-start.9 = (f32[480,128]{1,0:T(8,128)S(1)}, f32[480,128]{1,0:T(8,128)S(1)}, u32[]{:S(2)}, u32[]{:S(2)}) collective-permute-start(f32[480,128]{1,0:T(8,128)S(1)} %get-tuple-element.40), channel_id=1, source_target_pairs={{0,7},{1,2},{2,1},{3,4},{4,3},{5,6},{6,5},{7,0},{8,15},{9,10},{10,... | collective-permute-start | bytes 737288 | tf_op jit(solution)/shard_map/ppermute | solution.py:515
  46.6 6.1 %collective-permute-done.9.refs_2_ = f32[480,128]{1,0:T(8,128)S(1)} collective-permute-done((f32[480,128]{1,0:T(8,128)S(1)}, f32[480,128]{1,0:T(8,128)S(1)}, u32[]{:S(2)}, u32[]{:S(2)}) %collective-permute-start.9) | collective-permute-done | bytes 245792 | tf_op jit(solution)/shard_map/ppermute | solution.py:515
  52.9 2.9 %collective-permute-start.11 = (f32[480,128]{1,0:T(8,128)S(1)}, f32[480,128]{1,0:T(8,128)S(1)}, u32[]{:S(2)}, u32[]{:S(2)}) collective-permute-start(f32[480,128]{1,0:T(8,128)S(1)} %get-tuple-element.42.refs_4_), channel_id=1, source_target_pairs={{0,7},{1,2},{2,1},{3,4},{4,3},{5,6},{6,5},{7,0},{8,15},{9,10},{10,... | collective-permute-start | bytes 737288 | tf_op jit(solution)/shard_map/ppermute | solution.py:515
  55.8 6.1 %collective-permute-done.11.b_ref = f32[480,128]{1,0:T(8,128)S(1)} collective-permute-done((f32[480,128]{1,0:T(8,128)S(1)}, f32[480,128]{1,0:T(8,128)S(1)}, u32[]{:S(2)}, u32[]{:S(2)}) %collective-permute-start.11) | collective-permute-done | bytes 245792 | tf_op jit(solution)/shard_map/ppermute | solution.py:515
  61.9 3.0 %shard_map.82 = (f32[184,128]{1,0:T(8,128)S(1)}, f32[184,128]{1,0:T(8,128)S(1)}, f32[184,128]{1,0:T(8,128)S(1)}, f32[184,128]{1,0:T(8,128)S(1)}) custom-call(f32[192,384]{1,0:T(8,128)S(1)} %get-tuple-element.41.own_ref.refs_5_, f32[480,128]{1,0:T(8,128)S(1)} %collective-permute-done.10.a_ref, f32[480,128]{1,0:T(8,128)S(1)} %collective-permute-done.11.b_ref, ...), custom_call_target="tpu_custom_call" | custom-call | tf_op jit(solution)/shard_map/pallas_call | solution.py:531
  66.2 3.3 %collective-permute-start.14 = (f32[184,128]{1,0:T(8,128)S(1)}, f32[184,128]{1,0:T(8,128)S(1)}, u32[]{:S(2)}, u32[]{:S(2)}) collective-permute-start(f32[184,128]{1,0:T(8,128)S(1)} %get-tuple-element.46), channel_id=1, source_target_pairs={{0,24},{8,16},{16,8},{24,0},{1,25},{9,17},{17,9},{25,1},{2,26},{10... | collective-permute-start | bytes 282632 | tf_op jit(solution)/shard_map/ppermute | solution.py:518
  71.0 4.6 %collective-permute-done.13.refs_2_ = f32[184,128]{1,0:T(8,128)S(1)} collective-permute-done((f32[184,128]{1,0:T(8,128)S(1)}, f32[184,128]{1,0:T(8,128)S(1)}, u32[]{:S(2)}, u32[]{:S(2)}) %collective-permute-start.13) | collective-permute-done | bytes 94240 | tf_op jit(solution)/shard_map/ppermute | solution.py:518
  76.5 2.8 %all-to-all-start = ((f32[32,8,128]{2,1,0:T(8,128)}), f32[32,8,128]{2,1,0:T(8,128)S(1)}, u32[]{:S(2)}, u32[]{:S(2)}) async-start(f32[32,8,128]{2,1,0:T(8,128)} %bitcast), calls=%async_computation | async-start | bytes 262144 | tf_op jit(solution)/shard_map/all_to_all | solution.py:592
  79.3 3.7 %collective-permute-start.17 = (f32[184,128]{1,0:T(8,128)S(1)}, f32[184,128]{1,0:T(8,128)S(1)}, u32[]{:S(2)}, u32[]{:S(2)}) collective-permute-start(f32[184,128]{1,0:T(8,128)S(1)} %get-tuple-element.47.refs_0_.image0_ref), channel_id=1, source_target_pairs={{0,24},{8,16},{16,8},{24,0},{1,25},{9,17},{17,9},{25,1},{2,26},{10... | collective-permute-start | bytes 282632 | tf_op jit(solution)/shard_map/ppermute | solution.py:518
  83.8 4.9 %collective-permute-done.17.refs_3_ = f32[184,128]{1,0:T(8,128)S(1)} collective-permute-done((f32[184,128]{1,0:T(8,128)S(1)}, f32[184,128]{1,0:T(8,128)S(1)}, u32[]{:S(2)}, u32[]{:S(2)}) %collective-permute-start.17) | collective-permute-done | bytes 94240 | tf_op jit(solution)/shard_map/ppermute | solution.py:518
  88.6 5.3 %collective-permute-done.16.refs_2_ = f32[184,128]{1,0:T(8,128)S(1)} collective-permute-done((f32[184,128]{1,0:T(8,128)S(1)}, f32[184,128]{1,0:T(8,128)S(1)}, u32[]{:S(2)}, u32[]{:S(2)}) %collective-permute-start.16) | collective-permute-done | bytes 94240 | tf_op jit(solution)/shard_map/ppermute | solution.py:518
  94.0 2.7 %copy-done.2 = bf16[32,3,24,1280]{3,2,1,0:T(8,128)(2,1)S(1)} copy-done((bf16[32,3,24,1280]{3,2,1,0:T(8,128)(2,1)S(1)}, bf16[32,3,24,1280]{3,2,1,0:T(8,128)(2,1)}, u32[]{:S(2)}) %copy-start.2) | copy-done | bytes 5898264
  97.6 3.5 %shard_map.84 = (f32[480,128]{1,0:T(8,128)S(1)}, f32[480,128]{1,0:T(8,128)S(1)}, f32[192,384]{1,0:T(8,128)S(1)}) custom-call(f32[184,128]{1,0:T(8,128)S(1)} %get-tuple-element.47.refs_0_.image0_ref, f32[184,128]{1,0:T(8,128)S(1)} %collective-permute-done.15.refs_1_, f32[184,128]{1,0:T(8,128)S(1)} %collective-permute-done.16.refs_2_, ...), custom_call_target="tpu_custom_call" | custom-call | tf_op jit(solution)/shard_map/pallas_call | solution.py:575
  101.3 2.5 %collective-permute-start.19 = (f32[480,128]{1,0:T(8,128)S(1)}, f32[480,128]{1,0:T(8,128)S(1)}, u32[]{:S(2)}, u32[]{:S(2)}) collective-permute-start(f32[480,128]{1,0:T(8,128)S(1)} %get-tuple-element.52), channel_id=1, source_target_pairs={{0,7},{1,2},{2,1},{3,4},{4,3},{5,6},{6,5},{7,0},{8,15},{9,10},{10,... | collective-permute-start | bytes 737288 | tf_op jit(solution)/shard_map/ppermute | solution.py:515
  103.8 6.2 %collective-permute-done.19.refs_2_ = f32[480,128]{1,0:T(8,128)S(1)} collective-permute-done((f32[480,128]{1,0:T(8,128)S(1)}, f32[480,128]{1,0:T(8,128)S(1)}, u32[]{:S(2)}, u32[]{:S(2)}) %collective-permute-start.19) | collective-permute-done | bytes 245792 | tf_op jit(solution)/shard_map/ppermute | solution.py:515
  111.7 7.7 %collective-permute-done.21.b_ref = f32[480,128]{1,0:T(8,128)S(1)} collective-permute-done((f32[480,128]{1,0:T(8,128)S(1)}, f32[480,128]{1,0:T(8,128)S(1)}, u32[]{:S(2)}, u32[]{:S(2)}) %collective-permute-start.21) | collective-permute-done | bytes 245792 | tf_op jit(solution)/shard_map/ppermute | solution.py:515
  119.4 2.9 %shard_map.86 = (f32[184,128]{1,0:T(8,128)S(1)}, f32[184,128]{1,0:T(8,128)S(1)}, f32[184,128]{1,0:T(8,128)S(1)}, f32[184,128]{1,0:T(8,128)S(1)}) custom-call(f32[192,384]{1,0:T(8,128)S(1)} %get-tuple-element.54.own_ref.grad_ref, f32[480,128]{1,0:T(8,128)S(1)} %collective-permute-done.20.a_ref, f32[480,128]{1,0:T(8,128)S(1)} %collective-permute-done.21.b_ref, ...), custom_call_target="tpu_custom_call" | custom-call | tf_op jit(solution)/shard_map/pallas_call | solution.py:531
  124.0 2.7 %collective-permute-start.24 = (f32[184,128]{1,0:T(8,128)S(1)}, f32[184,128]{1,0:T(8,128)S(1)}, u32[]{:S(2)}, u32[]{:S(2)}) collective-permute-start(f32[184,128]{1,0:T(8,128)S(1)} %get-tuple-element.59), channel_id=1, source_target_pairs={{0,24},{8,16},{16,8},{24,0},{1,25},{9,17},{17,9},{25,1},{2,26},{10... | collective-permute-start | bytes 282632 | tf_op jit(solution)/shard_map/ppermute | solution.py:518
  126.9 4.7 %collective-permute-done.23.refs_2_ = f32[184,128]{1,0:T(8,128)S(1)} collective-permute-done((f32[184,128]{1,0:T(8,128)S(1)}, f32[184,128]{1,0:T(8,128)S(1)}, u32[]{:S(2)}, u32[]{:S(2)}) %collective-permute-start.23) | collective-permute-done | bytes 94240 | tf_op jit(solution)/shard_map/ppermute | solution.py:518
  131.8 11.4 %all_to_all.10 = f32[32,8,128]{2,1,0:T(8,128)S(1)} all-to-all(f32[32,8,128]{2,1,0:T(8,128)S(1)} %bitcast.10), channel_id=1, replica_groups=mesh['mem'=4,'lat'=8] {'mem','lat'}, dimensions={0} | all-to-all | bytes 262144 | tf_op jit(solution)/shard_map/all_to_all | solution.py:592
  (60 shorter events, 16.6 us)
Async XLA Ops:
  0.6 38.5 %copy-start.6 = (bf16[512,128]{1,0:T(8,128)(2,1)S(1)}, bf16[512,128]{1,0:T(8,128)(2,1)}, u32[]{:S(2)}) copy-start(bf16[512,128]{1,0:T(8,128)(2,1)} %constant.5.clone.refs_7_.refs_9_) | copy-start | bytes 393220
  0.6 38.5 %copy-start.9 = (f32[3]{0:T(128)S(1)}, f32[3]{0:T(128)}, u32[]{:S(2)}) copy-start(f32[3]{0:T(128)} %refs_7_.2) | copy-start | bytes 40
  0.7 38.5 %copy-start.3 = (f32[3,24,1280]{2,1,0:T(8,128)S(1)}, f32[3,24,1280]{2,1,0:T(8,128)}, u32[]{:S(2)}) copy-start(f32[3,24,1280]{2,1,0:T(8,128)} %refs_6_.3) | copy-start | bytes 1105924
  2.1 9.1 %collective-permute-start.1 = (f32[480,128]{1,0:T(8,128)S(1)}, f32[480,128]{1,0:T(8,128)S(1)}, u32[]{:S(2)}, u32[]{:S(2)}) collective-permute-start(f32[480,128]{1,0:T(8,128)S(1)} %get-tuple-element.33), channel_id=1, source_target_pairs={{0,7},{1,2},{2,1},{3,4},{4,3},{5,6},{6,5},{7,0},{8,15},{9,10},{10,... | collective-permute-start | bytes 737288 | tf_op jit(solution)/shard_map/ppermute | solution.py:515
  5.5 5.7 %collective-permute-start = (f32[480,128]{1,0:T(8,128)S(1)}, f32[480,128]{1,0:T(8,128)S(1)}, u32[]{:S(2)}, u32[]{:S(2)}) collective-permute-start(f32[480,128]{1,0:T(8,128)S(1)} %get-tuple-element.33), channel_id=1, source_target_pairs={{0,1},{1,0},{2,3},{3,2},{4,5},{5,4},{6,7},{7,6},{8,9},{9,8},{10,11... | collective-permute-start | bytes 737288 | tf_op jit(solution)/shard_map/ppermute | solution.py:515
  14.8 24.3 %copy-start.1 = (bf16[32,3,24,1280]{3,2,1,0:T(8,128)(2,1)S(1)}, bf16[32,3,24,1280]{3,2,1,0:T(8,128)(2,1)}, u32[]{:S(2)}) copy-start(bf16[32,3,24,1280]{3,2,1,0:T(8,128)(2,1)} %pert_ref.5) | copy-start | bytes 17694724
  14.8 47.1 %copy-start.5 = (bf16[256,256]{1,0:T(8,128)(2,1)S(1)}, bf16[256,256]{1,0:T(8,128)(2,1)}, u32[]{:S(2)}) copy-start(bf16[256,256]{1,0:T(8,128)(2,1)} %constant.4.clone.table_ref) | copy-start | bytes 393220
  17.7 6.6 %collective-permute-start.2 = (f32[184,128]{1,0:T(8,128)S(1)}, f32[184,128]{1,0:T(8,128)S(1)}, u32[]{:S(2)}, u32[]{:S(2)}) collective-permute-start(f32[184,128]{1,0:T(8,128)S(1)} %get-tuple-element.35), channel_id=1, source_target_pairs={{0,8},{8,0},{16,24},{24,16},{1,9},{9,1},{17,25},{25,17},{2,10},{10... | collective-permute-start | bytes 282632 | tf_op jit(solution)/shard_map/ppermute | solution.py:518
  20.8 7.7 %collective-permute-start.3 = (f32[184,128]{1,0:T(8,128)S(1)}, f32[184,128]{1,0:T(8,128)S(1)}, u32[]{:S(2)}, u32[]{:S(2)}) collective-permute-start(f32[184,128]{1,0:T(8,128)S(1)} %get-tuple-element.36), channel_id=1, source_target_pairs={{0,16},{8,24},{16,0},{24,8},{1,17},{9,25},{17,1},{25,9},{2,18},{10... | collective-permute-start | bytes 282632 | tf_op jit(solution)/shard_map/ppermute | solution.py:518
  23.4 6.5 %collective-permute-start.4 = (f32[184,128]{1,0:T(8,128)S(1)}, f32[184,128]{1,0:T(8,128)S(1)}, u32[]{:S(2)}, u32[]{:S(2)}) collective-permute-start(f32[184,128]{1,0:T(8,128)S(1)} %get-tuple-element.37), channel_id=1, source_target_pairs={{0,24},{8,16},{16,8},{24,0},{1,25},{9,17},{17,9},{25,1},{2,26},{10... | collective-permute-start | bytes 282632 | tf_op jit(solution)/shard_map/ppermute | solution.py:518
  29.9 6.6 %collective-permute-start.7 = (f32[184,128]{1,0:T(8,128)S(1)}, f32[184,128]{1,0:T(8,128)S(1)}, u32[]{:S(2)}, u32[]{:S(2)}) collective-permute-start(f32[184,128]{1,0:T(8,128)S(1)} %shard_map.79.refs_0_.field_ref), channel_id=1, source_target_pairs={{0,24},{8,16},{16,8},{24,0},{1,25},{9,17},{17,9},{25,1},{2,26},{10... | collective-permute-start | bytes 282632 | tf_op jit(solution)/shard_map/ppermute | solution.py:518
  32.1 7.0 %collective-permute-start.6 = (f32[184,128]{1,0:T(8,128)S(1)}, f32[184,128]{1,0:T(8,128)S(1)}, u32[]{:S(2)}, u32[]{:S(2)}) collective-permute-start(f32[184,128]{1,0:T(8,128)S(1)} %shard_map.79.refs_0_.field_ref), channel_id=1, source_target_pairs={{0,16},{8,24},{16,0},{24,8},{1,17},{9,25},{17,1},{25,9},{2,18},{10... | collective-permute-start | bytes 282632 | tf_op jit(solution)/shard_map/ppermute | solution.py:518
  32.7 6.4 %collective-permute-start.5 = (f32[184,128]{1,0:T(8,128)S(1)}, f32[184,128]{1,0:T(8,128)S(1)}, u32[]{:S(2)}, u32[]{:S(2)}) collective-permute-start(f32[184,128]{1,0:T(8,128)S(1)} %shard_map.79.refs_0_.field_ref), channel_id=1, source_target_pairs={{0,8},{8,0},{16,24},{24,16},{1,9},{9,1},{17,25},{25,17},{2,10},{10... | collective-permute-start | bytes 282632 | tf_op jit(solution)/shard_map/ppermute | solution.py:518
  42.8 3.8 %collective-permute-start.8 = (f32[480,128]{1,0:T(8,128)S(1)}, f32[480,128]{1,0:T(8,128)S(1)}, u32[]{:S(2)}, u32[]{:S(2)}) collective-permute-start(f32[480,128]{1,0:T(8,128)S(1)} %get-tuple-element.39), channel_id=1, source_target_pairs={{0,1},{1,0},{2,3},{3,2},{4,5},{5,4},{6,7},{7,6},{8,9},{9,8},{10,11... | collective-permute-start | bytes 737288 | tf_op jit(solution)/shard_map/ppermute | solution.py:515
  42.9 9.8 %collective-permute-start.9 = (f32[480,128]{1,0:T(8,128)S(1)}, f32[480,128]{1,0:T(8,128)S(1)}, u32[]{:S(2)}, u32[]{:S(2)}) collective-permute-start(f32[480,128]{1,0:T(8,128)S(1)} %get-tuple-element.40), channel_id=1, source_target_pairs={{0,7},{1,2},{2,1},{3,4},{4,3},{5,6},{6,5},{7,0},{8,15},{9,10},{10,... | collective-permute-start | bytes 737288 | tf_op jit(solution)/shard_map/ppermute | solution.py:515
  52.9 9.0 %collective-permute-start.11 = (f32[480,128]{1,0:T(8,128)S(1)}, f32[480,128]{1,0:T(8,128)S(1)}, u32[]{:S(2)}, u32[]{:S(2)}) collective-permute-start(f32[480,128]{1,0:T(8,128)S(1)} %get-tuple-element.42.refs_4_), channel_id=1, source_target_pairs={{0,7},{1,2},{2,1},{3,4},{4,3},{5,6},{6,5},{7,0},{8,15},{9,10},{10,... | collective-permute-start | bytes 737288 | tf_op jit(solution)/shard_map/ppermute | solution.py:515
  55.7 6.2 %collective-permute-start.10 = (f32[480,128]{1,0:T(8,128)S(1)}, f32[480,128]{1,0:T(8,128)S(1)}, u32[]{:S(2)}, u32[]{:S(2)}) collective-permute-start(f32[480,128]{1,0:T(8,128)S(1)} %get-tuple-element.42.refs_4_), channel_id=1, source_target_pairs={{0,1},{1,0},{2,3},{3,2},{4,5},{5,4},{6,7},{7,6},{8,9},{9,8},{10,11... | collective-permute-start | bytes 737288 | tf_op jit(solution)/shard_map/ppermute | solution.py:515
  61.9 57.4 %slice-start = ((s8[5898240]{0:T(1024)(128)(4,1)}), s8[1703936]{0:T(1024)(128)(4,1)S(1)}, s32[]{:S(2)}) async-start(s8[5898240]{0:T(1024)(128)(4,1)} %bitcast.4), calls=%async_computation.2 | async-start | bytes 3407872
  65.0 6.1 %collective-permute-start.12 = (f32[184,128]{1,0:T(8,128)S(1)}, f32[184,128]{1,0:T(8,128)S(1)}, u32[]{:S(2)}, u32[]{:S(2)}) collective-permute-start(f32[184,128]{1,0:T(8,128)S(1)} %get-tuple-element.44), channel_id=1, source_target_pairs={{0,8},{8,0},{16,24},{24,16},{1,9},{9,1},{17,25},{25,17},{2,10},{10... | collective-permute-start | bytes 282632 | tf_op jit(solution)/shard_map/ppermute | solution.py:518
  65.1 10.6 %collective-permute-start.13 = (f32[184,128]{1,0:T(8,128)S(1)}, f32[184,128]{1,0:T(8,128)S(1)}, u32[]{:S(2)}, u32[]{:S(2)}) collective-permute-start(f32[184,128]{1,0:T(8,128)S(1)} %get-tuple-element.45), channel_id=1, source_target_pairs={{0,16},{8,24},{16,0},{24,8},{1,17},{9,25},{17,1},{25,9},{2,18},{10... | collective-permute-start | bytes 282632 | tf_op jit(solution)/shard_map/ppermute | solution.py:518
  66.2 9.5 %collective-permute-start.14 = (f32[184,128]{1,0:T(8,128)S(1)}, f32[184,128]{1,0:T(8,128)S(1)}, u32[]{:S(2)}, u32[]{:S(2)}) collective-permute-start(f32[184,128]{1,0:T(8,128)S(1)} %get-tuple-element.46), channel_id=1, source_target_pairs={{0,24},{8,16},{16,8},{24,0},{1,25},{9,17},{17,9},{25,1},{2,26},{10... | collective-permute-start | bytes 282632 | tf_op jit(solution)/shard_map/ppermute | solution.py:518
  76.5 17.4 %all-to-all-start = ((f32[32,8,128]{2,1,0:T(8,128)}), f32[32,8,128]{2,1,0:T(8,128)S(1)}, u32[]{:S(2)}, u32[]{:S(2)}) async-start(f32[32,8,128]{2,1,0:T(8,128)} %bitcast), calls=%async_computation | async-start | bytes 262144 | tf_op jit(solution)/shard_map/all_to_all | solution.py:592
  79.3 9.3 %collective-permute-start.17 = (f32[184,128]{1,0:T(8,128)S(1)}, f32[184,128]{1,0:T(8,128)S(1)}, u32[]{:S(2)}, u32[]{:S(2)}) collective-permute-start(f32[184,128]{1,0:T(8,128)S(1)} %get-tuple-element.47.refs_0_.image0_ref), channel_id=1, source_target_pairs={{0,24},{8,16},{16,8},{24,0},{1,25},{9,17},{17,9},{25,1},{2,26},{10... | collective-permute-start | bytes 282632 | tf_op jit(solution)/shard_map/ppermute | solution.py:518
  83.0 11.0 %collective-permute-start.16 = (f32[184,128]{1,0:T(8,128)S(1)}, f32[184,128]{1,0:T(8,128)S(1)}, u32[]{:S(2)}, u32[]{:S(2)}) collective-permute-start(f32[184,128]{1,0:T(8,128)S(1)} %get-tuple-element.47.refs_0_.image0_ref), channel_id=1, source_target_pairs={{0,16},{8,24},{16,0},{24,8},{1,17},{9,25},{17,1},{25,9},{2,18},{10... | collective-permute-start | bytes 282632 | tf_op jit(solution)/shard_map/ppermute | solution.py:518
  83.0 11.0 %collective-permute-start.15 = (f32[184,128]{1,0:T(8,128)S(1)}, f32[184,128]{1,0:T(8,128)S(1)}, u32[]{:S(2)}, u32[]{:S(2)}) collective-permute-start(f32[184,128]{1,0:T(8,128)S(1)} %get-tuple-element.47.refs_0_.image0_ref), channel_id=1, source_target_pairs={{0,8},{8,0},{16,24},{24,16},{1,9},{9,1},{17,25},{25,17},{2,10},{10... | collective-permute-start | bytes 282632 | tf_op jit(solution)/shard_map/ppermute | solution.py:518
  101.2 2.6 %collective-permute-start.18 = (f32[480,128]{1,0:T(8,128)S(1)}, f32[480,128]{1,0:T(8,128)S(1)}, u32[]{:S(2)}, u32[]{:S(2)}) collective-permute-start(f32[480,128]{1,0:T(8,128)S(1)} %get-tuple-element.51), channel_id=1, source_target_pairs={{0,1},{1,0},{2,3},{3,2},{4,5},{5,4},{6,7},{7,6},{8,9},{9,8},{10,11... | collective-permute-start | bytes 737288 | tf_op jit(solution)/shard_map/ppermute | solution.py:515
  101.3 8.6 %collective-permute-start.19 = (f32[480,128]{1,0:T(8,128)S(1)}, f32[480,128]{1,0:T(8,128)S(1)}, u32[]{:S(2)}, u32[]{:S(2)}) collective-permute-start(f32[480,128]{1,0:T(8,128)S(1)} %get-tuple-element.52), channel_id=1, source_target_pairs={{0,7},{1,2},{2,1},{3,4},{4,3},{5,6},{6,5},{7,0},{8,15},{9,10},{10,... | collective-permute-start | bytes 737288 | tf_op jit(solution)/shard_map/ppermute | solution.py:515
  110.2 9.2 %collective-permute-start.21 = (f32[480,128]{1,0:T(8,128)S(1)}, f32[480,128]{1,0:T(8,128)S(1)}, u32[]{:S(2)}, u32[]{:S(2)}) collective-permute-start(f32[480,128]{1,0:T(8,128)S(1)} %get-tuple-element.55.refs_4_), channel_id=1, source_target_pairs={{0,7},{1,2},{2,1},{3,4},{4,3},{5,6},{6,5},{7,0},{8,15},{9,10},{10,... | collective-permute-start | bytes 737288 | tf_op jit(solution)/shard_map/ppermute | solution.py:515
  111.7 7.7 %collective-permute-start.20 = (f32[480,128]{1,0:T(8,128)S(1)}, f32[480,128]{1,0:T(8,128)S(1)}, u32[]{:S(2)}, u32[]{:S(2)}) collective-permute-start(f32[480,128]{1,0:T(8,128)S(1)} %get-tuple-element.55.refs_4_), channel_id=1, source_target_pairs={{0,1},{1,0},{2,3},{3,2},{4,5},{5,4},{6,7},{7,6},{8,9},{9,8},{10,11... | collective-permute-start | bytes 737288 | tf_op jit(solution)/shard_map/ppermute | solution.py:515
  122.3 4.6 %collective-permute-start.22 = (f32[184,128]{1,0:T(8,128)S(1)}, f32[184,128]{1,0:T(8,128)S(1)}, u32[]{:S(2)}, u32[]{:S(2)}) collective-permute-start(f32[184,128]{1,0:T(8,128)S(1)} %get-tuple-element.57), channel_id=1, source_target_pairs={{0,8},{8,0},{16,24},{24,16},{1,9},{9,1},{17,25},{25,17},{2,10},{10... | collective-permute-start | bytes 282632 | tf_op jit(solution)/shard_map/ppermute | solution.py:518
  122.4 9.2 %collective-permute-start.23 = (f32[184,128]{1,0:T(8,128)S(1)}, f32[184,128]{1,0:T(8,128)S(1)}, u32[]{:S(2)}, u32[]{:S(2)}) collective-permute-start(f32[184,128]{1,0:T(8,128)S(1)} %get-tuple-element.58), channel_id=1, source_target_pairs={{0,16},{8,24},{16,0},{24,8},{1,17},{9,25},{17,1},{25,9},{2,18},{10... | collective-permute-start | bytes 282632 | tf_op jit(solution)/shard_map/ppermute | solution.py:518
  124.0 7.6 %collective-permute-start.24 = (f32[184,128]{1,0:T(8,128)S(1)}, f32[184,128]{1,0:T(8,128)S(1)}, u32[]{:S(2)}, u32[]{:S(2)}) collective-permute-start(f32[184,128]{1,0:T(8,128)S(1)} %get-tuple-element.59), channel_id=1, source_target_pairs={{0,24},{8,16},{16,8},{24,0},{1,25},{9,17},{17,9},{25,1},{2,26},{10... | collective-permute-start | bytes 282632 | tf_op jit(solution)/shard_map/ppermute | solution.py:518
  (6 other events, 48.0 us)
where the time goes:
time: 145 us
  waiting for transfers between devices  64.2 us (44%)
  starting transfers between devices  40.5 us (28%)
  Pallas kernels  18.7 us (13%)
  blocking collectives  11.4 us (8%)
  local copies, waits for them, and re-layouts  9.24 us (6%)
    ppermute x15, waiting for transfers between devices, between(): return lax.ppermute(parts, 'mem', [(i, i ^ d) for i in range(n_mem)])  32.5 us
    ppermute x10, waiting for transfers between devices, swap(): return (lax.ppermute(to_a, 'lat', pairs), lax.ppermute(to_b, 'lat', cross))  31.7 us
    ppermute x15, starting transfers between devices, between(): return lax.ppermute(parts, 'mem', [(i, i ^ d) for i in range(n_mem)])  23.5 us
    ppermute x10, starting transfers between devices, swap(): return (lax.ppermute(to_a, 'lat', pairs), lax.ppermute(to_b, 'lat', cross))  14.2 us
    all_to_all x1, blocking collectives, everywhere(): lax.all_to_all(tile.reshape(devices, 8, LANES), ('mem', 'lat'), 0, 0)  11.4 us
    pallas_call x3, Pallas kernels, forward(): pl.pallas_call(functools.partial(forward_kernel, size), grid=(steps,), ou...  8.81 us
    unnamed x25, local copies, waits for them, and re-layouts  8.47 us
    pallas_call x2, Pallas kernels, adjoint(): pl.pallas_call(functools.partial(adjoint_kernel, size, later), grid=(step...  7.25 us
  transfers between devices with their start and end apart: 26, of which 16 were waited for; matrix products, arithmetic and copies ran while one was open for 0% of the time, Pallas kernels for 0%

commit v1 on v0

v1 whole, which is shorter than its diff:
```python
import functools

import jax
import jax.numpy as jnp
import ml_dtypes
import numpy as np
from jax import lax
from jax.experimental import pallas as pl
from jax.experimental.pallas import tpu as pltpu
from jax.sharding import PartitionSpec as P

RATIO = 4
HALF = 5
STEPS = 2
REACH = HALF + 1
LANES = 128
WIN = 64
MARGIN = 32
FINE = RATIO * WIN
CHUNK = 8
F32 = jnp.float32
BF16 = jnp.bfloat16


def tent(distance):
    return max(0.0, 1.0 - abs(distance) / RATIO)


def smooth(distance):
    return (1.0 - abs(distance) / REACH) / 2 if abs(distance) <= HALF else 0.0


def window_table():
    fine = np.arange(FINE, dtype=np.float64)[None, :]
    coarse = np.arange(LANES, dtype=np.float64)[:, None] - MARGIN
    table = np.maximum(0.0, 1.0 - np.abs(fine + 0.5 - RATIO * coarse - RATIO / 2) / RATIO)
    return table.astype(ml_dtypes.bfloat16)


class Sizes:
    def __init__(self, mesh, perturbations, control):
        self.n_mem = mesh.shape["mem"]
        self.n_lat = mesh.shape["lat"]
        self.members = control.shape[0]
        self.rows = control.shape[1]
        self.cols = control.shape[2]
        self.vars = perturbations.shape[1]
        self.fine_rows = perturbations.shape[2]
        self.fine_cols = perturbations.shape[3]
        assert self.rows == REACH and self.cols % LANES == WIN
        assert self.fine_rows == RATIO * self.rows and self.fine_cols == RATIO * self.cols
        self.windows = self.cols // WIN
        self.ext = self.cols + 2 * MARGIN
        self.slab = self.rows * self.members
        self.full = self.cols // LANES
        self.packed = self.full * self.slab + self.slab // 2
        self.field_rows = self.vars * self.fine_rows
        self.share = self.fine_cols // self.n_mem
        self.share_full = self.share // LANES
        self.share_rem = self.share % LANES
        self.groups = LANES // self.share_rem if self.share_rem else 1
        self.rem_rows = -(-self.field_rows // 8 // self.groups) * 8 if self.share_rem else 0
        self.part_rows = self.share_full * self.field_rows + self.rem_rows


def lane(shape):
    return lax.broadcasted_iota(jnp.int32, shape, 1)


def half_turn(x):
    return pltpu.roll(x, WIN, 1)


def pack_slab(size, first, last, middle):
    rows = size.slab
    at = lane((rows, LANES))
    pieces = list(middle)
    pieces.append(jnp.where(at < LANES - MARGIN, last, first))
    half = rows // 2
    at = lane((half, LANES))
    inner = (at >= MARGIN) & (at < LANES - MARGIN)
    pieces.append(jnp.where(inner, first[:half], half_turn(first[half:])))
    return pieces


def unpack_slab(size, packed):
    rows = size.slab
    middle = [packed[i * rows : (i + 1) * rows] for i in range(size.full - 1)]
    mixed = packed[(size.full - 1) * rows : size.full * rows]
    rest = packed[size.full * rows :]
    rest = jnp.concatenate([rest, half_turn(rest)], axis=0)
    at = lane((rows, LANES))
    first = jnp.where(at < MARGIN, half_turn(mixed), jnp.where(at < LANES - MARGIN, rest, mixed))
    last = jnp.where(at < LANES - MARGIN, mixed, half_turn(rest))
    return [first] + middle + [last]


def tiles_of(ref, count):
    return [ref[:, i * LANES : (i + 1) * LANES] for i in range(count)]


def put_packed(out, pieces):
    at = 0
    for piece in pieces:
        out[at : at + piece.shape[0], :] = piece
        at += piece.shape[0]


def pack_ref(size, out, tiles):
    put_packed(out, pack_slab(size, tiles[0], tiles[-1], tiles[1:-1]))


def place():
    lat = lax.axis_index("lat")
    odd = lax.rem(lat, 2) == 1
    low = (lat > 0).astype(F32)
    high = (lat < lax.axis_size("lat") - 1).astype(F32)
    return odd, low, high


def sides(a, b):
    odd, low, high = place()
    lower = jnp.where(odd, a, b) * low
    upper = jnp.where(odd, b, a) * high
    return lower, upper


def step_length(scal_ref):
    total = jnp.sum(scal_ref[...], axis=0, keepdims=True)
    at = lane(total.shape)
    grad_sq = jnp.sum(jnp.where(at == 0, total, 0.0), axis=1, keepdims=True)
    image_sq = jnp.sum(jnp.where(at == 1, total, 0.0), axis=1, keepdims=True)
    return grad_sq / (grad_sq + image_sq)


def enter_kernel(size, control_ref, own_ref, packed_ref):
    x = control_ref[...]
    x = jnp.concatenate([x[:, size.cols - MARGIN :], x, x[:, :MARGIN]], axis=1)
    own_ref[...] = x
    pack_ref(size, packed_ref, tiles_of(own_ref, size.ext // LANES))


def forward_kernel(size, own_ref, a_ref, b_ref, pert_ref, table_ref, *rest):
    outs = rest[: size.n_mem]
    ext_ref, coarse_ref, rows_ref, acc_ref, parts_ref = rest[size.n_mem :]
    members = size.members
    n_tiles = size.ext // LANES
    fine_rows = size.fine_rows

    unused, low, high = place()
    lower, upper = sides(a_ref[...], b_ref[...])
    lower = unpack_slab(size, lower)
    upper = unpack_slab(size, upper)
    n = size.slab
    for e in range(n_tiles):
        cut = slice(e * LANES, (e + 1) * LANES)
        ext_ref[0:n, cut] = lower[e]
        ext_ref[n : 2 * n, cut] = own_ref[:, cut]
        ext_ref[2 * n : 3 * n, cut] = upper[e]
    for e in range(n_tiles):
        cut = slice(e * LANES, (e + 1) * LANES)
        for g in range(0, members, 8):
            held = [
                ext_ref[k * members + g : k * members + g + 8, cut] for k in range(3 * REACH)
            ]
            for j in range(size.rows + 2):
                total = None
                for k in range(3 * REACH):
                    weight = smooth(j - 1 - (k - REACH))
                    if weight:
                        term = held[k] * weight
                        total = term if total is None else total + term
                if j == 0:
                    total = total * low
                if j == size.rows + 1:
                    total = total * high
                coarse_ref[j * members + g : j * members + g + 8, cut] = total
    for t in range(size.windows):
        e = t // 2
        held = []
        for j in range(size.rows + 2):
            at = slice(j * members, (j + 1) * members)
            value = coarse_ref[at, e * LANES : (e + 1) * LANES]
            if t % 2:
                other = coarse_ref[at, (e + 1) * LANES : (e + 2) * LANES]
                value = half_turn(jnp.where(lane(value.shape) < WIN, other, value))
            held.append(value)
        for i in range(fine_rows):
            total = None
            for j in range(size.rows + 2):
                weight = tent(i + 0.5 - RATIO * (j - 1) - RATIO / 2)
                if weight:
                    term = held[j] * weight
                    total = term if total is None else total + term
            rows_ref[t, pl.ds(i, members, stride=fine_rows), :] = total
    acc_ref[...] = jnp.zeros_like(acc_ref)
    block = CHUNK * fine_rows

    def chunk(step, unused):
        first = pl.multiple_of(step * block, 8)
        for t in range(size.windows):
            x = rows_ref[t, pl.ds(first, block), :]
            head = x.astype(BF16)
            tail = (x - head.astype(F32)).astype(BF16)
            refined = jnp.dot(
                jnp.concatenate([head, tail], axis=1), table_ref[...], preferred_element_type=F32
            )
            cut = slice(t * FINE, (t + 1) * FINE)
            for v in range(size.vars):
                at = slice(v * fine_rows, (v + 1) * fine_rows)
                total = acc_ref[at, cut]
                for m in range(CHUNK):
                    total = total + pert_ref[step * CHUNK + m, v, :, cut].astype(F32) * refined[
                        m * fine_rows : (m + 1) * fine_rows
                    ]
                acc_ref[at, cut] = total
        return unused

    lax.fori_loop(0, members // CHUNK, chunk, 0)
    for q in range(size.n_mem):
        put_part(size, parts_ref.at[q], acc_ref, q * size.share)
    mine = lax.axis_index("mem")
    for d in range(size.n_mem):
        outs[d][...] = parts_ref[mine ^ d]


def field_tile(acc_ref, start):
    e, shift = start // LANES, start % LANES
    tile = acc_ref[:, e * LANES : (e + 1) * LANES]
    if shift == 0:
        return tile
    if (e + 1) * LANES < acc_ref.shape[1]:
        other = acc_ref[:, (e + 1) * LANES : (e + 2) * LANES]
        tile = jnp.where(lane(tile.shape) < shift, other, tile)
    return pltpu.roll(tile, LANES - shift, 1)


def put_part(size, out, acc_ref, start):
    rows = size.field_rows
    for j in range(size.share_full):
        out[j * rows : (j + 1) * rows, :] = field_tile(acc_ref, start + j * LANES)
    if size.share_rem:
        tile = field_tile(acc_ref, start + size.share_full * LANES)
        tile = jnp.where(lane(tile.shape) < size.share_rem, tile, 0.0)
        missing = size.rem_rows * size.groups - rows
        if missing:
            tile = jnp.concatenate([tile, jnp.zeros((missing, LANES), F32)], axis=0)
        total = None
        for g in range(size.groups):
            term = tile[g * size.rem_rows : (g + 1) * size.rem_rows]
            if g:
                term = pltpu.roll(term, g * size.share_rem, 1)
            total = term if total is None else total + term
        out[size.share_full * rows :, :] = total


def part_tiles(size, part):
    rows = size.field_rows
    tiles = [(part[j * rows : (j + 1) * rows], LANES) for j in range(size.share_full)]
    if size.share_rem:
        rest = part[size.share_full * rows :]
        stack = [rest]
        for g in range(1, size.groups):
            stack.append(pltpu.roll(rest, LANES - g * size.share_rem, 1))
        tiles.append((jnp.concatenate(stack, axis=0)[:rows], size.share_rem))
    return tiles


def total_kernel(count, *refs):
    parts, out_ref = refs[:count], refs[count]
    total = parts[0][...]
    for part in parts[1:]:
        total = total + part[...]
    out_ref[...] = total


def squares_kernel(count, *refs):
    parts, grad_ref, out_ref, scal_ref = refs[:count], refs[count], refs[count + 1], refs[count + 2]
    total = parts[0][...]
    for part in parts[1:]:
        total = total + part[...]
    out_ref[...] = total
    image_sq = jnp.sum(total * total)
    grad = grad_ref[...]
    grad_sq = jnp.sum(grad * grad)
    at = lane(scal_ref.shape)
    scal_ref[...] = jnp.where(at == 0, grad_sq, jnp.where(at == 1, image_sq, 0.0))


def adjoint_kernel(size, later, *refs):
    refs = list(refs)
    parts = [refs.pop(0) for i in range(size.n_mem)]
    if later:
        scal_ref = refs.pop(0)
        before_ref = refs.pop(0)
    innov_ref, limit_ref, pert_ref, table_ref = refs[:4]
    refs = refs[4:]
    a_ref, b_ref, own_ref = refs[:3]
    refs = refs[3:]
    if not later:
        field_ref = refs.pop(0)
    misfit_ref, parts_ref, cols_ref, coarse_ref, spread_ref = refs
    members = size.members
    n_tiles = size.ext // LANES
    fine_rows = size.fine_rows

    mine = lax.axis_index("mem")
    for d in range(size.n_mem):
        parts_ref[mine ^ d] = parts[d][...]
    for q in range(size.n_mem):
        start = q * size.share
        for tile, width in part_tiles(size, parts_ref[q]):
            e, shift = start // LANES, start % LANES
            turned = pltpu.roll(tile, shift, 1) if shift else tile
            at = lane(turned.shape)
            cut = slice(e * LANES, (e + 1) * LANES)
            if shift == 0 and width == LANES:
                misfit_ref[:, cut] = turned
            else:
                inside = (at >= shift) & (at < shift + width)
                misfit_ref[:, cut] = jnp.where(inside, turned, misfit_ref[:, cut])
            if shift + width > LANES:
                cut = slice((e + 1) * LANES, (e + 2) * LANES)
                inside = at < shift + width - LANES
                misfit_ref[:, cut] = jnp.where(inside, turned, misfit_ref[:, cut])
            start += width
    value = misfit_ref[...]
    if later:
        value = before_ref[...] - step_length(scal_ref) * value
    else:
        field_ref[...] = value
    for v in range(size.vars):
        at = slice(v * fine_rows, (v + 1) * fine_rows)
        limit = limit_ref[v]
        misfit_ref[at, :] = jnp.clip(value[at] - innov_ref[v], -limit, limit)
    block = CHUNK * fine_rows

    def chunk(step, unused):
        first = pl.multiple_of(step * block, 8)
        tops = [None] * n_tiles
        for t in range(size.windows):
            cut = slice(t * FINE, (t + 1) * FINE)
            mis = [misfit_ref[v * fine_rows : (v + 1) * fine_rows, cut] for v in range(size.vars)]
            weighted = []
            for m in range(CHUNK):
                total = pert_ref[step * CHUNK + m, 0, :, cut].astype(F32) * mis[0]
                for v in range(1, size.vars):
                    total = total + pert_ref[step * CHUNK + m, v, :, cut].astype(F32) * mis[v]
                weighted.append(total)
            x = jnp.concatenate(weighted, axis=0)
            head = x.astype(BF16)
            tail = (x - head.astype(F32)).astype(BF16)
            columns = jnp.dot(
                jnp.concatenate([head, tail], axis=1), table_ref[...], preferred_element_type=F32
            )
            e = t // 2
            if t % 2 == 0:
                tops[e] = columns if tops[e] is None else tops[e] + columns
            else:
                turned = half_turn(columns)
                at = lane(turned.shape)
                tops[e] = tops[e] + jnp.where(at >= WIN, turned, 0.0)
                tops[e + 1] = jnp.where(at < WIN, turned, 0.0)
        for e in range(n_tiles):
            cols_ref[e, pl.ds(first, block), :] = tops[e]
        return unused

    lax.fori_loop(0, members // CHUNK, chunk, 0)
    odd, low, high = place()
    for e in range(n_tiles):
        cut = slice(e * LANES, (e + 1) * LANES)
        sums = [None] * (size.rows + 2)
        for i in range(fine_rows):
            value = cols_ref[e, pl.ds(i, members, stride=fine_rows), :]
            for j in range(size.rows + 2):
                weight = tent(i + 0.5 - RATIO * (j - 1) - RATIO / 2)
                if weight:
                    term = value * weight
                    sums[j] = term if sums[j] is None else sums[j] + term
        sums[0] = sums[0] * low
        sums[-1] = sums[-1] * high
        for j in range(size.rows + 2):
            coarse_ref[j * members : (j + 1) * members, cut] = sums[j]
    head = coarse_ref[:, 0:LANES]
    tail = coarse_ref[:, (n_tiles - 1) * LANES :]
    at = lane(head.shape)
    turned_head, turned_tail = half_turn(head), half_turn(tail)
    coarse_ref[:, 0:LANES] = head + jnp.where(at < WIN, turned_tail, 0.0)
    coarse_ref[:, (n_tiles - 1) * LANES :] = tail + jnp.where(at >= WIN, turned_head, 0.0)
    for e in range(n_tiles):
        cut = slice(e * LANES, (e + 1) * LANES)
        for g in range(0, members, 8):
            held = [
                coarse_ref[j * members + g : j * members + g + 8, cut]
                for j in range(size.rows + 2)
            ]
            for k in range(3 * REACH):
                total = None
                for j in range(size.rows + 2):
                    weight = smooth(j - 1 - (k - REACH))
                    if weight:
                        term = held[j] * weight
                        total = term if total is None else total + term
                spread_ref[k * members + g : k * members + g + 8, cut] = total
    n = size.slab

    def packed_of(part):
        tiles = [
            spread_ref[part * n : (part + 1) * n, e * LANES : (e + 1) * LANES]
            for e in range(n_tiles)
        ]
        return pack_slab(size, tiles[0], tiles[-1], tiles[1:-1])

    lower, upper = packed_of(0), packed_of(2)
    own_ref[...] = spread_ref[n : 2 * n, :]
    put_packed(a_ref, [jnp.where(odd, x, y) for x, y in zip(lower, upper)])
    put_packed(b_ref, [jnp.where(odd, y, x) for x, y in zip(lower, upper)])


def gradient_kernel(size, later, *refs):
    refs = list(refs)
    own_ref, a_ref, b_ref, weights_ref = refs[:4]
    refs = refs[4:]
    weights = weights_ref[...]
    if later:
        scal_ref, before_ref = refs.pop(0), refs.pop(0)
        weights = weights - step_length(scal_ref) * before_ref[...]
    grad_ref, packed_ref = refs[:2]
    if later:
        refs[2][...] = weights
    lower, upper = sides(a_ref[...], b_ref[...])
    arrived = unpack_slab(size, lower + upper)
    for e in range(size.ext // LANES):
        cut = slice(e * LANES, (e + 1) * LANES)
        grad_ref[:, cut] = weights[:, cut] + own_ref[:, cut] + arrived[e]
    pack_ref(size, packed_ref, tiles_of(grad_ref, size.ext // LANES))


def leave_kernel(size, weights_ref, grad_ref, field_ref, image0_ref, scal0_ref, image1_ref,
                 scal1_ref, out_weights_ref, out_field_ref):
    second = step_length(scal1_ref)
    weights = weights_ref[...] - second * grad_ref[...]
    n_tiles = size.ext // LANES
    tiles = [weights[:, e * LANES : (e + 1) * LANES] for e in range(n_tiles)]
    for e in range(n_tiles):
        tile = tiles[e]
        if e + 1 < n_tiles:
            tile = jnp.where(lane(tile.shape) < MARGIN, tiles[e + 1], tile)
        tile = pltpu.roll(tile, LANES - MARGIN, 1)
        start = e * LANES
        width = min(LANES, size.cols - start)
        out_weights_ref[:, start : start + width] = tile[:, :width]
    field = field_ref[...] - step_length(scal0_ref) * image0_ref[...] - second * image1_ref[...]
    start = 0
    for tile, width in part_tiles(size, field):
        for v in range(size.vars):
            rows = slice(v * size.fine_rows, (v + 1) * size.fine_rows)
            out_field_ref[v, :, start : start + width] = tile[rows, :width]
        start += width


def whole():
    return pl.BlockSpec(memory_space=pltpu.VMEM)


def params():
    return pltpu.CompilerParams(vmem_limit_bytes=24 * 1024 * 1024)


def array(*shape):
    return jax.ShapeDtypeStruct(shape, F32)


def call(kernel, outs, *args, scratch=()):
    return pl.pallas_call(
        kernel,
        out_shape=outs,
        in_specs=[
            pl.BlockSpec(memory_space=pltpu.SMEM) if arg.ndim == 1 else whole() for arg in args
        ],
        out_specs=jax.tree.map(lambda unused: whole(), outs),
        scratch_shapes=scratch,
        compiler_params=params(),
    )(*args)


def per_device(mesh, perturbations, control, innovations, thresholds):
    size = Sizes(mesh, perturbations, control)
    n_mem, n_lat, members = size.n_mem, size.n_lat, size.members
    devices = n_mem * n_lat
    table = window_table()
    up_table = jnp.asarray(np.concatenate([table, table], axis=0))
    down_table = jnp.asarray(np.concatenate([table.T, table.T], axis=0))
    pairs = [(i, i ^ 1) for i in range(n_lat)]
    cross = [(i, (i - 1 if i % 2 == 0 else i + 1) % n_lat) for i in range(n_lat)]
    slab = array(size.slab, size.ext)
    packed = array(size.packed, LANES)
    part = array(size.part_rows, LANES)
    scal = array(devices, LANES)

    def swap(to_a, to_b):
        return lax.ppermute(to_a, "lat", pairs), lax.ppermute(to_b, "lat", cross)

    def between(parts, d):
        return lax.ppermute(parts, "mem", [(i, i ^ d) for i in range(n_mem)])

    far_first = sorted(range(1, n_mem), key=lambda d: -d)

    def reduced(outs):
        moved = {d: between(outs[d], d) for d in far_first}
        return [outs[0]] + [moved[d] for d in range(1, n_mem)]

    def gathered(own):
        moved = {d: between(own, d) for d in far_first}
        return [own] + [moved[d] for d in range(1, n_mem)]

    def forward(own, a, b):
        return call(
            functools.partial(forward_kernel, size),
            [part] * n_mem,
            own,
            a,
            b,
            perturbations,
            up_table,
            scratch=[
                pltpu.VMEM((3 * size.slab, size.ext), F32),
                pltpu.VMEM(((size.rows + 2) * members, size.ext), F32),
                pltpu.VMEM((size.windows, members * size.fine_rows, LANES), F32),
                pltpu.VMEM((size.field_rows, size.fine_cols), F32),
                pltpu.VMEM((n_mem, size.part_rows, LANES), F32),
            ],
        )

    def adjoint(parts, *step):
        later = len(step) > 0
        field = array(size.field_rows, size.fine_cols)
        n_tiles = size.ext // LANES
        return call(
            functools.partial(adjoint_kernel, size, later),
            [packed, packed, slab] + ([] if later else [field]),
            *parts,
            *step,
            innovations,
            thresholds,
            perturbations,
            down_table,
            scratch=[
                pltpu.VMEM((size.field_rows, size.fine_cols), F32),
                pltpu.VMEM((n_mem, size.part_rows, LANES), F32),
                pltpu.VMEM((n_tiles, members * size.fine_rows, LANES), F32),
                pltpu.VMEM(((size.rows + 2) * members, size.ext), F32),
                pltpu.VMEM((3 * size.slab, size.ext), F32),
            ],
        )

    def everywhere(tile):
        moved = lax.all_to_all(tile.reshape(devices, 1, LANES), ("mem", "lat"), 0, 0)
        return moved.reshape(devices, LANES)

    own, sent = call(functools.partial(enter_kernel, size), [slab, packed],
        control.transpose(1, 0, 2).reshape(size.slab, size.cols))
    parts = reduced(forward(own, *swap(sent, sent)))
    field0 = call(functools.partial(total_kernel, n_mem), part, *parts)
    to_a, to_b, spread, field_all = adjoint(gathered(field0))
    grad0, sent = call(
        functools.partial(gradient_kernel, size, False),
        [slab, packed],
        spread,
        *swap(to_a, to_b),
        own,
    )
    parts = reduced(forward(grad0, *swap(sent, sent)))
    image0, scal0 = call(
        functools.partial(squares_kernel, n_mem), [part, scal], *parts, sent
    )
    images = gathered(image0)
    scal0 = everywhere(scal0)
    to_a, to_b, spread = adjoint(images, scal0, field_all)
    grad1, sent, weights1 = call(
        functools.partial(gradient_kernel, size, True),
        [slab, packed, slab],
        spread,
        *swap(to_a, to_b),
        own,
        scal0,
        grad0,
    )
    parts = reduced(forward(grad1, *swap(sent, sent)))
    image1, scal1 = call(
        functools.partial(squares_kernel, n_mem), [part, scal], *parts, sent
    )
    scal1 = everywhere(scal1)
    weights, field = call(
        functools.partial(leave_kernel, size),
        [array(size.slab, size.cols), array(size.vars, size.fine_rows, size.share)],
        weights1,
        grad1,
        field0,
        image0,
        scal0,
        image1,
        scal1,
    )
    return weights.reshape(size.rows, members, size.cols).transpose(1, 0, 2), field


def solution(mesh):
    return jax.shard_map(
        functools.partial(per_device, mesh),
        mesh=mesh,
        in_specs=(P("mem", None, "lat", None), P("mem", "lat", None), P(None, "lat", None), P()),
        out_specs=(P("mem", "lat", None), P(None, "lat", "mem")),
        check_vma=False,
    )
```

time: 145 us -> 135 us (0.931)
  blocking collectives: 11.4 us -> 18.5 us
  waiting for transfers between devices: 64.2 us -> 57.8 us
  starting transfers between devices: 40.5 us -> 34.7 us
  local copies, waits for them, and re-layouts: 9.24 us -> 4.59 us
    ppermute x15, waiting for transfers between devices: 32.5 us -> 23.7 us  [between(): return lax.ppermute(parts, 'mem', [(i, i ^ d) for i in range(n_mem)])]
    all_to_all x1 -> x2, blocking collectives: 11.4 us -> 18.5 us  [everywhere(): lax.all_to_all(tile.reshape(devices, 1, LANES), ('mem', 'lat'), 0, 0)]
    unnamed x25 -> x16, local copies, waits for them, and re-layouts: 8.47 us -> 4.59 us
    ppermute x10, starting transfers between devices: 14.2 us -> 11.2 us  [swap(): return (lax.ppermute(to_a, 'lat', pairs), lax.ppermute(to_b, 'lat', cross))]
    all_to_all x1 -> x0, starting transfers between devices: 2.78 us -> none  [everywhere(): lax.all_to_all(tile.reshape(devices, 8, LANES), ('mem', 'lat'), 0, 0)]
    ppermute x10, waiting for transfers between devices: 31.7 us -> 34.1 us  [swap(): return (lax.ppermute(to_a, 'lat', pairs), lax.ppermute(to_b, 'lat', cross))]
  transfers between devices with their start and end apart: 26 -> 25, of which waited for: 16 -> 15; matrix products, arithmetic and copies ran while one was open for 0% -> 0% of each run, Pallas kernels for 0% -> 0%
where the time goes in v1:
time: 135 us; the launch traced here: 134 us
  waiting for transfers between devices  57.8 us (43%)
  starting transfers between devices  34.7 us (26%)
  blocking collectives  18.5 us (14%)
  Pallas kernels  18.1 us (13%)
  local copies, waits for them, and re-layouts  4.59 us (3%)
    ppermute x10, waiting for transfers between devices, swap(): return (lax.ppermute(to_a, 'lat', pairs), lax.ppermute(to_b, 'lat', cross))  34.1 us
    ppermute x15, waiting for transfers between devices, between(): return lax.ppermute(parts, 'mem', [(i, i ^ d) for i in range(n_mem)])  23.7 us
    ppermute x15, starting transfers between devices, between(): return lax.ppermute(parts, 'mem', [(i, i ^ d) for i in range(n_mem)])  23.5 us
    all_to_all x2, blocking collectives, everywhere(): lax.all_to_all(tile.reshape(devices, 1, LANES), ('mem', 'lat'), 0, 0)  18.5 us
    pallas_call x12, Pallas kernels, call(): pl.pallas_call(kernel, out_shape=outs, in_specs=[pl.BlockSpec(memory_spac...  18.1 us
    ppermute x10, starting transfers between devices, swap(): return (lax.ppermute(to_a, 'lat', pairs), lax.ppermute(to_b, 'lat', cross))  11.2 us
    unnamed x16, local copies, waits for them, and re-layouts  4.59 us
  transfers between devices with their start and end apart: 25, of which 15 were waited for; matrix products, arithmetic and copies ran while one was open for 0% of the time, Pallas kernels for 0%

profile of v1, /device:TPU:0, one launch (start us, length us, event | category | flops | bytes accessed | tf_op | source)
XLA Modules:
  0.0 134.5 jit_solution(1460931591772383691)
XLA Ops:
  1.9 3.4 %collective-permute-start.1 = (f32[480,128]{1,0:T(8,128)S(1)}, f32[480,128]{1,0:T(8,128)S(1)}, u32[]{:S(2)}, u32[]{:S(2)}) collective-permute-start(f32[480,128]{1,0:T(8,128)S(1)} %get-tuple-element.35), channel_id=1, source_target_pairs={{0,7},{1,2},{2,1},{3,4},{4,3},{5,6},{6,5},{7,0},{8,15},{9,10},{10,... | collective-permute-start | bytes 737288 | tf_op jit(solution)/shard_map/ppermute | solution.py:502
  5.3 5.7 %collective-permute-done.1.b_ref = f32[480,128]{1,0:T(8,128)S(1)} collective-permute-done((f32[480,128]{1,0:T(8,128)S(1)}, f32[480,128]{1,0:T(8,128)S(1)}, u32[]{:S(2)}, u32[]{:S(2)}) %collective-permute-start.1) | collective-permute-done | bytes 245792 | tf_op jit(solution)/shard_map/ppermute | solution.py:502
  10.9 2.7 %copy-done = bf16[32,3,24,1280]{3,2,1,0:T(8,128)(2,1)S(1)} copy-done((bf16[32,3,24,1280]{3,2,1,0:T(8,128)(2,1)S(1)}, bf16[32,3,24,1280]{3,2,1,0:T(8,128)(2,1)}, u32[]{:S(2)}) %copy-start) | copy-done | bytes 5898264
  14.5 2.8 %shard_map.78 = (f32[184,128]{1,0:T(8,128)S(1)}, f32[184,128]{1,0:T(8,128)S(1)}, f32[184,128]{1,0:T(8,128)S(1)}, f32[184,128]{1,0:T(8,128)S(1)}) custom-call(f32[192,384]{1,0:T(8,128)S(1)} %get-tuple-element.34.own_ref.refs_3_, f32[480,128]{1,0:T(8,128)S(1)} %collective-permute-done.a_ref, f32[480,128]{1,0:T(8,128)S(1)} %collective-permute-done.1.b_ref, ...), custom_call_target="tpu_custom_call" | custom-call | tf_op jit(solution)/shard_map/pallas_call | solution.py:475
  17.4 3.1 %collective-permute-start.2 = (f32[184,128]{1,0:T(8,128)S(1)}, f32[184,128]{1,0:T(8,128)S(1)}, u32[]{:S(2)}, u32[]{:S(2)}) collective-permute-start(f32[184,128]{1,0:T(8,128)S(1)} %get-tuple-element.37), channel_id=1, source_target_pairs={{0,8},{8,0},{16,24},{24,16},{1,9},{9,1},{17,25},{25,17},{2,10},{10... | collective-permute-start | bytes 282632 | tf_op jit(solution)/shard_map/ppermute | solution.py:505
  20.5 2.6 %collective-permute-start.3 = (f32[184,128]{1,0:T(8,128)S(1)}, f32[184,128]{1,0:T(8,128)S(1)}, u32[]{:S(2)}, u32[]{:S(2)}) collective-permute-start(f32[184,128]{1,0:T(8,128)S(1)} %get-tuple-element.38), channel_id=1, source_target_pairs={{0,16},{8,24},{16,0},{24,8},{1,17},{9,25},{17,1},{25,9},{2,18},{10... | collective-permute-start | bytes 282632 | tf_op jit(solution)/shard_map/ppermute | solution.py:505
  24.0 4.2 %collective-permute-done.3.refs_2_ = f32[184,128]{1,0:T(8,128)S(1)} collective-permute-done((f32[184,128]{1,0:T(8,128)S(1)}, f32[184,128]{1,0:T(8,128)S(1)}, u32[]{:S(2)}, u32[]{:S(2)}) %collective-permute-start.3) | collective-permute-done | bytes 94240 | tf_op jit(solution)/shard_map/ppermute | solution.py:505
  28.2 1.3 collective-permute-done.4.refs_3_
  29.6 2.2 %collective-permute-start.7 = (f32[184,128]{1,0:T(8,128)S(1)}, f32[184,128]{1,0:T(8,128)S(1)}, u32[]{:S(2)}, u32[]{:S(2)}) collective-permute-start(f32[184,128]{1,0:T(8,128)S(1)} %shard_map.79.refs_0_.field_ref), channel_id=1, source_target_pairs={{0,24},{8,16},{16,8},{24,0},{1,25},{9,17},{17,9},{25,1},{2,26},{10... | collective-permute-start | bytes 282632 | tf_op jit(solution)/shard_map/ppermute | solution.py:505
  32.4 1.7 %collective-permute-start.5 = (f32[184,128]{1,0:T(8,128)S(1)}, f32[184,128]{1,0:T(8,128)S(1)}, u32[]{:S(2)}, u32[]{:S(2)}) collective-permute-start(f32[184,128]{1,0:T(8,128)S(1)} %shard_map.79.refs_0_.field_ref), channel_id=1, source_target_pairs={{0,8},{8,0},{16,24},{24,16},{1,9},{9,1},{17,25},{25,17},{2,10},{10... | collective-permute-start | bytes 282632 | tf_op jit(solution)/shard_map/ppermute | solution.py:505
  34.0 2.2 %collective-permute-done.7.refs_3_ = f32[184,128]{1,0:T(8,128)S(1)} collective-permute-done((f32[184,128]{1,0:T(8,128)S(1)}, f32[184,128]{1,0:T(8,128)S(1)}, u32[]{:S(2)}, u32[]{:S(2)}) %collective-permute-start.7) | collective-permute-done | bytes 94240 | tf_op jit(solution)/shard_map/ppermute | solution.py:505
  36.2 2.6 %collective-permute-done.6.refs_2_ = f32[184,128]{1,0:T(8,128)S(1)} collective-permute-done((f32[184,128]{1,0:T(8,128)S(1)}, f32[184,128]{1,0:T(8,128)S(1)}, u32[]{:S(2)}, u32[]{:S(2)}) %collective-permute-start.6) | collective-permute-done | bytes 94240 | tf_op jit(solution)/shard_map/ppermute | solution.py:505
  38.8 3.7 %shard_map.80 = (f32[480,128]{1,0:T(8,128)S(1)}, f32[480,128]{1,0:T(8,128)S(1)}, f32[192,384]{1,0:T(8,128)S(1)}, f32[72,1280]{1,0:T(8,128)S(1)}) custom-call(f32[184,128]{1,0:T(8,128)S(1)} %shard_map.79.refs_0_.field_ref, f32[184,128]{1,0:T(8,128)S(1)} %collective-permute-done.5.refs_1_, f32[184,128]{1,0:T(8,128)S(1)} %collective-permute-done.6.refs_2_, ...), custom_call_target="tpu_custom_call" | custom-call | tf_op jit(solution)/shard_map/pallas_call | solution.py:475
  42.6 3.7 %collective-permute-start.9 = (f32[480,128]{1,0:T(8,128)S(1)}, f32[480,128]{1,0:T(8,128)S(1)}, u32[]{:S(2)}, u32[]{:S(2)}) collective-permute-start(f32[480,128]{1,0:T(8,128)S(1)} %get-tuple-element.42), channel_id=1, source_target_pairs={{0,7},{1,2},{2,1},{3,4},{4,3},{5,6},{6,5},{7,0},{8,15},{9,10},{10,... | collective-permute-start | bytes 737288 | tf_op jit(solution)/shard_map/ppermute | solution.py:502
  46.2 6.1 %collective-permute-done.9.refs_2_ = f32[480,128]{1,0:T(8,128)S(1)} collective-permute-done((f32[480,128]{1,0:T(8,128)S(1)}, f32[480,128]{1,0:T(8,128)S(1)}, u32[]{:S(2)}, u32[]{:S(2)}) %collective-permute-start.9) | collective-permute-done | bytes 245792 | tf_op jit(solution)/shard_map/ppermute | solution.py:502
  52.5 2.9 %collective-permute-start.11 = (f32[480,128]{1,0:T(8,128)S(1)}, f32[480,128]{1,0:T(8,128)S(1)}, u32[]{:S(2)}, u32[]{:S(2)}) collective-permute-start(f32[480,128]{1,0:T(8,128)S(1)} %get-tuple-element.44.refs_4_), channel_id=1, source_target_pairs={{0,7},{1,2},{2,1},{3,4},{4,3},{5,6},{6,5},{7,0},{8,15},{9,10},{10,... | collective-permute-start | bytes 737288 | tf_op jit(solution)/shard_map/ppermute | solution.py:502
  55.4 6.1 %collective-permute-done.11.b_ref = f32[480,128]{1,0:T(8,128)S(1)} collective-permute-done((f32[480,128]{1,0:T(8,128)S(1)}, f32[480,128]{1,0:T(8,128)S(1)}, u32[]{:S(2)}, u32[]{:S(2)}) %collective-permute-start.11) | collective-permute-done | bytes 245792 | tf_op jit(solution)/shard_map/ppermute | solution.py:502
  61.6 2.9 %shard_map.82 = (f32[184,128]{1,0:T(8,128)S(1)}, f32[184,128]{1,0:T(8,128)S(1)}, f32[184,128]{1,0:T(8,128)S(1)}, f32[184,128]{1,0:T(8,128)S(1)}) custom-call(f32[192,384]{1,0:T(8,128)S(1)} %get-tuple-element.43.own_ref.refs_5_, f32[480,128]{1,0:T(8,128)S(1)} %collective-permute-done.10.a_ref, f32[480,128]{1,0:T(8,128)S(1)} %collective-permute-done.11.b_ref, ...), custom_call_target="tpu_custom_call" | custom-call | tf_op jit(solution)/shard_map/pallas_call | solution.py:475
  65.7 3.3 %collective-permute-start.14 = (f32[184,128]{1,0:T(8,128)S(1)}, f32[184,128]{1,0:T(8,128)S(1)}, u32[]{:S(2)}, u32[]{:S(2)}) collective-permute-start(f32[184,128]{1,0:T(8,128)S(1)} %get-tuple-element.48), channel_id=1, source_target_pairs={{0,24},{8,16},{16,8},{24,0},{1,25},{9,17},{17,9},{25,1},{2,26},{10... | collective-permute-start | bytes 282632 | tf_op jit(solution)/shard_map/ppermute | solution.py:505
  68.9 1.6 %collective-permute-done.12.refs_1_ = f32[184,128]{1,0:T(8,128)S(1)} collective-permute-done((f32[184,128]{1,0:T(8,128)S(1)}, f32[184,128]{1,0:T(8,128)S(1)}, u32[]{:S(2)}, u32[]{:S(2)}) %collective-permute-start.12) | collective-permute-done | bytes 94240 | tf_op jit(solution)/shard_map/ppermute | solution.py:505
  70.6 4.6 %collective-permute-done.13.refs_2_ = f32[184,128]{1,0:T(8,128)S(1)} collective-permute-done((f32[184,128]{1,0:T(8,128)S(1)}, f32[184,128]{1,0:T(8,128)S(1)}, u32[]{:S(2)}, u32[]{:S(2)}) %collective-permute-start.13) | collective-permute-done | bytes 94240 | tf_op jit(solution)/shard_map/ppermute | solution.py:505
  75.4 1.3 collective-permute-start.17
  76.7 1.9 %collective-permute-start.16 = (f32[184,128]{1,0:T(8,128)S(1)}, f32[184,128]{1,0:T(8,128)S(1)}, u32[]{:S(2)}, u32[]{:S(2)}) collective-permute-start(f32[184,128]{1,0:T(8,128)S(1)} %get-tuple-element.49.refs_0_.image0_ref), channel_id=1, source_target_pairs={{0,16},{8,24},{16,0},{24,8},{1,17},{9,25},{17,1},{25,9},{2,18},{10... | collective-permute-start | bytes 282632 | tf_op jit(solution)/shard_map/ppermute | solution.py:505
  79.8 9.6 %all_to_all.10 = f32[32,1,128]{2,1,0:T(1,128)S(1)} all-to-all(f32[32,1,128]{2,1,0:T(1,128)S(1)} %bitcast.19), channel_id=1, replica_groups=mesh['mem'=4,'lat'=8] {'mem','lat'}, dimensions={0} | all-to-all | bytes 32768 | tf_op jit(solution)/shard_map/all_to_all | solution.py:558
  89.5 3.7 %shard_map.84 = (f32[480,128]{1,0:T(8,128)S(1)}, f32[480,128]{1,0:T(8,128)S(1)}, f32[192,384]{1,0:T(8,128)S(1)}) custom-call(f32[184,128]{1,0:T(8,128)S(1)} %get-tuple-element.49.refs_0_.image0_ref, f32[184,128]{1,0:T(8,128)S(1)} %collective-permute-done.15.refs_1_, f32[184,128]{1,0:T(8,128)S(1)} %collective-permute-done.16.refs_2_, ...), custom_call_target="tpu_custom_call" | custom-call | tf_op jit(solution)/shard_map/pallas_call | solution.py:475
  94.8 7.4 %collective-permute-done.19.refs_2_ = f32[480,128]{1,0:T(8,128)S(1)} collective-permute-done((f32[480,128]{1,0:T(8,128)S(1)}, f32[480,128]{1,0:T(8,128)S(1)}, u32[]{:S(2)}, u32[]{:S(2)}) %collective-permute-start.19) | collective-permute-done | bytes 245792 | tf_op jit(solution)/shard_map/ppermute | solution.py:502
  102.7 8.0 %collective-permute-done.21.b_ref = f32[480,128]{1,0:T(8,128)S(1)} collective-permute-done((f32[480,128]{1,0:T(8,128)S(1)}, f32[480,128]{1,0:T(8,128)S(1)}, u32[]{:S(2)}, u32[]{:S(2)}) %collective-permute-start.21) | collective-permute-done | bytes 245792 | tf_op jit(solution)/shard_map/ppermute | solution.py:502
  110.7 2.9 %shard_map.86 = (f32[184,128]{1,0:T(8,128)S(1)}, f32[184,128]{1,0:T(8,128)S(1)}, f32[184,128]{1,0:T(8,128)S(1)}, f32[184,128]{1,0:T(8,128)S(1)}) custom-call(f32[192,384]{1,0:T(8,128)S(1)} %get-tuple-element.56.own_ref.grad_ref, f32[480,128]{1,0:T(8,128)S(1)} %collective-permute-done.20.a_ref, f32[480,128]{1,0:T(8,128)S(1)} %collective-permute-done.21.b_ref, ...), custom_call_target="tpu_custom_call" | custom-call | tf_op jit(solution)/shard_map/pallas_call | solution.py:475
  115.5 2.6 %collective-permute-start.24 = (f32[184,128]{1,0:T(8,128)S(1)}, f32[184,128]{1,0:T(8,128)S(1)}, u32[]{:S(2)}, u32[]{:S(2)}) collective-permute-start(f32[184,128]{1,0:T(8,128)S(1)} %get-tuple-element.61), channel_id=1, source_target_pairs={{0,24},{8,16},{16,8},{24,0},{1,25},{9,17},{17,9},{25,1},{2,26},{10... | collective-permute-start | bytes 282632 | tf_op jit(solution)/shard_map/ppermute | solution.py:505
  118.1 1.2 collective-permute-done.22.refs_1_
  119.3 5.0 %collective-permute-done.23.refs_2_ = f32[184,128]{1,0:T(8,128)S(1)} collective-permute-done((f32[184,128]{1,0:T(8,128)S(1)}, f32[184,128]{1,0:T(8,128)S(1)}, u32[]{:S(2)}, u32[]{:S(2)}) %collective-permute-start.23) | collective-permute-done | bytes 94240 | tf_op jit(solution)/shard_map/ppermute | solution.py:505
  124.6 8.9 %all_to_all.11 = f32[32,1,128]{2,1,0:T(1,128)S(1)} all-to-all(f32[32,1,128]{2,1,0:T(1,128)S(1)} %bitcast.20), channel_id=1, replica_groups=mesh['mem'=4,'lat'=8] {'mem','lat'}, dimensions={0} | all-to-all | bytes 32768 | tf_op jit(solution)/shard_map/all_to_all | solution.py:558
  (48 shorter events, 11.6 us)
Async XLA Ops:
  0.6 38.2 %copy-start.5 = (bf16[512,128]{1,0:T(8,128)(2,1)S(1)}, bf16[512,128]{1,0:T(8,128)(2,1)}, u32[]{:S(2)}) copy-start(bf16[512,128]{1,0:T(8,128)(2,1)} %constant.5.clone.refs_7_.refs_9_) | copy-start | bytes 393220
  0.6 1.0 copy-start.6
  1.6 37.1 %copy-start.7 = (f32[3]{0:T(128)S(1)}, f32[3]{0:T(128)}, u32[]{:S(2)}) copy-start(f32[3]{0:T(128)} %refs_7_.2) | copy-start | bytes 40
  1.9 9.1 %collective-permute-start.1 = (f32[480,128]{1,0:T(8,128)S(1)}, f32[480,128]{1,0:T(8,128)S(1)}, u32[]{:S(2)}, u32[]{:S(2)}) collective-permute-start(f32[480,128]{1,0:T(8,128)S(1)} %get-tuple-element.35), channel_id=1, source_target_pairs={{0,7},{1,2},{2,1},{3,4},{4,3},{5,6},{6,5},{7,0},{8,15},{9,10},{10,... | collective-permute-start | bytes 737288 | tf_op jit(solution)/shard_map/ppermute | solution.py:502
  5.3 5.7 %collective-permute-start = (f32[480,128]{1,0:T(8,128)S(1)}, f32[480,128]{1,0:T(8,128)S(1)}, u32[]{:S(2)}, u32[]{:S(2)}) collective-permute-start(f32[480,128]{1,0:T(8,128)S(1)} %get-tuple-element.35), channel_id=1, source_target_pairs={{0,1},{1,0},{2,3},{3,2},{4,5},{5,4},{6,7},{7,6},{8,9},{9,8},{10,11... | collective-permute-start | bytes 737288 | tf_op jit(solution)/shard_map/ppermute | solution.py:502
  10.9 2.7 %copy-start = (bf16[32,3,24,1280]{3,2,1,0:T(8,128)(2,1)S(1)}, bf16[32,3,24,1280]{3,2,1,0:T(8,128)(2,1)}, u32[]{:S(2)}) copy-start(bf16[32,3,24,1280]{3,2,1,0:T(8,128)(2,1)} %pert_ref.5) | copy-start | bytes 17694724
  14.5 24.3 %copy-start.1 = (bf16[32,3,24,1280]{3,2,1,0:T(8,128)(2,1)S(1)}, bf16[32,3,24,1280]{3,2,1,0:T(8,128)(2,1)}, u32[]{:S(2)}) copy-start(bf16[32,3,24,1280]{3,2,1,0:T(8,128)(2,1)} %pert_ref.5) | copy-start | bytes 17694724
  14.5 24.3 %copy-start.2 = (f32[3,24,1280]{2,1,0:T(8,128)S(1)}, f32[3,24,1280]{2,1,0:T(8,128)}, u32[]{:S(2)}) copy-start(f32[3,24,1280]{2,1,0:T(8,128)} %refs_6_.3) | copy-start | bytes 1105924
  14.5 47.0 %copy-start.4 = (bf16[256,256]{1,0:T(8,128)(2,1)S(1)}, bf16[256,256]{1,0:T(8,128)(2,1)}, u32[]{:S(2)}) copy-start(bf16[256,256]{1,0:T(8,128)(2,1)} %constant.4.clone.table_ref) | copy-start | bytes 393220
  17.4 6.6 %collective-permute-start.2 = (f32[184,128]{1,0:T(8,128)S(1)}, f32[184,128]{1,0:T(8,128)S(1)}, u32[]{:S(2)}, u32[]{:S(2)}) collective-permute-start(f32[184,128]{1,0:T(8,128)S(1)} %get-tuple-element.37), channel_id=1, source_target_pairs={{0,8},{8,0},{16,24},{24,16},{1,9},{9,1},{17,25},{25,17},{2,10},{10... | collective-permute-start | bytes 282632 | tf_op jit(solution)/shard_map/ppermute | solution.py:505
  20.5 7.7 %collective-permute-start.3 = (f32[184,128]{1,0:T(8,128)S(1)}, f32[184,128]{1,0:T(8,128)S(1)}, u32[]{:S(2)}, u32[]{:S(2)}) collective-permute-start(f32[184,128]{1,0:T(8,128)S(1)} %get-tuple-element.38), channel_id=1, source_target_pairs={{0,16},{8,24},{16,0},{24,8},{1,17},{9,25},{17,1},{25,9},{2,18},{10... | collective-permute-start | bytes 282632 | tf_op jit(solution)/shard_map/ppermute | solution.py:505
  23.1 6.5 %collective-permute-start.4 = (f32[184,128]{1,0:T(8,128)S(1)}, f32[184,128]{1,0:T(8,128)S(1)}, u32[]{:S(2)}, u32[]{:S(2)}) collective-permute-start(f32[184,128]{1,0:T(8,128)S(1)} %get-tuple-element.39), channel_id=1, source_target_pairs={{0,24},{8,16},{16,8},{24,0},{1,25},{9,17},{17,9},{25,1},{2,26},{10... | collective-permute-start | bytes 282632 | tf_op jit(solution)/shard_map/ppermute | solution.py:505
  29.6 6.6 %collective-permute-start.7 = (f32[184,128]{1,0:T(8,128)S(1)}, f32[184,128]{1,0:T(8,128)S(1)}, u32[]{:S(2)}, u32[]{:S(2)}) collective-permute-start(f32[184,128]{1,0:T(8,128)S(1)} %shard_map.79.refs_0_.field_ref), channel_id=1, source_target_pairs={{0,24},{8,16},{16,8},{24,0},{1,25},{9,17},{17,9},{25,1},{2,26},{10... | collective-permute-start | bytes 282632 | tf_op jit(solution)/shard_map/ppermute | solution.py:505
  31.8 7.0 %collective-permute-start.6 = (f32[184,128]{1,0:T(8,128)S(1)}, f32[184,128]{1,0:T(8,128)S(1)}, u32[]{:S(2)}, u32[]{:S(2)}) collective-permute-start(f32[184,128]{1,0:T(8,128)S(1)} %shard_map.79.refs_0_.field_ref), channel_id=1, source_target_pairs={{0,16},{8,24},{16,0},{24,8},{1,17},{9,25},{17,1},{25,9},{2,18},{10... | collective-permute-start | bytes 282632 | tf_op jit(solution)/shard_map/ppermute | solution.py:505
  32.4 6.4 %collective-permute-start.5 = (f32[184,128]{1,0:T(8,128)S(1)}, f32[184,128]{1,0:T(8,128)S(1)}, u32[]{:S(2)}, u32[]{:S(2)}) collective-permute-start(f32[184,128]{1,0:T(8,128)S(1)} %shard_map.79.refs_0_.field_ref), channel_id=1, source_target_pairs={{0,8},{8,0},{16,24},{24,16},{1,9},{9,1},{17,25},{25,17},{2,10},{10... | collective-permute-start | bytes 282632 | tf_op jit(solution)/shard_map/ppermute | solution.py:505
  42.5 3.8 %collective-permute-start.8 = (f32[480,128]{1,0:T(8,128)S(1)}, f32[480,128]{1,0:T(8,128)S(1)}, u32[]{:S(2)}, u32[]{:S(2)}) collective-permute-start(f32[480,128]{1,0:T(8,128)S(1)} %get-tuple-element.41), channel_id=1, source_target_pairs={{0,1},{1,0},{2,3},{3,2},{4,5},{5,4},{6,7},{7,6},{8,9},{9,8},{10,11... | collective-permute-start | bytes 737288 | tf_op jit(solution)/shard_map/ppermute | solution.py:502
  42.6 9.8 %collective-permute-start.9 = (f32[480,128]{1,0:T(8,128)S(1)}, f32[480,128]{1,0:T(8,128)S(1)}, u32[]{:S(2)}, u32[]{:S(2)}) collective-permute-start(f32[480,128]{1,0:T(8,128)S(1)} %get-tuple-element.42), channel_id=1, source_target_pairs={{0,7},{1,2},{2,1},{3,4},{4,3},{5,6},{6,5},{7,0},{8,15},{9,10},{10,... | collective-permute-start | bytes 737288 | tf_op jit(solution)/shard_map/ppermute | solution.py:502
  52.5 9.0 %collective-permute-start.11 = (f32[480,128]{1,0:T(8,128)S(1)}, f32[480,128]{1,0:T(8,128)S(1)}, u32[]{:S(2)}, u32[]{:S(2)}) collective-permute-start(f32[480,128]{1,0:T(8,128)S(1)} %get-tuple-element.44.refs_4_), channel_id=1, source_target_pairs={{0,7},{1,2},{2,1},{3,4},{4,3},{5,6},{6,5},{7,0},{8,15},{9,10},{10,... | collective-permute-start | bytes 737288 | tf_op jit(solution)/shard_map/ppermute | solution.py:502
  55.4 6.2 %collective-permute-start.10 = (f32[480,128]{1,0:T(8,128)S(1)}, f32[480,128]{1,0:T(8,128)S(1)}, u32[]{:S(2)}, u32[]{:S(2)}) collective-permute-start(f32[480,128]{1,0:T(8,128)S(1)} %get-tuple-element.44.refs_4_), channel_id=1, source_target_pairs={{0,1},{1,0},{2,3},{3,2},{4,5},{5,4},{6,7},{7,6},{8,9},{9,8},{10,11... | collective-permute-start | bytes 737288 | tf_op jit(solution)/shard_map/ppermute | solution.py:502
  64.5 6.1 %collective-permute-start.12 = (f32[184,128]{1,0:T(8,128)S(1)}, f32[184,128]{1,0:T(8,128)S(1)}, u32[]{:S(2)}, u32[]{:S(2)}) collective-permute-start(f32[184,128]{1,0:T(8,128)S(1)} %get-tuple-element.46), channel_id=1, source_target_pairs={{0,8},{8,0},{16,24},{24,16},{1,9},{9,1},{17,25},{25,17},{2,10},{10... | collective-permute-start | bytes 282632 | tf_op jit(solution)/shard_map/ppermute | solution.py:505
  64.6 10.6 %collective-permute-start.13 = (f32[184,128]{1,0:T(8,128)S(1)}, f32[184,128]{1,0:T(8,128)S(1)}, u32[]{:S(2)}, u32[]{:S(2)}) collective-permute-start(f32[184,128]{1,0:T(8,128)S(1)} %get-tuple-element.47), channel_id=1, source_target_pairs={{0,16},{8,24},{16,0},{24,8},{1,17},{9,25},{17,1},{25,9},{2,18},{10... | collective-permute-start | bytes 282632 | tf_op jit(solution)/shard_map/ppermute | solution.py:505
  65.7 9.5 %collective-permute-start.14 = (f32[184,128]{1,0:T(8,128)S(1)}, f32[184,128]{1,0:T(8,128)S(1)}, u32[]{:S(2)}, u32[]{:S(2)}) collective-permute-start(f32[184,128]{1,0:T(8,128)S(1)} %get-tuple-element.48), channel_id=1, source_target_pairs={{0,24},{8,16},{16,8},{24,0},{1,25},{9,17},{17,9},{25,1},{2,26},{10... | collective-permute-start | bytes 282632 | tf_op jit(solution)/shard_map/ppermute | solution.py:505
  75.4 14.1 %collective-permute-start.17 = (f32[184,128]{1,0:T(8,128)S(1)}, f32[184,128]{1,0:T(8,128)S(1)}, u32[]{:S(2)}, u32[]{:S(2)}) collective-permute-start(f32[184,128]{1,0:T(8,128)S(1)} %get-tuple-element.49.refs_0_.image0_ref), channel_id=1, source_target_pairs={{0,24},{8,16},{16,8},{24,0},{1,25},{9,17},{17,9},{25,1},{2,26},{10... | collective-permute-start | bytes 282632 | tf_op jit(solution)/shard_map/ppermute | solution.py:505
  76.7 12.7 %collective-permute-start.16 = (f32[184,128]{1,0:T(8,128)S(1)}, f32[184,128]{1,0:T(8,128)S(1)}, u32[]{:S(2)}, u32[]{:S(2)}) collective-permute-start(f32[184,128]{1,0:T(8,128)S(1)} %get-tuple-element.49.refs_0_.image0_ref), channel_id=1, source_target_pairs={{0,16},{8,24},{16,0},{24,8},{1,17},{9,25},{17,1},{25,9},{2,18},{10... | collective-permute-start | bytes 282632 | tf_op jit(solution)/shard_map/ppermute | solution.py:505
  78.7 10.8 %collective-permute-start.15 = (f32[184,128]{1,0:T(8,128)S(1)}, f32[184,128]{1,0:T(8,128)S(1)}, u32[]{:S(2)}, u32[]{:S(2)}) collective-permute-start(f32[184,128]{1,0:T(8,128)S(1)} %get-tuple-element.49.refs_0_.image0_ref), channel_id=1, source_target_pairs={{0,8},{8,0},{16,24},{24,16},{1,9},{9,1},{17,25},{25,17},{2,10},{10... | collective-permute-start | bytes 282632 | tf_op jit(solution)/shard_map/ppermute | solution.py:505
  93.2 1.6 %collective-permute-start.18 = (f32[480,128]{1,0:T(8,128)S(1)}, f32[480,128]{1,0:T(8,128)S(1)}, u32[]{:S(2)}, u32[]{:S(2)}) collective-permute-start(f32[480,128]{1,0:T(8,128)S(1)} %get-tuple-element.53), channel_id=1, source_target_pairs={{0,1},{1,0},{2,3},{3,2},{4,5},{5,4},{6,7},{7,6},{8,9},{9,8},{10,11... | collective-permute-start | bytes 737288 | tf_op jit(solution)/shard_map/ppermute | solution.py:502
  93.3 8.9 %collective-permute-start.19 = (f32[480,128]{1,0:T(8,128)S(1)}, f32[480,128]{1,0:T(8,128)S(1)}, u32[]{:S(2)}, u32[]{:S(2)}) collective-permute-start(f32[480,128]{1,0:T(8,128)S(1)} %get-tuple-element.54), channel_id=1, source_target_pairs={{0,7},{1,2},{2,1},{3,4},{4,3},{5,6},{6,5},{7,0},{8,15},{9,10},{10,... | collective-permute-start | bytes 737288 | tf_op jit(solution)/shard_map/ppermute | solution.py:502
  102.4 8.3 %collective-permute-start.21 = (f32[480,128]{1,0:T(8,128)S(1)}, f32[480,128]{1,0:T(8,128)S(1)}, u32[]{:S(2)}, u32[]{:S(2)}) collective-permute-start(f32[480,128]{1,0:T(8,128)S(1)} %get-tuple-element.57.refs_4_), channel_id=1, source_target_pairs={{0,7},{1,2},{2,1},{3,4},{4,3},{5,6},{6,5},{7,0},{8,15},{9,10},{10,... | collective-permute-start | bytes 737288 | tf_op jit(solution)/shard_map/ppermute | solution.py:502
  102.7 8.0 %collective-permute-start.20 = (f32[480,128]{1,0:T(8,128)S(1)}, f32[480,128]{1,0:T(8,128)S(1)}, u32[]{:S(2)}, u32[]{:S(2)}) collective-permute-start(f32[480,128]{1,0:T(8,128)S(1)} %get-tuple-element.57.refs_4_), channel_id=1, source_target_pairs={{0,1},{1,0},{2,3},{3,2},{4,5},{5,4},{6,7},{7,6},{8,9},{9,8},{10,11... | collective-permute-start | bytes 737288 | tf_op jit(solution)/shard_map/ppermute | solution.py:502
  113.7 5.6 %collective-permute-start.22 = (f32[184,128]{1,0:T(8,128)S(1)}, f32[184,128]{1,0:T(8,128)S(1)}, u32[]{:S(2)}, u32[]{:S(2)}) collective-permute-start(f32[184,128]{1,0:T(8,128)S(1)} %get-tuple-element.59), channel_id=1, source_target_pairs={{0,8},{8,0},{16,24},{24,16},{1,9},{9,1},{17,25},{25,17},{2,10},{10... | collective-permute-start | bytes 282632 | tf_op jit(solution)/shard_map/ppermute | solution.py:505
  114.3 10.1 %collective-permute-start.23 = (f32[184,128]{1,0:T(8,128)S(1)}, f32[184,128]{1,0:T(8,128)S(1)}, u32[]{:S(2)}, u32[]{:S(2)}) collective-permute-start(f32[184,128]{1,0:T(8,128)S(1)} %get-tuple-element.60), channel_id=1, source_target_pairs={{0,16},{8,24},{16,0},{24,8},{1,17},{9,25},{17,1},{25,9},{2,18},{10... | collective-permute-start | bytes 282632 | tf_op jit(solution)/shard_map/ppermute | solution.py:505
  115.5 8.9 %collective-permute-start.24 = (f32[184,128]{1,0:T(8,128)S(1)}, f32[184,128]{1,0:T(8,128)S(1)}, u32[]{:S(2)}, u32[]{:S(2)}) collective-permute-start(f32[184,128]{1,0:T(8,128)S(1)} %get-tuple-element.61), channel_id=1, source_target_pairs={{0,24},{8,16},{16,8},{24,0},{1,25},{9,17},{17,9},{25,1},{2,26},{10... | collective-permute-start | bytes 282632 | tf_op jit(solution)/shard_map/ppermute | solution.py:505
  (1 other events, 0.9 us)

commit v2 on v1

v2 whole, which is shorter than its diff:
```python
import functools

import jax
import jax.numpy as jnp
from jax import lax
from jax.experimental import pallas as pl
from jax.experimental.pallas import tpu as pltpu
from jax.sharding import PartitionSpec as P

RATIO = 4
HALF = 5
STEPS = 2
REACH = HALF + 1
LANES = 128
WIN = 64
MARGIN = 32
FINE = RATIO * WIN
CHUNK = 16
GROUPS = 2
F32 = jnp.float32
BF16 = jnp.bfloat16


def tent(distance):
    return max(0.0, 1.0 - abs(distance) / RATIO)


def smooth(distance):
    return (1.0 - abs(distance) / REACH) / 2 if abs(distance) <= HALF else 0.0


def window_table(fine_axis):
    shape = (FINE, LANES) if fine_axis == 0 else (LANES, FINE)
    fine = lax.broadcasted_iota(jnp.int32, shape, fine_axis).astype(F32)
    coarse = lax.broadcasted_iota(jnp.int32, shape, 1 - fine_axis).astype(F32) - MARGIN
    distance = fine + 0.5 - RATIO * coarse - RATIO / 2
    table = jnp.maximum(0.0, 1.0 - jnp.abs(distance) / RATIO).astype(BF16)
    return jnp.concatenate([table, table], axis=0)


class Sizes:
    def __init__(self, mesh, perturbations, control):
        self.n_mem = mesh.shape["mem"]
        self.n_lat = mesh.shape["lat"]
        self.members = control.shape[0]
        self.group = self.members // GROUPS
        self.rows = control.shape[1]
        self.cols = control.shape[2]
        self.vars = perturbations.shape[1]
        self.fine_rows = perturbations.shape[2]
        self.fine_cols = perturbations.shape[3]
        assert self.rows == REACH and self.cols % LANES == WIN
        assert self.fine_rows == RATIO * self.rows and self.fine_cols == RATIO * self.cols
        self.windows = self.cols // WIN
        self.ext = self.cols + 2 * MARGIN
        self.slab = self.rows * self.group
        self.full = self.cols // LANES
        self.packed = self.full * self.slab + self.slab // 2
        self.field_rows = self.vars * self.fine_rows
        self.share = self.fine_cols // self.n_mem
        self.share_full = self.share // LANES
        self.share_rem = self.share % LANES
        self.groups = LANES // self.share_rem if self.share_rem else 1
        self.rem_rows = -(-self.field_rows // 8 // self.groups) * 8 if self.share_rem else 0
        self.share_rows = self.share_full * self.field_rows + self.rem_rows
        self.field_tiles = self.fine_cols // LANES
        self.part_rows = -(-self.field_tiles * self.field_rows // 8 // self.n_mem) * 8
        self.list_rows = self.part_rows * self.n_mem


def lane(shape):
    return lax.broadcasted_iota(jnp.int32, shape, 1)


def half_turn(x):
    return pltpu.roll(x, WIN, 1)


def pack_slab(size, first, last, middle):
    rows = size.slab
    at = lane((rows, LANES))
    pieces = list(middle)
    pieces.append(jnp.where(at < LANES - MARGIN, last, first))
    half = rows // 2
    at = lane((half, LANES))
    inner = (at >= MARGIN) & (at < LANES - MARGIN)
    pieces.append(jnp.where(inner, first[:half], half_turn(first[half:])))
    return pieces


def unpack_slab(size, packed):
    rows = size.slab
    middle = [packed[i * rows : (i + 1) * rows] for i in range(size.full - 1)]
    mixed = packed[(size.full - 1) * rows : size.full * rows]
    rest = packed[size.full * rows :]
    rest = jnp.concatenate([rest, half_turn(rest)], axis=0)
    at = lane((rows, LANES))
    first = jnp.where(at < MARGIN, half_turn(mixed), jnp.where(at < LANES - MARGIN, rest, mixed))
    last = jnp.where(at < LANES - MARGIN, mixed, half_turn(rest))
    return [first] + middle + [last]


def tiles_of(ref, count):
    return [ref[:, i * LANES : (i + 1) * LANES] for i in range(count)]


def put_packed(out, pieces):
    at = 0
    for piece in pieces:
        out[at : at + piece.shape[0], :] = piece
        at += piece.shape[0]


def pack_ref(size, out, tiles):
    put_packed(out, pack_slab(size, tiles[0], tiles[-1], tiles[1:-1]))


def place():
    lat = lax.axis_index("lat")
    odd = lax.rem(lat, 2) == 1
    low = (lat > 0).astype(F32)
    high = (lat < lax.axis_size("lat") - 1).astype(F32)
    return odd, low, high


def sides(a, b):
    odd, low, high = place()
    lower = jnp.where(odd, a, b) * low
    upper = jnp.where(odd, b, a) * high
    return lower, upper


def step_length(scal_ref):
    total = jnp.sum(scal_ref[...], axis=0, keepdims=True)
    at = lane(total.shape)
    grad_sq = jnp.sum(jnp.where(at == 0, total, 0.0), axis=1, keepdims=True)
    image_sq = jnp.sum(jnp.where(at == 1, total, 0.0), axis=1, keepdims=True)
    return grad_sq / (grad_sq + image_sq)


def enter_kernel(size, control_ref, *outs):
    for g in range(GROUPS):
        own_ref, packed_ref = outs[2 * g : 2 * g + 2]
        x = jnp.concatenate(
            [
                control_ref[pl.ds(r * size.members + g * size.group, size.group), :]
                for r in range(size.rows)
            ],
            axis=0,
        )
        own_ref[...] = jnp.concatenate([x[:, size.cols - MARGIN :], x, x[:, :MARGIN]], axis=1)
        pack_ref(size, packed_ref, tiles_of(own_ref, size.ext // LANES))


def load_kernel(pert_ref, out_ref, sems):
    count = sems.shape[0]
    part = pert_ref.shape[0] // count
    copies = [
        pltpu.make_async_copy(
            pert_ref.at[pl.ds(i * part, part)], out_ref.at[pl.ds(i * part, part)], sems.at[i]
        )
        for i in range(count)
    ]
    for copy in copies:
        copy.start()
    for copy in copies:
        copy.wait()


def forward_kernel(size, g, shares, own_ref, a_ref, b_ref, pert_ref, *rest):
    rest = list(rest)
    start_ref = rest.pop(0) if g else None
    last = g == GROUPS - 1
    outs = [rest.pop(0) for i in range(size.n_mem if last else 1)]
    ext_ref, coarse_ref, rows_ref = rest[:3]
    acc_ref = rest[3] if last else outs[0]
    members = size.group
    n_tiles = size.ext // LANES
    fine_rows = size.fine_rows

    unused, low, high = place()
    lower, upper = sides(a_ref[...], b_ref[...])
    lower = unpack_slab(size, lower)
    upper = unpack_slab(size, upper)
    n = size.slab
    for e in range(n_tiles):
        cut = slice(e * LANES, (e + 1) * LANES)
        ext_ref[0:n, cut] = lower[e]
        ext_ref[n : 2 * n, cut] = own_ref[:, cut]
        ext_ref[2 * n : 3 * n, cut] = upper[e]
    for e in range(n_tiles):
        cut = slice(e * LANES, (e + 1) * LANES)
        for at in range(0, members, 8):
            held = [
                ext_ref[k * members + at : k * members + at + 8, cut] for k in range(3 * REACH)
            ]
            for j in range(size.rows + 2):
                total = None
                for k in range(3 * REACH):
                    weight = smooth(j - 1 - (k - REACH))
                    if weight:
                        term = held[k] * weight
                        total = term if total is None else total + term
                if j == 0:
                    total = total * low
                if j == size.rows + 1:
                    total = total * high
                coarse_ref[j * members + at : j * members + at + 8, cut] = total
    for t in range(size.windows):
        e = t // 2
        held = []
        for j in range(size.rows + 2):
            at = slice(j * members, (j + 1) * members)
            value = coarse_ref[at, e * LANES : (e + 1) * LANES]
            if t % 2:
                other = coarse_ref[at, (e + 1) * LANES : (e + 2) * LANES]
                value = half_turn(jnp.where(lane(value.shape) < WIN, other, value))
            held.append(value)
        for i in range(fine_rows):
            total = None
            for j in range(size.rows + 2):
                weight = tent(i + 0.5 - RATIO * (j - 1) - RATIO / 2)
                if weight:
                    term = held[j] * weight
                    total = term if total is None else total + term
            rows_ref[t, pl.ds(i, members, stride=fine_rows), :] = total
    table = window_table(1)
    block = CHUNK * fine_rows

    def chunk(step, unused):
        first = pl.multiple_of(step * block, 8)
        for t in range(size.windows):
            x = rows_ref[t, pl.ds(first, block), :]
            head = x.astype(BF16)
            tail = (x - head.astype(F32)).astype(BF16)
            refined = jnp.dot(
                jnp.concatenate([head, tail], axis=1), table, preferred_element_type=F32
            )
            for e in range(t * FINE // LANES, (t + 1) * FINE // LANES):
                cut = slice(e * LANES, (e + 1) * LANES)
                here = slice(e * LANES - t * FINE, (e + 1) * LANES - t * FINE)
                rows = [
                    pl.ds(e * size.field_rows + v * fine_rows, fine_rows)
                    for v in range(size.vars)
                ]
                totals = [acc_ref[at, :] for at in rows]
                for m in range(CHUNK):
                    value = refined[m * fine_rows : (m + 1) * fine_rows, here]
                    for v in range(size.vars):
                        pert = pert_ref[g * members + step * CHUNK + m, v, :, cut].astype(F32)
                        totals[v] = totals[v] + pert * value
                for v in range(size.vars):
                    acc_ref[rows[v], :] = totals[v]
        return unused

    if g:
        acc_ref[...] = start_ref[...]
    else:
        acc_ref[...] = jnp.zeros_like(acc_ref)
    lax.fori_loop(0, members // CHUNK, chunk, 0)
    if not last:
        return
    mine = lax.axis_index("mem")
    if shares:
        parts_ref = rest[4]
        for q in range(size.n_mem):
            put_share(size, parts_ref.at[q], acc_ref, q * size.share)
        for d in range(size.n_mem):
            outs[d][...] = parts_ref[mine ^ d]
    else:
        for d in range(size.n_mem):
            first = pl.multiple_of((mine ^ d) * size.part_rows, 8)
            outs[d][...] = acc_ref[pl.ds(first, size.part_rows), :]


def field_tile(size, list_ref, start):
    e, shift = start // LANES, start % LANES
    rows = size.field_rows
    tile = list_ref[e * rows : (e + 1) * rows, :]
    if shift == 0:
        return tile
    if e + 1 < size.field_tiles:
        other = list_ref[(e + 1) * rows : (e + 2) * rows, :]
        tile = jnp.where(lane(tile.shape) < shift, other, tile)
    return pltpu.roll(tile, LANES - shift, 1)


def put_share(size, out, list_ref, start):
    rows = size.field_rows
    for j in range(size.share_full):
        out[j * rows : (j + 1) * rows, :] = field_tile(size, list_ref, start + j * LANES)
    if size.share_rem:
        tile = field_tile(size, list_ref, start + size.share_full * LANES)
        tile = jnp.where(lane(tile.shape) < size.share_rem, tile, 0.0)
        missing = size.rem_rows * size.groups - rows
        if missing:
            tile = jnp.concatenate([tile, jnp.zeros((missing, LANES), F32)], axis=0)
        total = None
        for g in range(size.groups):
            term = tile[g * size.rem_rows : (g + 1) * size.rem_rows]
            if g:
                term = pltpu.roll(term, g * size.share_rem, 1)
            total = term if total is None else total + term
        out[size.share_full * rows :, :] = total


def share_tiles(size, part):
    rows = size.field_rows
    tiles = [(part[j * rows : (j + 1) * rows], LANES) for j in range(size.share_full)]
    if size.share_rem:
        rest = part[size.share_full * rows :]
        stack = [rest]
        for g in range(1, size.groups):
            stack.append(pltpu.roll(rest, LANES - g * size.share_rem, 1))
        tiles.append((jnp.concatenate(stack, axis=0)[:rows], size.share_rem))
    return tiles


def total_kernel(count, *refs):
    parts, out_ref = refs[:count], refs[count]
    total = parts[0][...]
    for part in parts[1:]:
        total = total + part[...]
    out_ref[...] = total


def squares_kernel(count, *refs):
    parts, grads = refs[:count], refs[count : count + GROUPS]
    out_ref, scal_ref = refs[count + GROUPS :]
    total = parts[0][...]
    for part in parts[1:]:
        total = total + part[...]
    out_ref[...] = total
    image_sq = jnp.sum(total * total)
    grad_sq = sum(jnp.sum(grad[...] * grad[...]) for grad in grads)
    at = lane(scal_ref.shape)
    scal_ref[...] = jnp.where(at == 0, grad_sq, jnp.where(at == 1, image_sq, 0.0))


def misfit_of(size, parts, before_ref, scal_ref, innov_ref, limit_ref, list_ref, misfit_ref):
    fine_rows = size.fine_rows
    mine = lax.axis_index("mem")
    for d in range(size.n_mem):
        first = pl.multiple_of((mine ^ d) * size.part_rows, 8)
        list_ref[pl.ds(first, size.part_rows), :] = parts[d][...]
    if before_ref is not None:
        length = step_length(scal_ref)
    for e in range(size.field_tiles):
        cut = slice(e * LANES, (e + 1) * LANES)
        for v in range(size.vars):
            at = pl.ds(e * size.field_rows + v * fine_rows, fine_rows)
            value = list_ref[at, :]
            if before_ref is not None:
                value = before_ref[at, :] - length * value
            limit = limit_ref[:, v : v + 1]
            misfit_ref[at, :] = jnp.clip(value - innov_ref[v, :, cut], -limit, limit)


def adjoint_kernel(size, g, later, *refs):
    refs = list(refs)
    pert_ref = refs.pop(0)
    if g == 0:
        parts = [refs.pop(0) for i in range(size.n_mem)]
        scal_ref, before_ref = (refs.pop(0), refs.pop(0)) if later else (None, None)
        innov_ref, limit_ref = refs.pop(0), refs.pop(0)
    else:
        misfit_ref = refs.pop(0)
    a_ref, b_ref, own_ref = refs[:3]
    refs = refs[3:]
    if g == 0:
        misfit_ref = refs.pop(0)
        list_ref = refs.pop(0)
    cols_ref, coarse_ref, spread_ref = refs[:3]
    members = size.group
    n_tiles = size.ext // LANES
    fine_rows = size.fine_rows
    if g == 0:
        misfit_of(size, parts, before_ref, scal_ref, innov_ref, limit_ref, list_ref, misfit_ref)
    table = window_table(0)
    block = CHUNK * fine_rows

    def chunk(step, unused):
        first = pl.multiple_of(step * block, 8)
        tops = [None] * n_tiles
        for t in range(size.windows):
            cut = slice(t * FINE, (t + 1) * FINE)
            tiles = range(t * FINE // LANES, (t + 1) * FINE // LANES)
            mis = [
                jnp.concatenate(
                    [
                        misfit_ref[pl.ds(e * size.field_rows + v * fine_rows, fine_rows), :]
                        for e in tiles
                    ],
                    axis=1,
                )
                for v in range(size.vars)
            ]
            weighted = []
            for m in range(CHUNK):
                total = pert_ref[g * members + step * CHUNK + m, 0, :, cut].astype(F32) * mis[0]
                for v in range(1, size.vars):
                    total = total + pert_ref[g * members + step * CHUNK + m, v, :, cut].astype(F32) * mis[v]
                weighted.append(total)
            x = jnp.concatenate(weighted, axis=0)
            head = x.astype(BF16)
            tail = (x - head.astype(F32)).astype(BF16)
            columns = jnp.dot(
                jnp.concatenate([head, tail], axis=1), table, preferred_element_type=F32
            )
            e = t // 2
            if t % 2 == 0:
                tops[e] = columns if tops[e] is None else tops[e] + columns
            else:
                turned = half_turn(columns)
                at = lane(turned.shape)
                tops[e] = tops[e] + jnp.where(at >= WIN, turned, 0.0)
                tops[e + 1] = jnp.where(at < WIN, turned, 0.0)
        for e in range(n_tiles):
            cols_ref[e, pl.ds(first, block), :] = tops[e]
        return unused

    lax.fori_loop(0, members // CHUNK, chunk, 0)
    odd, low, high = place()
    for e in range(n_tiles):
        cut = slice(e * LANES, (e + 1) * LANES)
        sums = [None] * (size.rows + 2)
        for i in range(fine_rows):
            value = cols_ref[e, pl.ds(i, members, stride=fine_rows), :]
            for j in range(size.rows + 2):
                weight = tent(i + 0.5 - RATIO * (j - 1) - RATIO / 2)
                if weight:
                    term = value * weight
                    sums[j] = term if sums[j] is None else sums[j] + term
        sums[0] = sums[0] * low
        sums[-1] = sums[-1] * high
        for j in range(size.rows + 2):
            coarse_ref[j * members : (j + 1) * members, cut] = sums[j]
    head = coarse_ref[:, 0:LANES]
    tail = coarse_ref[:, (n_tiles - 1) * LANES :]
    at = lane(head.shape)
    turned_head, turned_tail = half_turn(head), half_turn(tail)
    coarse_ref[:, 0:LANES] = head + jnp.where(at < WIN, turned_tail, 0.0)
    coarse_ref[:, (n_tiles - 1) * LANES :] = tail + jnp.where(at >= WIN, turned_head, 0.0)
    for e in range(n_tiles):
        cut = slice(e * LANES, (e + 1) * LANES)
        for at in range(0, members, 8):
            held = [
                coarse_ref[j * members + at : j * members + at + 8, cut]
                for j in range(size.rows + 2)
            ]
            for k in range(3 * REACH):
                total = None
                for j in range(size.rows + 2):
                    weight = smooth(j - 1 - (k - REACH))
                    if weight:
                        term = held[j] * weight
                        total = term if total is None else total + term
                spread_ref[k * members + at : k * members + at + 8, cut] = total
    n = size.slab

    def packed_of(part):
        tiles = [
            spread_ref[part * n : (part + 1) * n, e * LANES : (e + 1) * LANES]
            for e in range(n_tiles)
        ]
        return pack_slab(size, tiles[0], tiles[-1], tiles[1:-1])

    lower, upper = packed_of(0), packed_of(2)
    own_ref[...] = spread_ref[n : 2 * n, :]
    put_packed(a_ref, [jnp.where(odd, x, y) for x, y in zip(lower, upper)])
    put_packed(b_ref, [jnp.where(odd, y, x) for x, y in zip(lower, upper)])


def gradient_kernel(size, later, *refs):
    refs = list(refs)
    own_ref, a_ref, b_ref, weights_ref = refs[:4]
    refs = refs[4:]
    weights = weights_ref[...]
    if later:
        scal_ref, before_ref = refs.pop(0), refs.pop(0)
        weights = weights - step_length(scal_ref) * before_ref[...]
    grad_ref, packed_ref = refs[:2]
    if later:
        refs[2][...] = weights
    lower, upper = sides(a_ref[...], b_ref[...])
    arrived = unpack_slab(size, lower + upper)
    for e in range(size.ext // LANES):
        cut = slice(e * LANES, (e + 1) * LANES)
        grad_ref[:, cut] = weights[:, cut] + own_ref[:, cut] + arrived[e]
    pack_ref(size, packed_ref, tiles_of(grad_ref, size.ext // LANES))


def own_share_kernel(size, before_ref, image_ref, scal_ref, out_ref, list_ref, shares_ref):
    list_ref[...] = before_ref[...] - step_length(scal_ref) * image_ref[...]
    for q in range(size.n_mem):
        put_share(size, shares_ref.at[q], list_ref, q * size.share)
    out_ref[...] = shares_ref[lax.axis_index("mem")]


def leave_kernel(size, *refs):
    weights_refs, grad_refs = refs[:GROUPS], refs[GROUPS : 2 * GROUPS]
    field_ref, image_ref, scal1_ref = refs[2 * GROUPS : 2 * GROUPS + 3]
    out_weights_ref, out_field_ref = refs[2 * GROUPS + 3 :]
    second = step_length(scal1_ref)
    n_tiles = size.ext // LANES
    for g in range(GROUPS):
        weights = weights_refs[g][...] - second * grad_refs[g][...]
        tiles = [weights[:, e * LANES : (e + 1) * LANES] for e in range(n_tiles)]
        for e in range(n_tiles):
            tile = tiles[e]
            if e + 1 < n_tiles:
                tile = jnp.where(lane(tile.shape) < MARGIN, tiles[e + 1], tile)
            tile = pltpu.roll(tile, LANES - MARGIN, 1)
            start = e * LANES
            width = min(LANES, size.cols - start)
            for r in range(size.rows):
                to = pl.ds(r * size.members + g * size.group, size.group)
                rows = slice(r * size.group, (r + 1) * size.group)
                out_weights_ref[to, start : start + width] = tile[rows, :width]
    field = field_ref[...] - second * image_ref[...]
    start = 0
    for tile, width in share_tiles(size, field):
        for v in range(size.vars):
            rows = slice(v * size.fine_rows, (v + 1) * size.fine_rows)
            out_field_ref[v, :, start : start + width] = tile[rows, :width]
        start += width


def whole():
    return pl.BlockSpec(memory_space=pltpu.VMEM)


def params():
    return pltpu.CompilerParams(vmem_limit_bytes=24 * 1024 * 1024)


def array(*shape):
    return jax.ShapeDtypeStruct(shape, F32)


def call(kernel, outs, *args, scratch=(), flops=0, spaces=None):
    spaces = spaces or [
        pltpu.MemorySpace.SMEM if arg.ndim == 1 else pltpu.MemorySpace.VMEM for arg in args
    ]
    moved = sum(arg.size * arg.dtype.itemsize for arg in args)
    return pl.pallas_call(
        kernel,
        out_shape=outs,
        in_specs=[pl.BlockSpec(memory_space=space) for space in spaces],
        out_specs=jax.tree.map(lambda unused: whole(), outs),
        scratch_shapes=scratch,
        compiler_params=params(),
        cost_estimate=pl.CostEstimate(flops=flops, bytes_accessed=moved, transcendentals=0),
    )(*args)


def per_device(mesh, perturbations, control, innovations, thresholds):
    size = Sizes(mesh, perturbations, control)
    n_mem, n_lat, members = size.n_mem, size.n_lat, size.members
    devices = n_mem * n_lat
    pairs = [(i, i ^ 1) for i in range(n_lat)]
    cross = [(i, (i - 1 if i % 2 == 0 else i + 1) % n_lat) for i in range(n_lat)]
    far_first = sorted(range(1, n_mem), key=lambda d: -d)
    groups = range(GROUPS)
    slab = array(size.slab, size.ext)
    packed = array(size.packed, LANES)
    part = array(size.part_rows, LANES)
    share = array(size.share_rows, LANES)
    scal = array(devices, LANES)
    field = array(size.list_rows, LANES)
    map_flops = 4 * size.group * size.fine_rows * size.fine_cols * 2 * LANES

    def swap(to_a, to_b):
        return lax.ppermute(to_a, "lat", pairs), lax.ppermute(to_b, "lat", cross)

    def exchange(parts):
        moved = {
            d: lax.ppermute(parts[d], "mem", [(i, i ^ d) for i in range(n_mem)])
            for d in far_first
        }
        return [parts[0]] + [moved[d] for d in range(1, n_mem)]

    def forward(owns, arrived, shares=False):
        acc = []
        piece = share if shares else part
        for g in groups:
            last = g == GROUPS - 1
            scratch = [
                pltpu.VMEM((3 * size.slab, size.ext), F32),
                pltpu.VMEM(((size.rows + 2) * size.group, size.ext), F32),
                pltpu.VMEM((size.windows, size.group * size.fine_rows, LANES), F32),
            ]
            if last:
                scratch.append(pltpu.VMEM(field.shape, F32))
                if shares:
                    scratch.append(pltpu.VMEM((n_mem, *piece.shape), F32))
            acc = call(
                functools.partial(forward_kernel, size, g, shares),
                [piece] * n_mem if last else [field],
                owns[g],
                *arrived[g],
                resident,
                *acc,
                scratch=scratch,
                flops=map_flops,
            )
        return exchange(acc)

    def adjoint(parts, *step):
        later = len(step) > 0
        sent, spread, misfit, whole_field = [], [], None, None
        for g in groups:
            scratch = [
                pltpu.VMEM((size.ext // LANES, size.group * size.fine_rows, LANES), F32),
                pltpu.VMEM(((size.rows + 2) * size.group, size.ext), F32),
                pltpu.VMEM((3 * size.slab, size.ext), F32),
            ]
            outs = [packed, packed, slab]
            args = [misfit]
            if g == 0:
                outs += [field, field]
                args = [*parts, *step, innovations, thresholds.reshape(1, size.vars)]
            results = call(
                functools.partial(adjoint_kernel, size, g, later),
                outs,
                resident,
                *args,
                scratch=scratch,
                flops=map_flops,
            )
            sent.append(swap(*results[:2]))
            spread.append(results[2])
            if g == 0:
                misfit = results[3]
                whole_field = results[4]
        return sent, spread, whole_field

    def gradient(arrived, spread, weights, *step):
        later = len(step) > 0
        grads, sent, olds = [], [], []
        for g in groups:
            results = call(
                functools.partial(gradient_kernel, size, later),
                [slab, packed] + ([slab] if later else []),
                spread[g],
                *arrived[g],
                weights[g],
                *([step[0], step[1][g]] if later else []),
            )
            grads.append(results[0])
            sent.append(results[1])
            olds.append(results[2] if later else weights[g])
        return grads, sent, olds

    def squares(parts, sent):
        return call(
            functools.partial(squares_kernel, n_mem),
            [array(*parts[0].shape), scal],
            *parts,
            *sent,
        )

    def everywhere(tile):
        moved = lax.all_to_all(tile.reshape(devices, 1, LANES), ("mem", "lat"), 0, 0)
        return moved.reshape(devices, LANES)

    def both(sent):
        return [swap(x, x) for x in sent]

    entered = call(
        functools.partial(enter_kernel, size),
        [slab, packed] * GROUPS,
        control.transpose(1, 0, 2).reshape(size.rows * members, size.cols),
    )
    control_own, sent = entered[0::2], entered[1::2]
    copies = min(4, members)
    resident = call(
        load_kernel,
        jax.ShapeDtypeStruct(perturbations.shape, perturbations.dtype),
        perturbations,
        scratch=[pltpu.SemaphoreType.DMA((copies,))],
        spaces=[pltpu.MemorySpace.HBM],
        flops=2 * map_flops,
    )
    parts = forward(control_own, both(sent))
    field0 = call(functools.partial(total_kernel, n_mem), part, *parts)
    arrived, spread, before = adjoint(exchange([field0] * n_mem))
    grads0, sent, unused = gradient(arrived, spread, control_own)
    parts = forward(grads0, both(sent))
    image0, scal0 = squares(parts, sent)
    images = exchange([image0] * n_mem)
    scal0 = everywhere(scal0)
    arrived, spread, image_all = adjoint(images, scal0, before)
    grads1, sent, weights1 = gradient(arrived, spread, control_own, scal0, grads0)
    own_share = call(
        functools.partial(own_share_kernel, size),
        share,
        before,
        image_all,
        scal0,
        scratch=[pltpu.VMEM(field.shape, F32), pltpu.VMEM((n_mem, *share.shape), F32)],
        flops=map_flops // 8,
    )
    parts = forward(grads1, both(sent), shares=True)
    image1, scal1 = squares(parts, sent)
    scal1 = everywhere(scal1)
    weights, result = call(
        functools.partial(leave_kernel, size),
        [
            array(size.rows * members, size.cols),
            array(size.vars, size.fine_rows, size.share),
        ],
        *weights1,
        *grads1,
        own_share,
        image1,
        scal1,
    )
    return weights.reshape(size.rows, members, size.cols).transpose(1, 0, 2), result


def solution(mesh):
    return jax.shard_map(
        functools.partial(per_device, mesh),
        mesh=mesh,
        in_specs=(P("mem", None, "lat", None), P("mem", "lat", None), P(None, "lat", None), P()),
        out_specs=(P("mem", "lat", None), P(None, "lat", "mem")),
        check_vma=False,
    )
```

time: 135 us -> 120 us (0.89)
  waiting for transfers between devices: 57.8 us -> 44.6 us
  starting transfers between devices: 34.7 us -> 43.4 us
  blocking collectives: 18.5 us -> 9.91 us
    ppermute x10 -> x20, waiting for transfers between devices: 34.1 us -> 14.8 us  [swap(): return (lax.ppermute(to_a, 'lat', pairs), lax.ppermute(to_b, 'lat', cross))]
    all_to_all x2 -> x1, blocking collectives: 18.5 us -> 9.91 us  [everywhere(): lax.all_to_all(tile.reshape(devices, 1, LANES), ('mem', 'lat'), 0, 0)]
    all_to_all x0 -> x1, waiting for transfers between devices: none -> 6.8 us  [everywhere(): lax.all_to_all(tile.reshape(devices, 1, LANES), ('mem', 'lat'), 0, 0)]
    ppermute x10 -> x20, starting transfers between devices: 11.2 us -> 16.6 us  [swap(): return (lax.ppermute(to_a, 'lat', pairs), lax.ppermute(to_b, 'lat', cross))]
    all_to_all x0 -> x1, starting transfers between devices: none -> 3.19 us  [everywhere(): lax.all_to_all(tile.reshape(devices, 1, LANES), ('mem', 'lat'), 0, 0)]
    pallas_call x12 -> x21, Pallas kernels: 18.1 us -> 16.8 us  [call(): pl.pallas_call(kernel, out_shape=outs, in_specs=[pl.BlockSpec(memory_spac...]
    unnamed x16 -> x8, local copies, waits for them, and re-layouts: 4.59 us -> 3.64 us
  transfers between devices with their start and end apart: 25 -> 36, of which waited for: 15 -> 18; matrix products, arithmetic and copies ran while one was open for 0% -> 0% of each run, Pallas kernels for 0% -> 7%
where the time goes in v2:
time: 120 us; the launch traced here: 119 us
  waiting for transfers between devices  44.6 us (37%)
  starting transfers between devices  43.4 us (36%)
  Pallas kernels  16.8 us (14%)
  blocking collectives  9.91 us (8%)
  local copies, waits for them, and re-layouts  3.64 us (3%)
    ppermute x15, starting transfers between devices, exchange(): lax.ppermute(parts[d], 'mem', [(i, i ^ d) for i in range(n_mem)])  23.6 us
    ppermute x15, waiting for transfers between devices, exchange(): lax.ppermute(parts[d], 'mem', [(i, i ^ d) for i in range(n_mem)])  23 us
    pallas_call x21, Pallas kernels, call(): pl.pallas_call(kernel, out_shape=outs, in_specs=[pl.BlockSpec(memory_spac...  16.8 us
    ppermute x20, starting transfers between devices, swap(): return (lax.ppermute(to_a, 'lat', pairs), lax.ppermute(to_b, 'lat', cross))  16.6 us
    ppermute x20, waiting for transfers between devices, swap(): return (lax.ppermute(to_a, 'lat', pairs), lax.ppermute(to_b, 'lat', cross))  14.8 us
    all_to_all x1, blocking collectives, everywhere(): lax.all_to_all(tile.reshape(devices, 1, LANES), ('mem', 'lat'), 0, 0)  9.91 us
    all_to_all x1, waiting for transfers between devices, everywhere(): lax.all_to_all(tile.reshape(devices, 1, LANES), ('mem', 'lat'), 0, 0)  6.8 us
    unnamed x8, local copies, waits for them, and re-layouts  3.64 us
  transfers between devices with their start and end apart: 36, of which 18 were waited for; matrix products, arithmetic and copies ran while one was open for 0% of the time, Pallas kernels for 7%

profile of v2, /device:TPU:0, one launch (start us, length us, event | category | flops | bytes accessed | tf_op | source)
XLA Modules:
  0.0 119.3 jit_solution(3125291481610252204)
XLA Ops:
  1.8 3.4 %collective-permute-start.3 = (f32[240,128]{1,0:T(8,128)S(1)}, f32[240,128]{1,0:T(8,128)S(1)}, u32[]{:S(2)}, u32[]{:S(2)}) collective-permute-start(f32[240,128]{1,0:T(8,128)S(1)} %get-tuple-element.53), channel_id=1, source_target_pairs={{0,7},{1,2},{2,1},{3,4},{4,3},{5,6},{6,5},{7,0},{8,15},{9,10},{10,... | collective-permute-start | bytes 368648 | tf_op jit(solution)/shard_map/ppermute | solution.py:574
  6.6 2.7 %copy-done = bf16[32,3,24,1280]{3,2,1,0:T(8,128)(2,1)S(1)} copy-done((bf16[32,3,24,1280]{3,2,1,0:T(8,128)(2,1)S(1)}, bf16[32,3,24,1280]{3,2,1,0:T(8,128)(2,1)}, u32[]{:S(2)}) %copy-start) | copy-done | bytes 5898264
  12.9 2.3 %collective-permute-start.4 = (f32[184,128]{1,0:T(8,128)S(1)}, f32[184,128]{1,0:T(8,128)S(1)}, u32[]{:S(2)}, u32[]{:S(2)}) collective-permute-start(f32[184,128]{1,0:T(8,128)S(1)} %get-tuple-element.55), channel_id=1, source_target_pairs={{0,8},{8,0},{16,24},{24,16},{1,9},{9,1},{17,25},{25,17},{2,10},{10... | collective-permute-start | bytes 282632 | tf_op jit(solution)/shard_map/ppermute | solution.py:578
  15.2 2.6 %collective-permute-start.5 = (f32[184,128]{1,0:T(8,128)S(1)}, f32[184,128]{1,0:T(8,128)S(1)}, u32[]{:S(2)}, u32[]{:S(2)}) collective-permute-start(f32[184,128]{1,0:T(8,128)S(1)} %get-tuple-element.56), channel_id=1, source_target_pairs={{0,16},{8,24},{16,0},{24,8},{1,17},{9,25},{17,1},{25,9},{2,18},{10... | collective-permute-start | bytes 282632 | tf_op jit(solution)/shard_map/ppermute | solution.py:578
  17.8 7.0 %collective-permute-done.5.refs_2_ = f32[184,128]{1,0:T(8,128)S(1)} collective-permute-done((f32[184,128]{1,0:T(8,128)S(1)}, f32[184,128]{1,0:T(8,128)S(1)}, u32[]{:S(2)}, u32[]{:S(2)}) %collective-permute-start.5) | collective-permute-done | bytes 94240 | tf_op jit(solution)/shard_map/ppermute | solution.py:578
  24.9 2.5 %collective-permute-start.9 = (f32[184,128]{1,0:T(8,128)S(1)}, f32[184,128]{1,0:T(8,128)S(1)}, u32[]{:S(2)}, u32[]{:S(2)}) collective-permute-start(f32[184,128]{1,0:T(8,128)S(1)} %shard_map.63.refs_1_), channel_id=1, source_target_pairs={{0,24},{8,16},{16,8},{24,0},{1,25},{9,17},{17,9},{25,1},{2,26},{10... | collective-permute-start | bytes 282632 | tf_op jit(solution)/shard_map/ppermute | solution.py:578
  27.9 1.4 %collective-permute-start.7 = (f32[184,128]{1,0:T(8,128)S(1)}, f32[184,128]{1,0:T(8,128)S(1)}, u32[]{:S(2)}, u32[]{:S(2)}) collective-permute-start(f32[184,128]{1,0:T(8,128)S(1)} %shard_map.63.refs_1_), channel_id=1, source_target_pairs={{0,8},{8,0},{16,24},{24,16},{1,9},{9,1},{17,25},{25,17},{2,10},{10... | collective-permute-start | bytes 282632 | tf_op jit(solution)/shard_map/ppermute | solution.py:578
  29.3 2.9 %collective-permute-done.9.refs_4_ = f32[184,128]{1,0:T(8,128)S(1)} collective-permute-done((f32[184,128]{1,0:T(8,128)S(1)}, f32[184,128]{1,0:T(8,128)S(1)}, u32[]{:S(2)}, u32[]{:S(2)}) %collective-permute-start.9) | collective-permute-done | bytes 94240 | tf_op jit(solution)/shard_map/ppermute | solution.py:578
  32.2 2.9 %collective-permute-done.8.refs_3_ = f32[184,128]{1,0:T(8,128)S(1)} collective-permute-done((f32[184,128]{1,0:T(8,128)S(1)}, f32[184,128]{1,0:T(8,128)S(1)}, u32[]{:S(2)}, u32[]{:S(2)}) %collective-permute-start.8) | collective-permute-done | bytes 94240 | tf_op jit(solution)/shard_map/ppermute | solution.py:578
  35.1 1.4 %shard_map.64 = (f32[240,128]{1,0:T(8,128)S(1)}, f32[240,128]{1,0:T(8,128)S(1)}, f32[96,384]{1,0:T(8,128)S(1)}, f32[736,128]{1,0:T(8,128)S(1)}, f32[736,128]{1,0:T(8,128)S(1)}) custom-call(bf16[32,3,24,1280]{3,2,1,0:T(8,128)(2,1)S(1)} %shard_map.59.pert_ref.refs_0_, f32[184,128]{1,0:T(8,128)S(1)} %shard_map.63.refs_1_, ...), custom_call_target="tpu_custom_call" | custom-call | flops 503316480 | bytes 6643724 | tf_op jit(solution)/shard_map/pallas_call | solution.py:546
  36.6 2.1 %collective-permute-start.15 = (f32[240,128]{1,0:T(8,128)S(1)}, f32[240,128]{1,0:T(8,128)S(1)}, u32[]{:S(2)}, u32[]{:S(2)}) collective-permute-start(f32[240,128]{1,0:T(8,128)S(1)} %get-tuple-element.66), channel_id=1, source_target_pairs={{0,7},{1,2},{2,1},{3,4},{4,3},{5,6},{6,5},{7,0},{8,15},{9,10},{10,... | collective-permute-start | bytes 368648 | tf_op jit(solution)/shard_map/ppermute | solution.py:574
  42.4 2.8 %collective-permute-start.17 = (f32[240,128]{1,0:T(8,128)S(1)}, f32[240,128]{1,0:T(8,128)S(1)}, u32[]{:S(2)}, u32[]{:S(2)}) collective-permute-start(f32[240,128]{1,0:T(8,128)S(1)} %get-tuple-element.68.refs_4_), channel_id=1, source_target_pairs={{0,7},{1,2},{2,1},{3,4},{4,3},{5,6},{6,5},{7,0},{8,15},{9,10},{10,... | collective-permute-start | bytes 368648 | tf_op jit(solution)/shard_map/ppermute | solution.py:574
  45.3 1.9 %collective-permute-done.11.refs_2_ = f32[240,128]{1,0:T(8,128)S(1)} collective-permute-done((f32[240,128]{1,0:T(8,128)S(1)}, f32[240,128]{1,0:T(8,128)S(1)}, u32[]{:S(2)}, u32[]{:S(2)}) %collective-permute-start.11) | collective-permute-done | bytes 122912 | tf_op jit(solution)/shard_map/ppermute | solution.py:574
  48.1 1.7 %collective-permute-done.17.b_ref = f32[240,128]{1,0:T(8,128)S(1)} collective-permute-done((f32[240,128]{1,0:T(8,128)S(1)}, f32[240,128]{1,0:T(8,128)S(1)}, u32[]{:S(2)}, u32[]{:S(2)}) %collective-permute-start.17) | collective-permute-done | bytes 122912 | tf_op jit(solution)/shard_map/ppermute | solution.py:574
  50.9 2.7 %collective-permute-done.13.b_ref = f32[240,128]{1,0:T(8,128)S(1)} collective-permute-done((f32[240,128]{1,0:T(8,128)S(1)}, f32[240,128]{1,0:T(8,128)S(1)}, u32[]{:S(2)}, u32[]{:S(2)}) %collective-permute-start.13) | collective-permute-done | bytes 122912 | tf_op jit(solution)/shard_map/ppermute | solution.py:574
  54.9 2.9 %collective-permute-start.19 = (f32[184,128]{1,0:T(8,128)S(1)}, f32[184,128]{1,0:T(8,128)S(1)}, u32[]{:S(2)}, u32[]{:S(2)}) collective-permute-start(f32[184,128]{1,0:T(8,128)S(1)} %get-tuple-element.71), channel_id=1, source_target_pairs={{0,16},{8,24},{16,0},{24,8},{1,17},{9,25},{17,1},{25,9},{2,18},{10... | collective-permute-start | bytes 282632 | tf_op jit(solution)/shard_map/ppermute | solution.py:578
  57.8 1.5 %collective-permute-start.20 = (f32[184,128]{1,0:T(8,128)S(1)}, f32[184,128]{1,0:T(8,128)S(1)}, u32[]{:S(2)}, u32[]{:S(2)}) collective-permute-start(f32[184,128]{1,0:T(8,128)S(1)} %get-tuple-element.72), channel_id=1, source_target_pairs={{0,24},{8,16},{16,8},{24,0},{1,25},{9,17},{17,9},{25,1},{2,26},{10... | collective-permute-start | bytes 282632 | tf_op jit(solution)/shard_map/ppermute | solution.py:578
  59.5 3.0 %collective-permute-done.19.refs_2_ = f32[184,128]{1,0:T(8,128)S(1)} collective-permute-done((f32[184,128]{1,0:T(8,128)S(1)}, f32[184,128]{1,0:T(8,128)S(1)}, u32[]{:S(2)}, u32[]{:S(2)}) %collective-permute-start.19) | collective-permute-done | bytes 94240 | tf_op jit(solution)/shard_map/ppermute | solution.py:578
  62.5 1.8 %collective-permute-done.20.refs_3_ = f32[184,128]{1,0:T(8,128)S(1)} collective-permute-done((f32[184,128]{1,0:T(8,128)S(1)}, f32[184,128]{1,0:T(8,128)S(1)}, u32[]{:S(2)}, u32[]{:S(2)}) %collective-permute-start.20) | collective-permute-done | bytes 94240 | tf_op jit(solution)/shard_map/ppermute | solution.py:578
  64.4 1.6 %collective-permute-start.23 = (f32[184,128]{1,0:T(8,128)S(1)}, f32[184,128]{1,0:T(8,128)S(1)}, u32[]{:S(2)}, u32[]{:S(2)}) collective-permute-start(f32[184,128]{1,0:T(8,128)S(1)} %get-tuple-element.73.refs_1_), channel_id=1, source_target_pairs={{0,24},{8,16},{16,8},{24,0},{1,25},{9,17},{17,9},{25,1},{2,26},{10... | collective-permute-start | bytes 282632 | tf_op jit(solution)/shard_map/ppermute | solution.py:578
  66.0 3.8 %collective-permute-start.22 = (f32[184,128]{1,0:T(8,128)S(1)}, f32[184,128]{1,0:T(8,128)S(1)}, u32[]{:S(2)}, u32[]{:S(2)}) collective-permute-start(f32[184,128]{1,0:T(8,128)S(1)} %get-tuple-element.73.refs_1_), channel_id=1, source_target_pairs={{0,16},{8,24},{16,0},{24,8},{1,17},{9,25},{17,1},{25,9},{2,18},{10... | collective-permute-start | bytes 282632 | tf_op jit(solution)/shard_map/ppermute | solution.py:578
  69.8 9.9 %all_to_all.10 = f32[32,1,128]{2,1,0:T(1,128)S(1)} all-to-all(f32[32,1,128]{2,1,0:T(1,128)S(1)} %bitcast.21), channel_id=1, replica_groups=mesh['mem'=4,'lat'=8] {'mem','lat'}, dimensions={0} | all-to-all | bytes 32768 | tf_op jit(solution)/shard_map/all_to_all | solution.py:664
  79.7 1.4 %shard_map.71 = (f32[240,128]{1,0:T(8,128)S(1)}, f32[240,128]{1,0:T(8,128)S(1)}, f32[96,384]{1,0:T(8,128)S(1)}, f32[736,128]{1,0:T(8,128)S(1)}, f32[736,128]{1,0:T(8,128)S(1)}) custom-call(bf16[32,3,24,1280]{3,2,1,0:T(8,128)(2,1)S(1)} %shard_map.59.pert_ref.refs_0_, f32[184,128]{1,0:T(8,128)S(1)} %get-tuple-element.73.refs_1_, ...), custom_call_target="tpu_custom_call" | custom-call | flops 503316480 | bytes 7036940 | tf_op jit(solution)/shard_map/pallas_call | solution.py:546
  83.3 2.1 %collective-permute-start.27 = (f32[240,128]{1,0:T(8,128)S(1)}, f32[240,128]{1,0:T(8,128)S(1)}, u32[]{:S(2)}, u32[]{:S(2)}) collective-permute-start(f32[240,128]{1,0:T(8,128)S(1)} %get-tuple-element.83), channel_id=1, source_target_pairs={{0,7},{1,2},{2,1},{3,4},{4,3},{5,6},{6,5},{7,0},{8,15},{9,10},{10,... | collective-permute-start | bytes 368648 | tf_op jit(solution)/shard_map/ppermute | solution.py:574
  85.4 2.1 %collective-permute-done.25.refs_2_ = f32[240,128]{1,0:T(8,128)S(1)} collective-permute-done((f32[240,128]{1,0:T(8,128)S(1)}, f32[240,128]{1,0:T(8,128)S(1)}, u32[]{:S(2)}, u32[]{:S(2)}) %collective-permute-start.25) | collective-permute-done | bytes 122912 | tf_op jit(solution)/shard_map/ppermute | solution.py:574
  88.0 1.8 %collective-permute-done.27.refs_2_ = f32[240,128]{1,0:T(8,128)S(1)} collective-permute-done((f32[240,128]{1,0:T(8,128)S(1)}, f32[240,128]{1,0:T(8,128)S(1)}, u32[]{:S(2)}, u32[]{:S(2)}) %collective-permute-start.27) | collective-permute-done | bytes 122912 | tf_op jit(solution)/shard_map/ppermute | solution.py:574
  91.3 2.1 %collective-permute-done.31.b_ref = f32[240,128]{1,0:T(8,128)S(1)} collective-permute-done((f32[240,128]{1,0:T(8,128)S(1)}, f32[240,128]{1,0:T(8,128)S(1)}, u32[]{:S(2)}, u32[]{:S(2)}) %collective-permute-start.31) | collective-permute-done | bytes 122912 | tf_op jit(solution)/shard_map/ppermute | solution.py:574
  94.5 1.8 %collective-permute-done.29.b_ref = f32[240,128]{1,0:T(8,128)S(1)} collective-permute-done((f32[240,128]{1,0:T(8,128)S(1)}, f32[240,128]{1,0:T(8,128)S(1)}, u32[]{:S(2)}, u32[]{:S(2)}) %collective-permute-start.29) | collective-permute-done | bytes 122912 | tf_op jit(solution)/shard_map/ppermute | solution.py:574
  98.7 3.3 %collective-permute-start.34 = (f32[184,128]{1,0:T(8,128)S(1)}, f32[184,128]{1,0:T(8,128)S(1)}, u32[]{:S(2)}, u32[]{:S(2)}) collective-permute-start(f32[184,128]{1,0:T(8,128)S(1)} %get-tuple-element.93), channel_id=1, source_target_pairs={{0,24},{8,16},{16,8},{24,0},{1,25},{9,17},{17,9},{25,1},{2,26},{10... | collective-permute-start | bytes 282632 | tf_op jit(solution)/shard_map/ppermute | solution.py:578
  102.2 5.0 %collective-permute-done.33.refs_2_ = f32[184,128]{1,0:T(8,128)S(1)} collective-permute-done((f32[184,128]{1,0:T(8,128)S(1)}, f32[184,128]{1,0:T(8,128)S(1)}, u32[]{:S(2)}, u32[]{:S(2)}) %collective-permute-start.33) | collective-permute-done | bytes 94240 | tf_op jit(solution)/shard_map/ppermute | solution.py:578
  108.0 3.2 %all-to-all-start.1 = ((f32[32,1,128]{2,1,0:T(1,128)}), f32[32,1,128]{2,1,0:T(1,128)S(1)}, u32[]{:S(2)}, u32[]{:S(2)}) async-start(f32[32,1,128]{2,1,0:T(1,128)} %bitcast.7), calls=%async_computation.1 | async-start | bytes 32768 | tf_op jit(solution)/shard_map/all_to_all | solution.py:664
  111.5 6.8 %all-to-all-done.1 = f32[32,1,128]{2,1,0:T(1,128)S(1)} async-done(((f32[32,1,128]{2,1,0:T(1,128)}), f32[32,1,128]{2,1,0:T(1,128)S(1)}, u32[]{:S(2)}, u32[]{:S(2)}) %all-to-all-start.1) | async-done | bytes 16416 | tf_op jit(solution)/shard_map/all_to_all | solution.py:664
  (70 shorter events, 24.2 us)
Async XLA Ops:
  1.8 8.6 %collective-permute-start.3 = (f32[240,128]{1,0:T(8,128)S(1)}, f32[240,128]{1,0:T(8,128)S(1)}, u32[]{:S(2)}, u32[]{:S(2)}) collective-permute-start(f32[240,128]{1,0:T(8,128)S(1)} %get-tuple-element.53), channel_id=1, source_target_pairs={{0,7},{1,2},{2,1},{3,4},{4,3},{5,6},{6,5},{7,0},{8,15},{9,10},{10,... | collective-permute-start | bytes 368648 | tf_op jit(solution)/shard_map/ppermute | solution.py:574
  5.2 5.3 %collective-permute-start.2 = (f32[240,128]{1,0:T(8,128)S(1)}, f32[240,128]{1,0:T(8,128)S(1)}, u32[]{:S(2)}, u32[]{:S(2)}) collective-permute-start(f32[240,128]{1,0:T(8,128)S(1)} %get-tuple-element.53), channel_id=1, source_target_pairs={{0,1},{1,0},{2,3},{3,2},{4,5},{5,4},{6,7},{7,6},{8,9},{9,8},{10,11... | collective-permute-start | bytes 368648 | tf_op jit(solution)/shard_map/ppermute | solution.py:574
  5.2 6.5 %collective-permute-start.1 = (f32[240,128]{1,0:T(8,128)S(1)}, f32[240,128]{1,0:T(8,128)S(1)}, u32[]{:S(2)}, u32[]{:S(2)}) collective-permute-start(f32[240,128]{1,0:T(8,128)S(1)} %get-tuple-element.51), channel_id=1, source_target_pairs={{0,7},{1,2},{2,1},{3,4},{4,3},{5,6},{6,5},{7,0},{8,15},{9,10},{10,... | collective-permute-start | bytes 368648 | tf_op jit(solution)/shard_map/ppermute | solution.py:574
  6.0 5.8 %collective-permute-start = (f32[240,128]{1,0:T(8,128)S(1)}, f32[240,128]{1,0:T(8,128)S(1)}, u32[]{:S(2)}, u32[]{:S(2)}) collective-permute-start(f32[240,128]{1,0:T(8,128)S(1)} %get-tuple-element.51), channel_id=1, source_target_pairs={{0,1},{1,0},{2,3},{3,2},{4,5},{5,4},{6,7},{7,6},{8,9},{9,8},{10,11... | collective-permute-start | bytes 368648 | tf_op jit(solution)/shard_map/ppermute | solution.py:574
  12.9 4.9 %collective-permute-start.4 = (f32[184,128]{1,0:T(8,128)S(1)}, f32[184,128]{1,0:T(8,128)S(1)}, u32[]{:S(2)}, u32[]{:S(2)}) collective-permute-start(f32[184,128]{1,0:T(8,128)S(1)} %get-tuple-element.55), channel_id=1, source_target_pairs={{0,8},{8,0},{16,24},{24,16},{1,9},{9,1},{17,25},{25,17},{2,10},{10... | collective-permute-start | bytes 282632 | tf_op jit(solution)/shard_map/ppermute | solution.py:578
  15.2 9.6 %collective-permute-start.5 = (f32[184,128]{1,0:T(8,128)S(1)}, f32[184,128]{1,0:T(8,128)S(1)}, u32[]{:S(2)}, u32[]{:S(2)}) collective-permute-start(f32[184,128]{1,0:T(8,128)S(1)} %get-tuple-element.56), channel_id=1, source_target_pairs={{0,16},{8,24},{16,0},{24,8},{1,17},{9,25},{17,1},{25,9},{2,18},{10... | collective-permute-start | bytes 282632 | tf_op jit(solution)/shard_map/ppermute | solution.py:578
  17.8 7.0 %collective-permute-start.6 = (f32[184,128]{1,0:T(8,128)S(1)}, f32[184,128]{1,0:T(8,128)S(1)}, u32[]{:S(2)}, u32[]{:S(2)}) collective-permute-start(f32[184,128]{1,0:T(8,128)S(1)} %get-tuple-element.57), channel_id=1, source_target_pairs={{0,24},{8,16},{16,8},{24,0},{1,25},{9,17},{17,9},{25,1},{2,26},{10... | collective-permute-start | bytes 282632 | tf_op jit(solution)/shard_map/ppermute | solution.py:578
  24.9 7.3 %collective-permute-start.9 = (f32[184,128]{1,0:T(8,128)S(1)}, f32[184,128]{1,0:T(8,128)S(1)}, u32[]{:S(2)}, u32[]{:S(2)}) collective-permute-start(f32[184,128]{1,0:T(8,128)S(1)} %shard_map.63.refs_1_), channel_id=1, source_target_pairs={{0,24},{8,16},{16,8},{24,0},{1,25},{9,17},{17,9},{25,1},{2,26},{10... | collective-permute-start | bytes 282632 | tf_op jit(solution)/shard_map/ppermute | solution.py:578
  27.4 7.7 %collective-permute-start.8 = (f32[184,128]{1,0:T(8,128)S(1)}, f32[184,128]{1,0:T(8,128)S(1)}, u32[]{:S(2)}, u32[]{:S(2)}) collective-permute-start(f32[184,128]{1,0:T(8,128)S(1)} %shard_map.63.refs_1_), channel_id=1, source_target_pairs={{0,16},{8,24},{16,0},{24,8},{1,17},{9,25},{17,1},{25,9},{2,18},{10... | collective-permute-start | bytes 282632 | tf_op jit(solution)/shard_map/ppermute | solution.py:578
  27.9 7.2 %collective-permute-start.7 = (f32[184,128]{1,0:T(8,128)S(1)}, f32[184,128]{1,0:T(8,128)S(1)}, u32[]{:S(2)}, u32[]{:S(2)}) collective-permute-start(f32[184,128]{1,0:T(8,128)S(1)} %shard_map.63.refs_1_), channel_id=1, source_target_pairs={{0,8},{8,0},{16,24},{24,16},{1,9},{9,1},{17,25},{25,17},{2,10},{10... | collective-permute-start | bytes 282632 | tf_op jit(solution)/shard_map/ppermute | solution.py:578
  36.5 5.0 %collective-permute-start.14 = (f32[240,128]{1,0:T(8,128)S(1)}, f32[240,128]{1,0:T(8,128)S(1)}, u32[]{:S(2)}, u32[]{:S(2)}) collective-permute-start(f32[240,128]{1,0:T(8,128)S(1)} %get-tuple-element.65), channel_id=1, source_target_pairs={{0,1},{1,0},{2,3},{3,2},{4,5},{5,4},{6,7},{7,6},{8,9},{9,8},{10,11... | collective-permute-start | bytes 368648 | tf_op jit(solution)/shard_map/ppermute | solution.py:574
  36.6 5.6 %collective-permute-start.15 = (f32[240,128]{1,0:T(8,128)S(1)}, f32[240,128]{1,0:T(8,128)S(1)}, u32[]{:S(2)}, u32[]{:S(2)}) collective-permute-start(f32[240,128]{1,0:T(8,128)S(1)} %get-tuple-element.66), channel_id=1, source_target_pairs={{0,7},{1,2},{2,1},{3,4},{4,3},{5,6},{6,5},{7,0},{8,15},{9,10},{10,... | collective-permute-start | bytes 368648 | tf_op jit(solution)/shard_map/ppermute | solution.py:574
  40.0 5.2 %collective-permute-start.10 = (f32[240,128]{1,0:T(8,128)S(1)}, f32[240,128]{1,0:T(8,128)S(1)}, u32[]{:S(2)}, u32[]{:S(2)}) collective-permute-start(f32[240,128]{1,0:T(8,128)S(1)} %get-tuple-element.60), channel_id=1, source_target_pairs={{0,1},{1,0},{2,3},{3,2},{4,5},{5,4},{6,7},{7,6},{8,9},{9,8},{10,11... | collective-permute-start | bytes 368648 | tf_op jit(solution)/shard_map/ppermute | solution.py:574
  41.2 6.0 %collective-permute-start.11 = (f32[240,128]{1,0:T(8,128)S(1)}, f32[240,128]{1,0:T(8,128)S(1)}, u32[]{:S(2)}, u32[]{:S(2)}) collective-permute-start(f32[240,128]{1,0:T(8,128)S(1)} %get-tuple-element.61), channel_id=1, source_target_pairs={{0,7},{1,2},{2,1},{3,4},{4,3},{5,6},{6,5},{7,0},{8,15},{9,10},{10,... | collective-permute-start | bytes 368648 | tf_op jit(solution)/shard_map/ppermute | solution.py:574
  42.4 7.4 %collective-permute-start.17 = (f32[240,128]{1,0:T(8,128)S(1)}, f32[240,128]{1,0:T(8,128)S(1)}, u32[]{:S(2)}, u32[]{:S(2)}) collective-permute-start(f32[240,128]{1,0:T(8,128)S(1)} %get-tuple-element.68.refs_4_), channel_id=1, source_target_pairs={{0,7},{1,2},{2,1},{3,4},{4,3},{5,6},{6,5},{7,0},{8,15},{9,10},{10,... | collective-permute-start | bytes 368648 | tf_op jit(solution)/shard_map/ppermute | solution.py:574
  47.3 6.3 %collective-permute-start.13 = (f32[240,128]{1,0:T(8,128)S(1)}, f32[240,128]{1,0:T(8,128)S(1)}, u32[]{:S(2)}, u32[]{:S(2)}) collective-permute-start(f32[240,128]{1,0:T(8,128)S(1)} %get-tuple-element.63.refs_5_), channel_id=1, source_target_pairs={{0,7},{1,2},{2,1},{3,4},{4,3},{5,6},{6,5},{7,0},{8,15},{9,10},{10,... | collective-permute-start | bytes 368648 | tf_op jit(solution)/shard_map/ppermute | solution.py:574
  48.1 5.5 %collective-permute-start.12 = (f32[240,128]{1,0:T(8,128)S(1)}, f32[240,128]{1,0:T(8,128)S(1)}, u32[]{:S(2)}, u32[]{:S(2)}) collective-permute-start(f32[240,128]{1,0:T(8,128)S(1)} %get-tuple-element.63.refs_5_), channel_id=1, source_target_pairs={{0,1},{1,0},{2,3},{3,2},{4,5},{5,4},{6,7},{7,6},{8,9},{9,8},{10,11... | collective-permute-start | bytes 368648 | tf_op jit(solution)/shard_map/ppermute | solution.py:574
  54.9 7.6 %collective-permute-start.19 = (f32[184,128]{1,0:T(8,128)S(1)}, f32[184,128]{1,0:T(8,128)S(1)}, u32[]{:S(2)}, u32[]{:S(2)}) collective-permute-start(f32[184,128]{1,0:T(8,128)S(1)} %get-tuple-element.71), channel_id=1, source_target_pairs={{0,16},{8,24},{16,0},{24,8},{1,17},{9,25},{17,1},{25,9},{2,18},{10... | collective-permute-start | bytes 282632 | tf_op jit(solution)/shard_map/ppermute | solution.py:578
  57.8 6.5 %collective-permute-start.20 = (f32[184,128]{1,0:T(8,128)S(1)}, f32[184,128]{1,0:T(8,128)S(1)}, u32[]{:S(2)}, u32[]{:S(2)}) collective-permute-start(f32[184,128]{1,0:T(8,128)S(1)} %get-tuple-element.72), channel_id=1, source_target_pairs={{0,24},{8,16},{16,8},{24,0},{1,25},{9,17},{17,9},{25,1},{2,26},{10... | collective-permute-start | bytes 282632 | tf_op jit(solution)/shard_map/ppermute | solution.py:578
  64.4 15.3 %collective-permute-start.23 = (f32[184,128]{1,0:T(8,128)S(1)}, f32[184,128]{1,0:T(8,128)S(1)}, u32[]{:S(2)}, u32[]{:S(2)}) collective-permute-start(f32[184,128]{1,0:T(8,128)S(1)} %get-tuple-element.73.refs_1_), channel_id=1, source_target_pairs={{0,24},{8,16},{16,8},{24,0},{1,25},{9,17},{17,9},{25,1},{2,26},{10... | collective-permute-start | bytes 282632 | tf_op jit(solution)/shard_map/ppermute | solution.py:578
  66.0 13.7 %collective-permute-start.22 = (f32[184,128]{1,0:T(8,128)S(1)}, f32[184,128]{1,0:T(8,128)S(1)}, u32[]{:S(2)}, u32[]{:S(2)}) collective-permute-start(f32[184,128]{1,0:T(8,128)S(1)} %get-tuple-element.73.refs_1_), channel_id=1, source_target_pairs={{0,16},{8,24},{16,0},{24,8},{1,17},{9,25},{17,1},{25,9},{2,18},{10... | collective-permute-start | bytes 282632 | tf_op jit(solution)/shard_map/ppermute | solution.py:578
  69.8 9.9 %collective-permute-start.21 = (f32[184,128]{1,0:T(8,128)S(1)}, f32[184,128]{1,0:T(8,128)S(1)}, u32[]{:S(2)}, u32[]{:S(2)}) collective-permute-start(f32[184,128]{1,0:T(8,128)S(1)} %get-tuple-element.73.refs_1_), channel_id=1, source_target_pairs={{0,8},{8,0},{16,24},{24,16},{1,9},{9,1},{17,25},{25,17},{2,10},{10... | collective-permute-start | bytes 282632 | tf_op jit(solution)/shard_map/ppermute | solution.py:578
  81.3 6.3 %collective-permute-start.25 = (f32[240,128]{1,0:T(8,128)S(1)}, f32[240,128]{1,0:T(8,128)S(1)}, u32[]{:S(2)}, u32[]{:S(2)}) collective-permute-start(f32[240,128]{1,0:T(8,128)S(1)} %get-tuple-element.78), channel_id=1, source_target_pairs={{0,7},{1,2},{2,1},{3,4},{4,3},{5,6},{6,5},{7,0},{8,15},{9,10},{10,... | collective-permute-start | bytes 368648 | tf_op jit(solution)/shard_map/ppermute | solution.py:574
  83.3 4.8 %collective-permute-start.26 = (f32[240,128]{1,0:T(8,128)S(1)}, f32[240,128]{1,0:T(8,128)S(1)}, u32[]{:S(2)}, u32[]{:S(2)}) collective-permute-start(f32[240,128]{1,0:T(8,128)S(1)} %get-tuple-element.82), channel_id=1, source_target_pairs={{0,1},{1,0},{2,3},{3,2},{4,5},{5,4},{6,7},{7,6},{8,9},{9,8},{10,11... | collective-permute-start | bytes 368648 | tf_op jit(solution)/shard_map/ppermute | solution.py:574
  83.3 6.5 %collective-permute-start.27 = (f32[240,128]{1,0:T(8,128)S(1)}, f32[240,128]{1,0:T(8,128)S(1)}, u32[]{:S(2)}, u32[]{:S(2)}) collective-permute-start(f32[240,128]{1,0:T(8,128)S(1)} %get-tuple-element.83), channel_id=1, source_target_pairs={{0,7},{1,2},{2,1},{3,4},{4,3},{5,6},{6,5},{7,0},{8,15},{9,10},{10,... | collective-permute-start | bytes 368648 | tf_op jit(solution)/shard_map/ppermute | solution.py:574
  87.7 5.7 %collective-permute-start.31 = (f32[240,128]{1,0:T(8,128)S(1)}, f32[240,128]{1,0:T(8,128)S(1)}, u32[]{:S(2)}, u32[]{:S(2)}) collective-permute-start(f32[240,128]{1,0:T(8,128)S(1)} %get-tuple-element.89.refs_4_), channel_id=1, source_target_pairs={{0,7},{1,2},{2,1},{3,4},{4,3},{5,6},{6,5},{7,0},{8,15},{9,10},{10,... | collective-permute-start | bytes 368648 | tf_op jit(solution)/shard_map/ppermute | solution.py:574
  88.0 5.4 %collective-permute-start.30 = (f32[240,128]{1,0:T(8,128)S(1)}, f32[240,128]{1,0:T(8,128)S(1)}, u32[]{:S(2)}, u32[]{:S(2)}) collective-permute-start(f32[240,128]{1,0:T(8,128)S(1)} %get-tuple-element.89.refs_4_), channel_id=1, source_target_pairs={{0,1},{1,0},{2,3},{3,2},{4,5},{5,4},{6,7},{7,6},{8,9},{9,8},{10,11... | collective-permute-start | bytes 368648 | tf_op jit(solution)/shard_map/ppermute | solution.py:574
  90.0 6.3 %collective-permute-start.29 = (f32[240,128]{1,0:T(8,128)S(1)}, f32[240,128]{1,0:T(8,128)S(1)}, u32[]{:S(2)}, u32[]{:S(2)}) collective-permute-start(f32[240,128]{1,0:T(8,128)S(1)} %get-tuple-element.88.refs_5_), channel_id=1, source_target_pairs={{0,7},{1,2},{2,1},{3,4},{4,3},{5,6},{6,5},{7,0},{8,15},{9,10},{10,... | collective-permute-start | bytes 368648 | tf_op jit(solution)/shard_map/ppermute | solution.py:574
  91.3 5.0 %collective-permute-start.28 = (f32[240,128]{1,0:T(8,128)S(1)}, f32[240,128]{1,0:T(8,128)S(1)}, u32[]{:S(2)}, u32[]{:S(2)}) collective-permute-start(f32[240,128]{1,0:T(8,128)S(1)} %get-tuple-element.88.refs_5_), channel_id=1, source_target_pairs={{0,1},{1,0},{2,3},{3,2},{4,5},{5,4},{6,7},{7,6},{8,9},{9,8},{10,11... | collective-permute-start | bytes 368648 | tf_op jit(solution)/shard_map/ppermute | solution.py:574
  98.2 9.0 %collective-permute-start.33 = (f32[184,128]{1,0:T(8,128)S(1)}, f32[184,128]{1,0:T(8,128)S(1)}, u32[]{:S(2)}, u32[]{:S(2)}) collective-permute-start(f32[184,128]{1,0:T(8,128)S(1)} %get-tuple-element.92), channel_id=1, source_target_pairs={{0,16},{8,24},{16,0},{24,8},{1,17},{9,25},{17,1},{25,9},{2,18},{10... | collective-permute-start | bytes 282632 | tf_op jit(solution)/shard_map/ppermute | solution.py:578
  98.7 8.5 %collective-permute-start.34 = (f32[184,128]{1,0:T(8,128)S(1)}, f32[184,128]{1,0:T(8,128)S(1)}, u32[]{:S(2)}, u32[]{:S(2)}) collective-permute-start(f32[184,128]{1,0:T(8,128)S(1)} %get-tuple-element.93), channel_id=1, source_target_pairs={{0,24},{8,16},{16,8},{24,0},{1,25},{9,17},{17,9},{25,1},{2,26},{10... | collective-permute-start | bytes 282632 | tf_op jit(solution)/shard_map/ppermute | solution.py:578
  108.0 10.3 %all-to-all-start.1 = ((f32[32,1,128]{2,1,0:T(1,128)}), f32[32,1,128]{2,1,0:T(1,128)S(1)}, u32[]{:S(2)}, u32[]{:S(2)}) async-start(f32[32,1,128]{2,1,0:T(1,128)} %bitcast.7), calls=%async_computation.1 | async-start | bytes 32768 | tf_op jit(solution)/shard_map/all_to_all | solution.py:664
  (8 other events, 71.1 us)

commit v3 on v2

--- a/solution.py
+++ b/solution.py
@@ -42,6 +42,7 @@
     def __init__(self, mesh, perturbations, control):
         self.n_mem = mesh.shape["mem"]
         self.n_lat = mesh.shape["lat"]
+        self.far_first = range(self.n_mem - 1, 0, -1)
         self.members = control.shape[0]
         self.group = self.members // GROUPS
         self.rows = control.shape[1]
@@ -152,26 +153,38 @@
         pack_ref(size, packed_ref, tiles_of(own_ref, size.ext // LANES))
 
 
-def load_kernel(pert_ref, out_ref, sems):
+def load_kernel(pert_ref, out_ref, held_ref, sems):
     count = sems.shape[0]
     part = pert_ref.shape[0] // count
     copies = [
         pltpu.make_async_copy(
-            pert_ref.at[pl.ds(i * part, part)], out_ref.at[pl.ds(i * part, part)], sems.at[i]
+            pert_ref.at[pl.ds(i * part, part)], held_ref.at[pl.ds(i * part, part)], sems.at[i]
         )
         for i in range(count)
     ]
     for copy in copies:
         copy.start()
-    for copy in copies:
+    for i, copy in enumerate(copies):
         copy.wait()
 
-
-def forward_kernel(size, g, shares, own_ref, a_ref, b_ref, pert_ref, *rest):
+        def widen(m, unused):
+            for v in range(pert_ref.shape[1]):
+                out_ref[m, v] = held_ref[m, v].astype(F32)
+            return unused
+
+        lax.fori_loop(i * part, (i + 1) * part, widen, 0)
+
+
+def forward_kernel(size, g, shares, own_ref, b_ref, a_ref, pert_ref, *rest):
     rest = list(rest)
     start_ref = rest.pop(0) if g else None
     last = g == GROUPS - 1
+    extra = shares and g == 0
+    if extra:
+        sources = [rest.pop(0) for i in range(3)]
     outs = [rest.pop(0) for i in range(size.n_mem if last else 1)]
+    if extra:
+        own_share_kernel(size, *sources, rest.pop(0), *rest[-2:])
     ext_ref, coarse_ref, rows_ref = rest[:3]
     acc_ref = rest[3] if last else outs[0]
     members = size.group
@@ -247,7 +260,7 @@
                 for m in range(CHUNK):
                     value = refined[m * fine_rows : (m + 1) * fine_rows, here]
                     for v in range(size.vars):
-                        pert = pert_ref[g * members + step * CHUNK + m, v, :, cut].astype(F32)
+                        pert = pert_ref[g * members + step * CHUNK + m, v, :, cut]
                         totals[v] = totals[v] + pert * value
                 for v in range(size.vars):
                     acc_ref[rows[v], :] = totals[v]
@@ -340,9 +353,9 @@
 def misfit_of(size, parts, before_ref, scal_ref, innov_ref, limit_ref, list_ref, misfit_ref):
     fine_rows = size.fine_rows
     mine = lax.axis_index("mem")
-    for d in range(size.n_mem):
+    for i, d in enumerate((0, *size.far_first)):
         first = pl.multiple_of((mine ^ d) * size.part_rows, 8)
-        list_ref[pl.ds(first, size.part_rows), :] = parts[d][...]
+        list_ref[pl.ds(first, size.part_rows), :] = parts[i][...]
     if before_ref is not None:
         length = step_length(scal_ref)
     for e in range(size.field_tiles):
@@ -397,9 +410,9 @@
             ]
             weighted = []
             for m in range(CHUNK):
-                total = pert_ref[g * members + step * CHUNK + m, 0, :, cut].astype(F32) * mis[0]
+                total = pert_ref[g * members + step * CHUNK + m, 0, :, cut]* mis[0]
                 for v in range(1, size.vars):
-                    total = total + pert_ref[g * members + step * CHUNK + m, v, :, cut].astype(F32) * mis[v]
+                    total = total + pert_ref[g * members + step * CHUNK + m, v, :, cut]* mis[v]
                 weighted.append(total)
             x = jnp.concatenate(weighted, axis=0)
             head = x.astype(BF16)
@@ -473,7 +486,7 @@
 
 def gradient_kernel(size, later, *refs):
     refs = list(refs)
-    own_ref, a_ref, b_ref, weights_ref = refs[:4]
+    own_ref, b_ref, a_ref, weights_ref = refs[:4]
     refs = refs[4:]
     weights = weights_ref[...]
     if later:
@@ -530,26 +543,27 @@
     return pl.BlockSpec(memory_space=pltpu.VMEM)
 
 
-def params():
-    return pltpu.CompilerParams(vmem_limit_bytes=24 * 1024 * 1024)
+def params(limit):
+    return pltpu.CompilerParams(vmem_limit_bytes=limit * 1024 * 1024)
 
 
 def array(*shape):
     return jax.ShapeDtypeStruct(shape, F32)
 
 
-def call(kernel, outs, *args, scratch=(), flops=0, spaces=None):
+def call(kernel, outs, *args, scratch=(), flops=0, spaces=None, moved=None, limit=24):
     spaces = spaces or [
         pltpu.MemorySpace.SMEM if arg.ndim == 1 else pltpu.MemorySpace.VMEM for arg in args
     ]
-    moved = sum(arg.size * arg.dtype.itemsize for arg in args)
+    if moved is None:
+        moved = sum(arg.size * arg.dtype.itemsize for arg in args)
     return pl.pallas_call(
         kernel,
         out_shape=outs,
         in_specs=[pl.BlockSpec(memory_space=space) for space in spaces],
         out_specs=jax.tree.map(lambda unused: whole(), outs),
         scratch_shapes=scratch,
-        compiler_params=params(),
+        compiler_params=params(limit),
         cost_estimate=pl.CostEstimate(flops=flops, bytes_accessed=moved, transcendentals=0),
     )(*args)
 
@@ -560,7 +574,7 @@
     devices = n_mem * n_lat
     pairs = [(i, i ^ 1) for i in range(n_lat)]
     cross = [(i, (i - 1 if i % 2 == 0 else i + 1) % n_lat) for i in range(n_lat)]
-    far_first = sorted(range(1, n_mem), key=lambda d: -d)
+    middle_first = sorted(range(1, n_mem), key=lambda d: (d != n_mem // 2, d))
     groups = range(GROUPS)
     slab = array(size.slab, size.ext)
     packed = array(size.packed, LANES)
@@ -573,14 +587,13 @@
     def swap(to_a, to_b):
         return lax.ppermute(to_a, "lat", pairs), lax.ppermute(to_b, "lat", cross)
 
-    def exchange(parts):
-        moved = {
-            d: lax.ppermute(parts[d], "mem", [(i, i ^ d) for i in range(n_mem)])
-            for d in far_first
-        }
-        return [parts[0]] + [moved[d] for d in range(1, n_mem)]
-
-    def forward(owns, arrived, shares=False):
+    def exchange(parts, order):
+        return [parts[0]] + [
+            lax.ppermute(parts[d], "mem", [(i, i ^ d) for i in range(n_mem)]) for d in order
+        ]
+
+    def forward(owns, arrived, *first_step):
+        shares = len(first_step) > 0
         acc = []
         piece = share if shares else part
         for g in groups:
@@ -594,17 +607,26 @@
                 scratch.append(pltpu.VMEM(field.shape, F32))
                 if shares:
                     scratch.append(pltpu.VMEM((n_mem, *piece.shape), F32))
+            outs = [piece] * n_mem if last else [field]
+            extra = shares and g == 0
+            if extra:
+                outs.append(share)
+                scratch += [pltpu.VMEM(field.shape, F32), pltpu.VMEM((n_mem, *share.shape), F32)]
             acc = call(
                 functools.partial(forward_kernel, size, g, shares),
-                [piece] * n_mem if last else [field],
+                outs,
                 owns[g],
-                *arrived[g],
+                *arrived[g][::-1],
                 resident,
                 *acc,
+                *(first_step if extra else ()),
                 scratch=scratch,
                 flops=map_flops,
             )
-        return exchange(acc)
+            if extra:
+                *acc, own_share = acc
+        acc = exchange(acc, middle_first)
+        return (acc, own_share) if shares else acc
 
     def adjoint(parts, *step):
         later = len(step) > 0
@@ -643,7 +665,7 @@
                 functools.partial(gradient_kernel, size, later),
                 [slab, packed] + ([slab] if later else []),
                 spread[g],
-                *arrived[g],
+                *arrived[g][::-1],
                 weights[g],
                 *([step[0], step[1][g]] if later else []),
             )
@@ -676,32 +698,26 @@
     copies = min(4, members)
     resident = call(
         load_kernel,
-        jax.ShapeDtypeStruct(perturbations.shape, perturbations.dtype),
-        perturbations,
-        scratch=[pltpu.SemaphoreType.DMA((copies,))],
+        pltpu.VMEM(perturbations.shape, F32),
+        pltpu.with_memory_space_constraint(perturbations, pltpu.HBM),
+        scratch=[
+            pltpu.VMEM(perturbations.shape, perturbations.dtype),
+            pltpu.SemaphoreType.DMA((copies,)),
+        ],
         spaces=[pltpu.MemorySpace.HBM],
         flops=2 * map_flops,
     )
     parts = forward(control_own, both(sent))
     field0 = call(functools.partial(total_kernel, n_mem), part, *parts)
-    arrived, spread, before = adjoint(exchange([field0] * n_mem))
+    arrived, spread, before = adjoint(exchange([field0] * n_mem, size.far_first))
     grads0, sent, unused = gradient(arrived, spread, control_own)
     parts = forward(grads0, both(sent))
     image0, scal0 = squares(parts, sent)
-    images = exchange([image0] * n_mem)
+    images = exchange([image0] * n_mem, size.far_first)
     scal0 = everywhere(scal0)
     arrived, spread, image_all = adjoint(images, scal0, before)
     grads1, sent, weights1 = gradient(arrived, spread, control_own, scal0, grads0)
-    own_share = call(
-        functools.partial(own_share_kernel, size),
-        share,
-        before,
-        image_all,
-        scal0,
-        scratch=[pltpu.VMEM(field.shape, F32), pltpu.VMEM((n_mem, *share.shape), F32)],
-        flops=map_flops // 8,
-    )
-    parts = forward(grads1, both(sent), shares=True)
+    parts, own_share = forward(grads1, both(sent), before, image_all, scal0)
     image1, scal1 = squares(parts, sent)
     scal1 = everywhere(scal1)
     weights, result = call(

time: 120 us -> 116 us (0.967)
  blocking collectives: 9.91 us -> 19 us
  starting transfers between devices: 43.4 us -> 37.3 us
  waiting for transfers between devices: 44.6 us -> 40.2 us
  local copies, waits for them, and re-layouts: 3.64 us -> 0.97 us
    all_to_all x1 -> x2, blocking collectives: 9.91 us -> 19 us  [everywhere(): lax.all_to_all(tile.reshape(devices, 1, LANES), ('mem', 'lat'), 0, 0)]
    all_to_all x1 -> x0, waiting for transfers between devices: 6.8 us -> none  [everywhere(): lax.all_to_all(tile.reshape(devices, 1, LANES), ('mem', 'lat'), 0, 0)]
    all_to_all x1 -> x0, starting transfers between devices: 3.19 us -> none  [everywhere(): lax.all_to_all(tile.reshape(devices, 1, LANES), ('mem', 'lat'), 0, 0)]
    unnamed x8 -> x6, local copies, waits for them, and re-layouts: 3.64 us -> 0.97 us
    ppermute x20, waiting for transfers between devices: 14.8 us -> 17.4 us  [swap(): return (lax.ppermute(to_a, 'lat', pairs), lax.ppermute(to_b, 'lat', cross))]
    ppermute x20, starting transfers between devices: 16.6 us -> 14.6 us  [swap(): return (lax.ppermute(to_a, 'lat', pairs), lax.ppermute(to_b, 'lat', cross))]
    pallas_call x21 -> x20, Pallas kernels: 16.8 us -> 17 us  [call(): pl.pallas_call(kernel, out_shape=outs, in_specs=[pl.BlockSpec(memory_spac...]
  transfers between devices with their start and end apart: 36 -> 35, of which waited for: 18 -> 17; matrix products, arithmetic and copies ran while one was open for 0% -> 0% of each run, Pallas kernels for 7% -> 8%
where the time goes in v3:
time: 116 us; the launch traced here: 115 us
  waiting for transfers between devices  40.2 us (35%)
  starting transfers between devices  37.3 us (32%)
  blocking collectives  19 us (16%)
  Pallas kernels  17 us (15%)
    ppermute x15, waiting for transfers between devices, exchange(): lax.ppermute(parts[d], 'mem', [(i, i ^ d) for i in range(n_mem)])  22.8 us
    ppermute x15, starting transfers between devices, exchange(): lax.ppermute(parts[d], 'mem', [(i, i ^ d) for i in range(n_mem)])  22.7 us
    all_to_all x2, blocking collectives, everywhere(): lax.all_to_all(tile.reshape(devices, 1, LANES), ('mem', 'lat'), 0, 0)  19 us
    ppermute x20, waiting for transfers between devices, swap(): return (lax.ppermute(to_a, 'lat', pairs), lax.ppermute(to_b, 'lat', cross))  17.4 us
    pallas_call x20, Pallas kernels, call(): pl.pallas_call(kernel, out_shape=outs, in_specs=[pl.BlockSpec(memory_spac...  17 us
    ppermute x20, starting transfers between devices, swap(): return (lax.ppermute(to_a, 'lat', pairs), lax.ppermute(to_b, 'lat', cross))  14.6 us
  transfers between devices with their start and end apart: 35, of which 17 were waited for; matrix products, arithmetic and copies ran while one was open for 0% of the time, Pallas kernels for 8%

profile of v3, /device:TPU:0, one launch (start us, length us, event | category | flops | bytes accessed | tf_op | source)
XLA Modules:
  0.0 115.4 jit_solution(8246814349403565043)
XLA Ops:
  1.8 3.4 %collective-permute-start.2 = (f32[240,128]{1,0:T(8,128)S(1)}, f32[240,128]{1,0:T(8,128)S(1)}, u32[]{:S(2)}, u32[]{:S(2)}) collective-permute-start(f32[240,128]{1,0:T(8,128)S(1)} %get-tuple-element.55), channel_id=1, source_target_pairs={{0,7},{1,2},{2,1},{3,4},{4,3},{5,6},{6,5},{7,0},{8,15},{9,10},{10,... | collective-permute-start | bytes 368648 | tf_op jit(solution)/shard_map/ppermute | solution.py:588
  6.6 2.9 %shard_map.59.pert_ref.refs_0_ = f32[32,3,24,1280]{3,2,1,0:T(8,128)S(1)} custom-call(bf16[32,3,24,1280]{3,2,1,0:T(8,128)(2,1)} %pert_ref.1), custom_call_target="tpu_custom_call" | custom-call | flops 1006632960 | bytes 5898240 | tf_op jit(solution)/shard_map/pallas_call | solution.py:560
  12.9 3.3 %collective-permute-start.4 = (f32[184,128]{1,0:T(8,128)S(1)}, f32[184,128]{1,0:T(8,128)S(1)}, u32[]{:S(2)}, u32[]{:S(2)}) collective-permute-start(f32[184,128]{1,0:T(8,128)S(1)} %get-tuple-element.57), channel_id=1, source_target_pairs={{0,16},{8,24},{16,0},{24,8},{1,17},{9,25},{17,1},{25,9},{2,18},{10... | collective-permute-start | bytes 282632 | tf_op jit(solution)/shard_map/ppermute | solution.py:592
  16.2 1.6 %collective-permute-start.5 = (f32[184,128]{1,0:T(8,128)S(1)}, f32[184,128]{1,0:T(8,128)S(1)}, u32[]{:S(2)}, u32[]{:S(2)}) collective-permute-start(f32[184,128]{1,0:T(8,128)S(1)} %get-tuple-element.58), channel_id=1, source_target_pairs={{0,8},{8,0},{16,24},{24,16},{1,9},{9,1},{17,25},{25,17},{2,10},{10... | collective-permute-start | bytes 282632 | tf_op jit(solution)/shard_map/ppermute | solution.py:592
  17.7 3.1 %collective-permute-done.4.refs_1_ = f32[184,128]{1,0:T(8,128)S(1)} collective-permute-done((f32[184,128]{1,0:T(8,128)S(1)}, f32[184,128]{1,0:T(8,128)S(1)}, u32[]{:S(2)}, u32[]{:S(2)}) %collective-permute-start.4) | collective-permute-done | bytes 94240 | tf_op jit(solution)/shard_map/ppermute | solution.py:592
  20.9 3.3 %collective-permute-done.6.refs_3_ = f32[184,128]{1,0:T(8,128)S(1)} collective-permute-done((f32[184,128]{1,0:T(8,128)S(1)}, f32[184,128]{1,0:T(8,128)S(1)}, u32[]{:S(2)}, u32[]{:S(2)}) %collective-permute-start.6) | collective-permute-done | bytes 94240 | tf_op jit(solution)/shard_map/ppermute | solution.py:592
  24.2 2.5 %collective-permute-start.7 = (f32[184,128]{1,0:T(8,128)S(1)}, f32[184,128]{1,0:T(8,128)S(1)}, u32[]{:S(2)}, u32[]{:S(2)}) collective-permute-start(f32[184,128]{1,0:T(8,128)S(1)} %shard_map.63.refs_1_), channel_id=1, source_target_pairs={{0,24},{8,16},{16,8},{24,0},{1,25},{9,17},{17,9},{25,1},{2,26},{10... | collective-permute-start | bytes 282632 | tf_op jit(solution)/shard_map/ppermute | solution.py:592
  27.2 1.5 %collective-permute-start.9 = (f32[184,128]{1,0:T(8,128)S(1)}, f32[184,128]{1,0:T(8,128)S(1)}, u32[]{:S(2)}, u32[]{:S(2)}) collective-permute-start(f32[184,128]{1,0:T(8,128)S(1)} %shard_map.63.refs_1_), channel_id=1, source_target_pairs={{0,8},{8,0},{16,24},{24,16},{1,9},{9,1},{17,25},{25,17},{2,10},{10... | collective-permute-start | bytes 282632 | tf_op jit(solution)/shard_map/ppermute | solution.py:592
  28.7 3.0 %collective-permute-done.7.refs_2_ = f32[184,128]{1,0:T(8,128)S(1)} collective-permute-done((f32[184,128]{1,0:T(8,128)S(1)}, f32[184,128]{1,0:T(8,128)S(1)}, u32[]{:S(2)}, u32[]{:S(2)}) %collective-permute-start.7) | collective-permute-done | bytes 94240 | tf_op jit(solution)/shard_map/ppermute | solution.py:592
  31.7 3.1 %collective-permute-done.8.refs_3_ = f32[184,128]{1,0:T(8,128)S(1)} collective-permute-done((f32[184,128]{1,0:T(8,128)S(1)}, f32[184,128]{1,0:T(8,128)S(1)}, u32[]{:S(2)}, u32[]{:S(2)}) %collective-permute-start.8) | collective-permute-done | bytes 94240 | tf_op jit(solution)/shard_map/ppermute | solution.py:592
  34.9 1.3 %shard_map.64 = (f32[240,128]{1,0:T(8,128)S(1)}, f32[240,128]{1,0:T(8,128)S(1)}, f32[96,384]{1,0:T(8,128)S(1)}, f32[736,128]{1,0:T(8,128)S(1)}, f32[736,128]{1,0:T(8,128)S(1)}) custom-call(f32[32,3,24,1280]{3,2,1,0:T(8,128)S(1)} %shard_map.59.pert_ref.refs_0_, f32[184,128]{1,0:T(8,128)S(1)} %shard_map.63.refs_1_, ...), custom_call_target="tpu_custom_call" | custom-call | flops 503316480 | bytes 12541964 | tf_op jit(solution)/shard_map/pallas_call | solution.py:560
  37.6 1.5 %collective-permute-start.15 = (f32[240,128]{1,0:T(8,128)S(1)}, f32[240,128]{1,0:T(8,128)S(1)}, u32[]{:S(2)}, u32[]{:S(2)}) collective-permute-start(f32[240,128]{1,0:T(8,128)S(1)} %get-tuple-element.68), channel_id=1, source_target_pairs={{0,1},{1,0},{2,3},{3,2},{4,5},{5,4},{6,7},{7,6},{8,9},{9,8},{10,11... | collective-permute-start | bytes 368648 | tf_op jit(solution)/shard_map/ppermute | solution.py:588
  41.2 1.5 %collective-permute-done.14.refs_1_ = f32[240,128]{1,0:T(8,128)S(1)} collective-permute-done((f32[240,128]{1,0:T(8,128)S(1)}, f32[240,128]{1,0:T(8,128)S(1)}, u32[]{:S(2)}, u32[]{:S(2)}) %collective-permute-start.14) | collective-permute-done | bytes 122912 | tf_op jit(solution)/shard_map/ppermute | solution.py:588
  44.1 2.5 %collective-permute-done.10.refs_1_ = f32[240,128]{1,0:T(8,128)S(1)} collective-permute-done((f32[240,128]{1,0:T(8,128)S(1)}, f32[240,128]{1,0:T(8,128)S(1)}, u32[]{:S(2)}, u32[]{:S(2)}) %collective-permute-start.10) | collective-permute-done | bytes 122912 | tf_op jit(solution)/shard_map/ppermute | solution.py:588
  47.1 2.4 %collective-permute-done.16.b_ref = f32[240,128]{1,0:T(8,128)S(1)} collective-permute-done((f32[240,128]{1,0:T(8,128)S(1)}, f32[240,128]{1,0:T(8,128)S(1)}, u32[]{:S(2)}, u32[]{:S(2)}) %collective-permute-start.16) | collective-permute-done | bytes 122912 | tf_op jit(solution)/shard_map/ppermute | solution.py:588
  50.5 2.6 %collective-permute-done.12.b_ref = f32[240,128]{1,0:T(8,128)S(1)} collective-permute-done((f32[240,128]{1,0:T(8,128)S(1)}, f32[240,128]{1,0:T(8,128)S(1)}, u32[]{:S(2)}, u32[]{:S(2)}) %collective-permute-start.12) | collective-permute-done | bytes 122912 | tf_op jit(solution)/shard_map/ppermute | solution.py:588
  54.3 2.9 %collective-permute-start.19 = (f32[184,128]{1,0:T(8,128)S(1)}, f32[184,128]{1,0:T(8,128)S(1)}, u32[]{:S(2)}, u32[]{:S(2)}) collective-permute-start(f32[184,128]{1,0:T(8,128)S(1)} %get-tuple-element.73), channel_id=1, source_target_pairs={{0,8},{8,0},{16,24},{24,16},{1,9},{9,1},{17,25},{25,17},{2,10},{10... | collective-permute-start | bytes 282632 | tf_op jit(solution)/shard_map/ppermute | solution.py:592
  57.2 1.5 %collective-permute-start.20 = (f32[184,128]{1,0:T(8,128)S(1)}, f32[184,128]{1,0:T(8,128)S(1)}, u32[]{:S(2)}, u32[]{:S(2)}) collective-permute-start(f32[184,128]{1,0:T(8,128)S(1)} %get-tuple-element.74), channel_id=1, source_target_pairs={{0,24},{8,16},{16,8},{24,0},{1,25},{9,17},{17,9},{25,1},{2,26},{10... | collective-permute-start | bytes 282632 | tf_op jit(solution)/shard_map/ppermute | solution.py:592
  58.7 3.1 %collective-permute-done.18.refs_1_ = f32[184,128]{1,0:T(8,128)S(1)} collective-permute-done((f32[184,128]{1,0:T(8,128)S(1)}, f32[184,128]{1,0:T(8,128)S(1)}, u32[]{:S(2)}, u32[]{:S(2)}) %collective-permute-start.18) | collective-permute-done | bytes 94240 | tf_op jit(solution)/shard_map/ppermute | solution.py:592
  61.8 1.9 %collective-permute-done.20.refs_3_ = f32[184,128]{1,0:T(8,128)S(1)} collective-permute-done((f32[184,128]{1,0:T(8,128)S(1)}, f32[184,128]{1,0:T(8,128)S(1)}, u32[]{:S(2)}, u32[]{:S(2)}) %collective-permute-start.20) | collective-permute-done | bytes 94240 | tf_op jit(solution)/shard_map/ppermute | solution.py:592
  63.8 1.6 %collective-permute-start.21 = (f32[184,128]{1,0:T(8,128)S(1)}, f32[184,128]{1,0:T(8,128)S(1)}, u32[]{:S(2)}, u32[]{:S(2)}) collective-permute-start(f32[184,128]{1,0:T(8,128)S(1)} %get-tuple-element.75.refs_1_), channel_id=1, source_target_pairs={{0,24},{8,16},{16,8},{24,0},{1,25},{9,17},{17,9},{25,1},{2,26},{10... | collective-permute-start | bytes 282632 | tf_op jit(solution)/shard_map/ppermute | solution.py:592
  66.0 2.3 %collective-permute-start.23 = (f32[184,128]{1,0:T(8,128)S(1)}, f32[184,128]{1,0:T(8,128)S(1)}, u32[]{:S(2)}, u32[]{:S(2)}) collective-permute-start(f32[184,128]{1,0:T(8,128)S(1)} %get-tuple-element.75.refs_1_), channel_id=1, source_target_pairs={{0,8},{8,0},{16,24},{24,16},{1,9},{9,1},{17,25},{25,17},{2,10},{10... | collective-permute-start | bytes 282632 | tf_op jit(solution)/shard_map/ppermute | solution.py:592
  68.3 9.0 %all_to_all.10 = f32[32,1,128]{2,1,0:T(1,128)S(1)} all-to-all(f32[32,1,128]{2,1,0:T(1,128)S(1)} %bitcast.21), channel_id=1, replica_groups=mesh['mem'=4,'lat'=8] {'mem','lat'}, dimensions={0} | all-to-all | bytes 32768 | tf_op jit(solution)/shard_map/all_to_all | solution.py:686
  77.4 1.4 %shard_map.71 = (f32[240,128]{1,0:T(8,128)S(1)}, f32[240,128]{1,0:T(8,128)S(1)}, f32[96,384]{1,0:T(8,128)S(1)}, f32[736,128]{1,0:T(8,128)S(1)}, f32[736,128]{1,0:T(8,128)S(1)}) custom-call(f32[32,3,24,1280]{3,2,1,0:T(8,128)S(1)} %shard_map.59.pert_ref.refs_0_, f32[184,128]{1,0:T(8,128)S(1)} %get-tuple-element.75.refs_1_, ...), custom_call_target="tpu_custom_call" | custom-call | flops 503316480 | bytes 12935180 | tf_op jit(solution)/shard_map/pallas_call | solution.py:560
  80.7 2.1 %collective-permute-start.26 = (f32[240,128]{1,0:T(8,128)S(1)}, f32[240,128]{1,0:T(8,128)S(1)}, u32[]{:S(2)}, u32[]{:S(2)}) collective-permute-start(f32[240,128]{1,0:T(8,128)S(1)} %get-tuple-element.84), channel_id=1, source_target_pairs={{0,7},{1,2},{2,1},{3,4},{4,3},{5,6},{6,5},{7,0},{8,15},{9,10},{10,... | collective-permute-start | bytes 368648 | tf_op jit(solution)/shard_map/ppermute | solution.py:588
  82.7 1.7 %collective-permute-done.24.refs_1_ = f32[240,128]{1,0:T(8,128)S(1)} collective-permute-done((f32[240,128]{1,0:T(8,128)S(1)}, f32[240,128]{1,0:T(8,128)S(1)}, u32[]{:S(2)}, u32[]{:S(2)}) %collective-permute-start.24) | collective-permute-done | bytes 122912 | tf_op jit(solution)/shard_map/ppermute | solution.py:588
  85.5 1.7 %collective-permute-done.26.refs_1_ = f32[240,128]{1,0:T(8,128)S(1)} collective-permute-done((f32[240,128]{1,0:T(8,128)S(1)}, f32[240,128]{1,0:T(8,128)S(1)}, u32[]{:S(2)}, u32[]{:S(2)}) %collective-permute-start.26) | collective-permute-done | bytes 122912 | tf_op jit(solution)/shard_map/ppermute | solution.py:588
  88.4 1.5 %collective-permute-done.28.b_ref = f32[240,128]{1,0:T(8,128)S(1)} collective-permute-done((f32[240,128]{1,0:T(8,128)S(1)}, f32[240,128]{1,0:T(8,128)S(1)}, u32[]{:S(2)}, u32[]{:S(2)}) %collective-permute-start.28) | collective-permute-done | bytes 122912 | tf_op jit(solution)/shard_map/ppermute | solution.py:588
  91.0 2.4 %collective-permute-done.30.b_ref = f32[240,128]{1,0:T(8,128)S(1)} collective-permute-done((f32[240,128]{1,0:T(8,128)S(1)}, f32[240,128]{1,0:T(8,128)S(1)}, u32[]{:S(2)}, u32[]{:S(2)}) %collective-permute-start.30) | collective-permute-done | bytes 122912 | tf_op jit(solution)/shard_map/ppermute | solution.py:588
  96.0 3.1 %collective-permute-start.34 = (f32[184,128]{1,0:T(8,128)S(1)}, f32[184,128]{1,0:T(8,128)S(1)}, u32[]{:S(2)}, u32[]{:S(2)}) collective-permute-start(f32[184,128]{1,0:T(8,128)S(1)} %get-tuple-element.97), channel_id=1, source_target_pairs={{0,24},{8,16},{16,8},{24,0},{1,25},{9,17},{17,9},{25,1},{2,26},{10... | collective-permute-start | bytes 282632 | tf_op jit(solution)/shard_map/ppermute | solution.py:592
  99.0 5.2 %collective-permute-done.32.refs_1_ = f32[184,128]{1,0:T(8,128)S(1)} collective-permute-done((f32[184,128]{1,0:T(8,128)S(1)}, f32[184,128]{1,0:T(8,128)S(1)}, u32[]{:S(2)}, u32[]{:S(2)}) %collective-permute-start.32) | collective-permute-done | bytes 94240 | tf_op jit(solution)/shard_map/ppermute | solution.py:592
  104.4 10.0 %all_to_all.11 = f32[32,1,128]{2,1,0:T(1,128)S(1)} all-to-all(f32[32,1,128]{2,1,0:T(1,128)S(1)} %bitcast.22), channel_id=1, replica_groups=mesh['mem'=4,'lat'=8] {'mem','lat'}, dimensions={0} | all-to-all | bytes 32768 | tf_op jit(solution)/shard_map/all_to_all | solution.py:686
  (66 shorter events, 23.8 us)
Async XLA Ops:
  1.8 7.7 %collective-permute-start.2 = (f32[240,128]{1,0:T(8,128)S(1)}, f32[240,128]{1,0:T(8,128)S(1)}, u32[]{:S(2)}, u32[]{:S(2)}) collective-permute-start(f32[240,128]{1,0:T(8,128)S(1)} %get-tuple-element.55), channel_id=1, source_target_pairs={{0,7},{1,2},{2,1},{3,4},{4,3},{5,6},{6,5},{7,0},{8,15},{9,10},{10,... | collective-permute-start | bytes 368648 | tf_op jit(solution)/shard_map/ppermute | solution.py:588
  5.2 6.5 %collective-permute-start = (f32[240,128]{1,0:T(8,128)S(1)}, f32[240,128]{1,0:T(8,128)S(1)}, u32[]{:S(2)}, u32[]{:S(2)}) collective-permute-start(f32[240,128]{1,0:T(8,128)S(1)} %get-tuple-element.53), channel_id=1, source_target_pairs={{0,7},{1,2},{2,1},{3,4},{4,3},{5,6},{6,5},{7,0},{8,15},{9,10},{10,... | collective-permute-start | bytes 368648 | tf_op jit(solution)/shard_map/ppermute | solution.py:588
  6.0 5.8 %collective-permute-start.1 = (f32[240,128]{1,0:T(8,128)S(1)}, f32[240,128]{1,0:T(8,128)S(1)}, u32[]{:S(2)}, u32[]{:S(2)}) collective-permute-start(f32[240,128]{1,0:T(8,128)S(1)} %get-tuple-element.53), channel_id=1, source_target_pairs={{0,1},{1,0},{2,3},{3,2},{4,5},{5,4},{6,7},{7,6},{8,9},{9,8},{10,11... | collective-permute-start | bytes 368648 | tf_op jit(solution)/shard_map/ppermute | solution.py:588
  12.9 8.0 %collective-permute-start.4 = (f32[184,128]{1,0:T(8,128)S(1)}, f32[184,128]{1,0:T(8,128)S(1)}, u32[]{:S(2)}, u32[]{:S(2)}) collective-permute-start(f32[184,128]{1,0:T(8,128)S(1)} %get-tuple-element.57), channel_id=1, source_target_pairs={{0,16},{8,24},{16,0},{24,8},{1,17},{9,25},{17,1},{25,9},{2,18},{10... | collective-permute-start | bytes 282632 | tf_op jit(solution)/shard_map/ppermute | solution.py:592
  16.2 4.8 %collective-permute-start.5 = (f32[184,128]{1,0:T(8,128)S(1)}, f32[184,128]{1,0:T(8,128)S(1)}, u32[]{:S(2)}, u32[]{:S(2)}) collective-permute-start(f32[184,128]{1,0:T(8,128)S(1)} %get-tuple-element.58), channel_id=1, source_target_pairs={{0,8},{8,0},{16,24},{24,16},{1,9},{9,1},{17,25},{25,17},{2,10},{10... | collective-permute-start | bytes 282632 | tf_op jit(solution)/shard_map/ppermute | solution.py:592
  17.7 6.5 %collective-permute-start.6 = (f32[184,128]{1,0:T(8,128)S(1)}, f32[184,128]{1,0:T(8,128)S(1)}, u32[]{:S(2)}, u32[]{:S(2)}) collective-permute-start(f32[184,128]{1,0:T(8,128)S(1)} %get-tuple-element.59), channel_id=1, source_target_pairs={{0,24},{8,16},{16,8},{24,0},{1,25},{9,17},{17,9},{25,1},{2,26},{10... | collective-permute-start | bytes 282632 | tf_op jit(solution)/shard_map/ppermute | solution.py:592
  24.2 7.5 %collective-permute-start.7 = (f32[184,128]{1,0:T(8,128)S(1)}, f32[184,128]{1,0:T(8,128)S(1)}, u32[]{:S(2)}, u32[]{:S(2)}) collective-permute-start(f32[184,128]{1,0:T(8,128)S(1)} %shard_map.63.refs_1_), channel_id=1, source_target_pairs={{0,24},{8,16},{16,8},{24,0},{1,25},{9,17},{17,9},{25,1},{2,26},{10... | collective-permute-start | bytes 282632 | tf_op jit(solution)/shard_map/ppermute | solution.py:592
  26.8 8.1 %collective-permute-start.8 = (f32[184,128]{1,0:T(8,128)S(1)}, f32[184,128]{1,0:T(8,128)S(1)}, u32[]{:S(2)}, u32[]{:S(2)}) collective-permute-start(f32[184,128]{1,0:T(8,128)S(1)} %shard_map.63.refs_1_), channel_id=1, source_target_pairs={{0,16},{8,24},{16,0},{24,8},{1,17},{9,25},{17,1},{25,9},{2,18},{10... | collective-permute-start | bytes 282632 | tf_op jit(solution)/shard_map/ppermute | solution.py:592
  27.2 7.7 %collective-permute-start.9 = (f32[184,128]{1,0:T(8,128)S(1)}, f32[184,128]{1,0:T(8,128)S(1)}, u32[]{:S(2)}, u32[]{:S(2)}) collective-permute-start(f32[184,128]{1,0:T(8,128)S(1)} %shard_map.63.refs_1_), channel_id=1, source_target_pairs={{0,8},{8,0},{16,24},{24,16},{1,9},{9,1},{17,25},{25,17},{2,10},{10... | collective-permute-start | bytes 282632 | tf_op jit(solution)/shard_map/ppermute | solution.py:592
  36.2 6.4 %collective-permute-start.14 = (f32[240,128]{1,0:T(8,128)S(1)}, f32[240,128]{1,0:T(8,128)S(1)}, u32[]{:S(2)}, u32[]{:S(2)}) collective-permute-start(f32[240,128]{1,0:T(8,128)S(1)} %get-tuple-element.67), channel_id=1, source_target_pairs={{0,7},{1,2},{2,1},{3,4},{4,3},{5,6},{6,5},{7,0},{8,15},{9,10},{10,... | collective-permute-start | bytes 368648 | tf_op jit(solution)/shard_map/ppermute | solution.py:588
  37.6 5.1 %collective-permute-start.15 = (f32[240,128]{1,0:T(8,128)S(1)}, f32[240,128]{1,0:T(8,128)S(1)}, u32[]{:S(2)}, u32[]{:S(2)}) collective-permute-start(f32[240,128]{1,0:T(8,128)S(1)} %get-tuple-element.68), channel_id=1, source_target_pairs={{0,1},{1,0},{2,3},{3,2},{4,5},{5,4},{6,7},{7,6},{8,9},{9,8},{10,11... | collective-permute-start | bytes 368648 | tf_op jit(solution)/shard_map/ppermute | solution.py:588
  40.3 6.3 %collective-permute-start.10 = (f32[240,128]{1,0:T(8,128)S(1)}, f32[240,128]{1,0:T(8,128)S(1)}, u32[]{:S(2)}, u32[]{:S(2)}) collective-permute-start(f32[240,128]{1,0:T(8,128)S(1)} %get-tuple-element.62), channel_id=1, source_target_pairs={{0,7},{1,2},{2,1},{3,4},{4,3},{5,6},{6,5},{7,0},{8,15},{9,10},{10,... | collective-permute-start | bytes 368648 | tf_op jit(solution)/shard_map/ppermute | solution.py:588
  40.4 6.3 %collective-permute-start.11 = (f32[240,128]{1,0:T(8,128)S(1)}, f32[240,128]{1,0:T(8,128)S(1)}, u32[]{:S(2)}, u32[]{:S(2)}) collective-permute-start(f32[240,128]{1,0:T(8,128)S(1)} %get-tuple-element.63), channel_id=1, source_target_pairs={{0,1},{1,0},{2,3},{3,2},{4,5},{5,4},{6,7},{7,6},{8,9},{9,8},{10,11... | collective-permute-start | bytes 368648 | tf_op jit(solution)/shard_map/ppermute | solution.py:588
  42.8 6.6 %collective-permute-start.16 = (f32[240,128]{1,0:T(8,128)S(1)}, f32[240,128]{1,0:T(8,128)S(1)}, u32[]{:S(2)}, u32[]{:S(2)}) collective-permute-start(f32[240,128]{1,0:T(8,128)S(1)} %get-tuple-element.70.refs_4_), channel_id=1, source_target_pairs={{0,7},{1,2},{2,1},{3,4},{4,3},{5,6},{6,5},{7,0},{8,15},{9,10},{10,... | collective-permute-start | bytes 368648 | tf_op jit(solution)/shard_map/ppermute | solution.py:588
  43.6 5.9 %collective-permute-start.17 = (f32[240,128]{1,0:T(8,128)S(1)}, f32[240,128]{1,0:T(8,128)S(1)}, u32[]{:S(2)}, u32[]{:S(2)}) collective-permute-start(f32[240,128]{1,0:T(8,128)S(1)} %get-tuple-element.70.refs_4_), channel_id=1, source_target_pairs={{0,1},{1,0},{2,3},{3,2},{4,5},{5,4},{6,7},{7,6},{8,9},{9,8},{10,11... | collective-permute-start | bytes 368648 | tf_op jit(solution)/shard_map/ppermute | solution.py:588
  46.8 6.3 %collective-permute-start.12 = (f32[240,128]{1,0:T(8,128)S(1)}, f32[240,128]{1,0:T(8,128)S(1)}, u32[]{:S(2)}, u32[]{:S(2)}) collective-permute-start(f32[240,128]{1,0:T(8,128)S(1)} %get-tuple-element.65.refs_5_), channel_id=1, source_target_pairs={{0,7},{1,2},{2,1},{3,4},{4,3},{5,6},{6,5},{7,0},{8,15},{9,10},{10,... | collective-permute-start | bytes 368648 | tf_op jit(solution)/shard_map/ppermute | solution.py:588
  47.1 6.1 %collective-permute-start.13 = (f32[240,128]{1,0:T(8,128)S(1)}, f32[240,128]{1,0:T(8,128)S(1)}, u32[]{:S(2)}, u32[]{:S(2)}) collective-permute-start(f32[240,128]{1,0:T(8,128)S(1)} %get-tuple-element.65.refs_5_), channel_id=1, source_target_pairs={{0,1},{1,0},{2,3},{3,2},{4,5},{5,4},{6,7},{7,6},{8,9},{9,8},{10,11... | collective-permute-start | bytes 368648 | tf_op jit(solution)/shard_map/ppermute | solution.py:588
  54.2 7.5 %collective-permute-start.18 = (f32[184,128]{1,0:T(8,128)S(1)}, f32[184,128]{1,0:T(8,128)S(1)}, u32[]{:S(2)}, u32[]{:S(2)}) collective-permute-start(f32[184,128]{1,0:T(8,128)S(1)} %get-tuple-element.72), channel_id=1, source_target_pairs={{0,16},{8,24},{16,0},{24,8},{1,17},{9,25},{17,1},{25,9},{2,18},{10... | collective-permute-start | bytes 282632 | tf_op jit(solution)/shard_map/ppermute | solution.py:592
  54.3 7.5 %collective-permute-start.19 = (f32[184,128]{1,0:T(8,128)S(1)}, f32[184,128]{1,0:T(8,128)S(1)}, u32[]{:S(2)}, u32[]{:S(2)}) collective-permute-start(f32[184,128]{1,0:T(8,128)S(1)} %get-tuple-element.73), channel_id=1, source_target_pairs={{0,8},{8,0},{16,24},{24,16},{1,9},{9,1},{17,25},{25,17},{2,10},{10... | collective-permute-start | bytes 282632 | tf_op jit(solution)/shard_map/ppermute | solution.py:592
  57.2 6.5 %collective-permute-start.20 = (f32[184,128]{1,0:T(8,128)S(1)}, f32[184,128]{1,0:T(8,128)S(1)}, u32[]{:S(2)}, u32[]{:S(2)}) collective-permute-start(f32[184,128]{1,0:T(8,128)S(1)} %get-tuple-element.74), channel_id=1, source_target_pairs={{0,24},{8,16},{16,8},{24,0},{1,25},{9,17},{17,9},{25,1},{2,26},{10... | collective-permute-start | bytes 282632 | tf_op jit(solution)/shard_map/ppermute | solution.py:592
  63.8 13.5 %collective-permute-start.21 = (f32[184,128]{1,0:T(8,128)S(1)}, f32[184,128]{1,0:T(8,128)S(1)}, u32[]{:S(2)}, u32[]{:S(2)}) collective-permute-start(f32[184,128]{1,0:T(8,128)S(1)} %get-tuple-element.75.refs_1_), channel_id=1, source_target_pairs={{0,24},{8,16},{16,8},{24,0},{1,25},{9,17},{17,9},{25,1},{2,26},{10... | collective-permute-start | bytes 282632 | tf_op jit(solution)/shard_map/ppermute | solution.py:592
  65.4 12.0 %collective-permute-start.22 = (f32[184,128]{1,0:T(8,128)S(1)}, f32[184,128]{1,0:T(8,128)S(1)}, u32[]{:S(2)}, u32[]{:S(2)}) collective-permute-start(f32[184,128]{1,0:T(8,128)S(1)} %get-tuple-element.75.refs_1_), channel_id=1, source_target_pairs={{0,16},{8,24},{16,0},{24,8},{1,17},{9,25},{17,1},{25,9},{2,18},{10... | collective-permute-start | bytes 282632 | tf_op jit(solution)/shard_map/ppermute | solution.py:592
  66.0 11.3 %collective-permute-start.23 = (f32[184,128]{1,0:T(8,128)S(1)}, f32[184,128]{1,0:T(8,128)S(1)}, u32[]{:S(2)}, u32[]{:S(2)}) collective-permute-start(f32[184,128]{1,0:T(8,128)S(1)} %get-tuple-element.75.refs_1_), channel_id=1, source_target_pairs={{0,8},{8,0},{16,24},{24,16},{1,9},{9,1},{17,25},{25,17},{2,10},{10... | collective-permute-start | bytes 282632 | tf_op jit(solution)/shard_map/ppermute | solution.py:592
  78.7 5.7 %collective-permute-start.24 = (f32[240,128]{1,0:T(8,128)S(1)}, f32[240,128]{1,0:T(8,128)S(1)}, u32[]{:S(2)}, u32[]{:S(2)}) collective-permute-start(f32[240,128]{1,0:T(8,128)S(1)} %get-tuple-element.79), channel_id=1, source_target_pairs={{0,7},{1,2},{2,1},{3,4},{4,3},{5,6},{6,5},{7,0},{8,15},{9,10},{10,... | collective-permute-start | bytes 368648 | tf_op jit(solution)/shard_map/ppermute | solution.py:588
  78.8 5.6 %collective-permute-start.25 = (f32[240,128]{1,0:T(8,128)S(1)}, f32[240,128]{1,0:T(8,128)S(1)}, u32[]{:S(2)}, u32[]{:S(2)}) collective-permute-start(f32[240,128]{1,0:T(8,128)S(1)} %get-tuple-element.80), channel_id=1, source_target_pairs={{0,1},{1,0},{2,3},{3,2},{4,5},{5,4},{6,7},{7,6},{8,9},{9,8},{10,11... | collective-permute-start | bytes 368648 | tf_op jit(solution)/shard_map/ppermute | solution.py:588
  80.7 6.5 %collective-permute-start.26 = (f32[240,128]{1,0:T(8,128)S(1)}, f32[240,128]{1,0:T(8,128)S(1)}, u32[]{:S(2)}, u32[]{:S(2)}) collective-permute-start(f32[240,128]{1,0:T(8,128)S(1)} %get-tuple-element.84), channel_id=1, source_target_pairs={{0,7},{1,2},{2,1},{3,4},{4,3},{5,6},{6,5},{7,0},{8,15},{9,10},{10,... | collective-permute-start | bytes 368648 | tf_op jit(solution)/shard_map/ppermute | solution.py:588
  84.6 5.3 %collective-permute-start.28 = (f32[240,128]{1,0:T(8,128)S(1)}, f32[240,128]{1,0:T(8,128)S(1)}, u32[]{:S(2)}, u32[]{:S(2)}) collective-permute-start(f32[240,128]{1,0:T(8,128)S(1)} %get-tuple-element.89.refs_4_), channel_id=1, source_target_pairs={{0,7},{1,2},{2,1},{3,4},{4,3},{5,6},{6,5},{7,0},{8,15},{9,10},{10,... | collective-permute-start | bytes 368648 | tf_op jit(solution)/shard_map/ppermute | solution.py:588
  87.4 6.0 %collective-permute-start.30 = (f32[240,128]{1,0:T(8,128)S(1)}, f32[240,128]{1,0:T(8,128)S(1)}, u32[]{:S(2)}, u32[]{:S(2)}) collective-permute-start(f32[240,128]{1,0:T(8,128)S(1)} %get-tuple-element.92.refs_5_), channel_id=1, source_target_pairs={{0,7},{1,2},{2,1},{3,4},{4,3},{5,6},{6,5},{7,0},{8,15},{9,10},{10,... | collective-permute-start | bytes 368648 | tf_op jit(solution)/shard_map/ppermute | solution.py:588
  88.4 5.0 %collective-permute-start.31 = (f32[240,128]{1,0:T(8,128)S(1)}, f32[240,128]{1,0:T(8,128)S(1)}, u32[]{:S(2)}, u32[]{:S(2)}) collective-permute-start(f32[240,128]{1,0:T(8,128)S(1)} %get-tuple-element.92.refs_5_), channel_id=1, source_target_pairs={{0,1},{1,0},{2,3},{3,2},{4,5},{5,4},{6,7},{7,6},{8,9},{9,8},{10,11... | collective-permute-start | bytes 368648 | tf_op jit(solution)/shard_map/ppermute | solution.py:588
  94.6 9.6 %collective-permute-start.32 = (f32[184,128]{1,0:T(8,128)S(1)}, f32[184,128]{1,0:T(8,128)S(1)}, u32[]{:S(2)}, u32[]{:S(2)}) collective-permute-start(f32[184,128]{1,0:T(8,128)S(1)} %get-tuple-element.95), channel_id=1, source_target_pairs={{0,16},{8,24},{16,0},{24,8},{1,17},{9,25},{17,1},{25,9},{2,18},{10... | collective-permute-start | bytes 282632 | tf_op jit(solution)/shard_map/ppermute | solution.py:592
  95.2 9.0 %collective-permute-start.33 = (f32[184,128]{1,0:T(8,128)S(1)}, f32[184,128]{1,0:T(8,128)S(1)}, u32[]{:S(2)}, u32[]{:S(2)}) collective-permute-start(f32[184,128]{1,0:T(8,128)S(1)} %get-tuple-element.96), channel_id=1, source_target_pairs={{0,8},{8,0},{16,24},{24,16},{1,9},{9,1},{17,25},{25,17},{2,10},{10... | collective-permute-start | bytes 282632 | tf_op jit(solution)/shard_map/ppermute | solution.py:592
  96.0 8.3 %collective-permute-start.34 = (f32[184,128]{1,0:T(8,128)S(1)}, f32[184,128]{1,0:T(8,128)S(1)}, u32[]{:S(2)}, u32[]{:S(2)}) collective-permute-start(f32[184,128]{1,0:T(8,128)S(1)} %get-tuple-element.97), channel_id=1, source_target_pairs={{0,24},{8,16},{16,8},{24,0},{1,25},{9,17},{17,9},{25,1},{2,26},{10... | collective-permute-start | bytes 282632 | tf_op jit(solution)/shard_map/ppermute | solution.py:592
  (6 other events, 64.8 us)

commit v4 on v3

--- a/solution.py
+++ b/solution.py
@@ -15,7 +15,6 @@
 WIN = 64
 MARGIN = 32
 FINE = RATIO * WIN
-CHUNK = 16
 GROUPS = 2
 F32 = jnp.float32
 BF16 = jnp.bfloat16
@@ -29,10 +28,11 @@
     return (1.0 - abs(distance) / REACH) / 2 if abs(distance) <= HALF else 0.0
 
 
-def window_table(fine_axis):
-    shape = (FINE, LANES) if fine_axis == 0 else (LANES, FINE)
+def window_table(fine_axis, width=LANES):
+    shape = (FINE, width) if fine_axis == 0 else (width, FINE)
     fine = lax.broadcasted_iota(jnp.int32, shape, fine_axis).astype(F32)
-    coarse = lax.broadcasted_iota(jnp.int32, shape, 1 - fine_axis).astype(F32) - MARGIN
+    coarse = lax.broadcasted_iota(jnp.int32, shape, 1 - fine_axis).astype(F32)
+    coarse = coarse - (MARGIN + (width - LANES) // 2)
     distance = fine + 0.5 - RATIO * coarse - RATIO / 2
     table = jnp.maximum(0.0, 1.0 - jnp.abs(distance) / RATIO).astype(BF16)
     return jnp.concatenate([table, table], axis=0)
@@ -51,6 +51,7 @@
         self.fine_rows = perturbations.shape[2]
         self.fine_cols = perturbations.shape[3]
         assert self.rows == REACH and self.cols % LANES == WIN
+        assert self.members % (8 * GROUPS) == 0 and self.n_lat % 2 == 0
         assert self.fine_rows == RATIO * self.rows and self.fine_cols == RATIO * self.cols
         self.windows = self.cols // WIN
         self.ext = self.cols + 2 * MARGIN
@@ -238,39 +239,32 @@
                     total = term if total is None else total + term
             rows_ref[t, pl.ds(i, members, stride=fine_rows), :] = total
     table = window_table(1)
-    block = CHUNK * fine_rows
-
-    def chunk(step, unused):
-        first = pl.multiple_of(step * block, 8)
-        for t in range(size.windows):
-            x = rows_ref[t, pl.ds(first, block), :]
-            head = x.astype(BF16)
-            tail = (x - head.astype(F32)).astype(BF16)
-            refined = jnp.dot(
-                jnp.concatenate([head, tail], axis=1), table, preferred_element_type=F32
-            )
-            for e in range(t * FINE // LANES, (t + 1) * FINE // LANES):
-                cut = slice(e * LANES, (e + 1) * LANES)
-                here = slice(e * LANES - t * FINE, (e + 1) * LANES - t * FINE)
-                rows = [
-                    pl.ds(e * size.field_rows + v * fine_rows, fine_rows)
-                    for v in range(size.vars)
-                ]
-                totals = [acc_ref[at, :] for at in rows]
-                for m in range(CHUNK):
-                    value = refined[m * fine_rows : (m + 1) * fine_rows, here]
-                    for v in range(size.vars):
-                        pert = pert_ref[g * members + step * CHUNK + m, v, :, cut]
-                        totals[v] = totals[v] + pert * value
-                for v in range(size.vars):
-                    acc_ref[rows[v], :] = totals[v]
-        return unused
-
     if g:
         acc_ref[...] = start_ref[...]
     else:
         acc_ref[...] = jnp.zeros_like(acc_ref)
-    lax.fori_loop(0, members // CHUNK, chunk, 0)
+    for t in range(size.windows):
+        x = rows_ref[t]
+        head = x.astype(BF16)
+        tail = (x - head.astype(F32)).astype(BF16)
+        refined = jnp.dot(
+            jnp.concatenate([head, tail], axis=1), table, preferred_element_type=F32
+        )
+        for e in range(t * FINE // LANES, (t + 1) * FINE // LANES):
+            cut = slice(e * LANES, (e + 1) * LANES)
+            here = slice(e * LANES - t * FINE, (e + 1) * LANES - t * FINE)
+            rows = [
+                pl.ds(e * size.field_rows + v * fine_rows, fine_rows)
+                for v in range(size.vars)
+            ]
+            totals = [acc_ref[at, :] for at in rows]
+            for m in range(members):
+                value = refined[m * fine_rows : (m + 1) * fine_rows, here]
+                for v in range(size.vars):
+                    pert = pert_ref[g * members + m, v, :, cut]
+                    totals[v] = totals[v] + pert * value
+            for v in range(size.vars):
+                acc_ref[rows[v], :] = totals[v]
     if not last:
         return
     mine = lax.axis_index("mem")
@@ -383,56 +377,53 @@
     if g == 0:
         misfit_ref = refs.pop(0)
         list_ref = refs.pop(0)
-    cols_ref, coarse_ref, spread_ref = refs[:3]
+    cols_ref, coarse_ref, spread_ref, held_ref = refs[:4]
     members = size.group
     n_tiles = size.ext // LANES
     fine_rows = size.fine_rows
     if g == 0:
         misfit_of(size, parts, before_ref, scal_ref, innov_ref, limit_ref, list_ref, misfit_ref)
-    table = window_table(0)
-    block = CHUNK * fine_rows
-
-    def chunk(step, unused):
-        first = pl.multiple_of(step * block, 8)
-        tops = [None] * n_tiles
-        for t in range(size.windows):
-            cut = slice(t * FINE, (t + 1) * FINE)
-            tiles = range(t * FINE // LANES, (t + 1) * FINE // LANES)
-            mis = [
-                jnp.concatenate(
-                    [
-                        misfit_ref[pl.ds(e * size.field_rows + v * fine_rows, fine_rows), :]
-                        for e in tiles
-                    ],
-                    axis=1,
-                )
-                for v in range(size.vars)
-            ]
-            weighted = []
-            for m in range(CHUNK):
-                total = pert_ref[g * members + step * CHUNK + m, 0, :, cut]* mis[0]
-                for v in range(1, size.vars):
-                    total = total + pert_ref[g * members + step * CHUNK + m, v, :, cut]* mis[v]
-                weighted.append(total)
-            x = jnp.concatenate(weighted, axis=0)
-            head = x.astype(BF16)
-            tail = (x - head.astype(F32)).astype(BF16)
-            columns = jnp.dot(
-                jnp.concatenate([head, tail], axis=1), table, preferred_element_type=F32
+    tables = [window_table(0), window_table(0, 2 * LANES)]
+
+    def weighted(t):
+        cut = slice(t * FINE, (t + 1) * FINE)
+        tiles = range(t * FINE // LANES, (t + 1) * FINE // LANES)
+        mis = [
+            jnp.concatenate(
+                [
+                    misfit_ref[pl.ds(e * size.field_rows + v * fine_rows, fine_rows), :]
+                    for e in tiles
+                ],
+                axis=1,
             )
-            e = t // 2
-            if t % 2 == 0:
-                tops[e] = columns if tops[e] is None else tops[e] + columns
-            else:
-                turned = half_turn(columns)
-                at = lane(turned.shape)
-                tops[e] = tops[e] + jnp.where(at >= WIN, turned, 0.0)
-                tops[e + 1] = jnp.where(at < WIN, turned, 0.0)
-        for e in range(n_tiles):
-            cols_ref[e, pl.ds(first, block), :] = tops[e]
-        return unused
-
-    lax.fori_loop(0, members // CHUNK, chunk, 0)
+            for v in range(size.vars)
+        ]
+        rows = []
+        for m in range(members):
+            total = pert_ref[g * members + m, 0, :, cut] * mis[0]
+            for v in range(1, size.vars):
+                total = total + pert_ref[g * members + m, v, :, cut] * mis[v]
+            rows.append(total)
+        x = jnp.concatenate(rows, axis=0)
+        head = x.astype(BF16)
+        tail = (x - head.astype(F32)).astype(BF16)
+        held_ref[t, :, :FINE] = head
+        held_ref[t, :, FINE:] = tail
+
+    def place_columns(t):
+        columns = jnp.dot(held_ref[t], tables[t % 2], preferred_element_type=F32)
+        e = t // 2
+        if t % 2 == 0:
+            cols_ref[e] = cols_ref[e] + columns if t else columns
+        else:
+            cols_ref[e] = cols_ref[e] + columns[:, :LANES]
+            cols_ref[e + 1] = columns[:, LANES:]
+
+    weighted(0)
+    for t in range(size.windows):
+        if t + 1 < size.windows:
+            weighted(t + 1)
+        place_columns(t)
     odd, low, high = place()
     for e in range(n_tiles):
         cut = slice(e * LANES, (e + 1) * LANES)
@@ -592,7 +583,7 @@
             lax.ppermute(parts[d], "mem", [(i, i ^ d) for i in range(n_mem)]) for d in order
         ]
 
-    def forward(owns, arrived, *first_step):
+    def forward(order, owns, arrived, *first_step):
         shares = len(first_step) > 0
         acc = []
         piece = share if shares else part
@@ -625,7 +616,7 @@
             )
             if extra:
                 *acc, own_share = acc
-        acc = exchange(acc, middle_first)
+        acc = exchange(acc, order)
         return (acc, own_share) if shares else acc
 
     def adjoint(parts, *step):
@@ -636,6 +627,7 @@
                 pltpu.VMEM((size.ext // LANES, size.group * size.fine_rows, LANES), F32),
                 pltpu.VMEM(((size.rows + 2) * size.group, size.ext), F32),
                 pltpu.VMEM((3 * size.slab, size.ext), F32),
+                pltpu.VMEM((size.windows, size.group * size.fine_rows, 2 * FINE), BF16),
             ]
             outs = [packed, packed, slab]
             args = [misfit]
@@ -707,17 +699,17 @@
         spaces=[pltpu.MemorySpace.HBM],
         flops=2 * map_flops,
     )
-    parts = forward(control_own, both(sent))
+    parts = forward(size.far_first, control_own, both(sent))
     field0 = call(functools.partial(total_kernel, n_mem), part, *parts)
     arrived, spread, before = adjoint(exchange([field0] * n_mem, size.far_first))
     grads0, sent, unused = gradient(arrived, spread, control_own)
-    parts = forward(grads0, both(sent))
+    parts = forward(middle_first, grads0, both(sent))
     image0, scal0 = squares(parts, sent)
     images = exchange([image0] * n_mem, size.far_first)
     scal0 = everywhere(scal0)
     arrived, spread, image_all = adjoint(images, scal0, before)
     grads1, sent, weights1 = gradient(arrived, spread, control_own, scal0, grads0)
-    parts, own_share = forward(grads1, both(sent), before, image_all, scal0)
+    parts, own_share = forward(middle_first, grads1, both(sent), before, image_all, scal0)
     image1, scal1 = squares(parts, sent)
     scal1 = everywhere(scal1)
     weights, result = call(

time: 116 us -> 115 us (level)
  waiting for transfers between devices: 40.2 us -> 38.6 us
    ppermute x20, waiting for transfers between devices: 17.4 us -> 15.5 us  [swap(): return (lax.ppermute(to_a, 'lat', pairs), lax.ppermute(to_b, 'lat', cross))]
  transfers between devices with their start and end apart: 35 -> 35, of which waited for: 17 -> 16; matrix products, arithmetic and copies ran while one was open for 0% -> 0% of each run, Pallas kernels for 8% -> 8%
where the time goes in v4:
time: 115 us
  waiting for transfers between devices  38.6 us (34%)
  starting transfers between devices  38.1 us (33%)
  blocking collectives  19.2 us (17%)
  Pallas kernels  16.9 us (15%)
    ppermute x15, waiting for transfers between devices, exchange(): lax.ppermute(parts[d], 'mem', [(i, i ^ d) for i in range(n_mem)])  23.1 us
    ppermute x15, starting transfers between devices, exchange(): lax.ppermute(parts[d], 'mem', [(i, i ^ d) for i in range(n_mem)])  22.8 us
    all_to_all x2, blocking collectives, everywhere(): lax.all_to_all(tile.reshape(devices, 1, LANES), ('mem', 'lat'), 0, 0)  19.2 us
    pallas_call x20, Pallas kernels, call(): pl.pallas_call(kernel, out_shape=outs, in_specs=[pl.BlockSpec(memory_spac...  16.9 us
    ppermute x20, waiting for transfers between devices, swap(): return (lax.ppermute(to_a, 'lat', pairs), lax.ppermute(to_b, 'lat', cross))  15.5 us
    ppermute x20, starting transfers between devices, swap(): return (lax.ppermute(to_a, 'lat', pairs), lax.ppermute(to_b, 'lat', cross))  15.3 us
  transfers between devices with their start and end apart: 35, of which 16 were waited for; matrix products, arithmetic and copies ran while one was open for 0% of the time, Pallas kernels for 8%

profile of v4, /device:TPU:0, one launch (start us, length us, event | category | flops | bytes accessed | tf_op | source)
XLA Modules:
  0.0 114.6 jit_solution(10030293462279851361)
XLA Ops:
  1.8 3.4 %collective-permute-start.2 = (f32[240,128]{1,0:T(8,128)S(1)}, f32[240,128]{1,0:T(8,128)S(1)}, u32[]{:S(2)}, u32[]{:S(2)}) collective-permute-start(f32[240,128]{1,0:T(8,128)S(1)} %get-tuple-element.55), channel_id=1, source_target_pairs={{0,7},{1,2},{2,1},{3,4},{4,3},{5,6},{6,5},{7,0},{8,15},{9,10},{10,... | collective-permute-start | bytes 368648 | tf_op jit(solution)/shard_map/ppermute | solution.py:579
  6.6 2.9 %shard_map.59.pert_ref.refs_0_ = f32[32,3,24,1280]{3,2,1,0:T(8,128)S(1)} custom-call(bf16[32,3,24,1280]{3,2,1,0:T(8,128)(2,1)} %pert_ref.1), custom_call_target="tpu_custom_call" | custom-call | flops 1006632960 | bytes 5898240 | tf_op jit(solution)/shard_map/pallas_call | solution.py:551
  12.9 4.3 %collective-permute-start.4 = (f32[184,128]{1,0:T(8,128)S(1)}, f32[184,128]{1,0:T(8,128)S(1)}, u32[]{:S(2)}, u32[]{:S(2)}) collective-permute-start(f32[184,128]{1,0:T(8,128)S(1)} %get-tuple-element.57), channel_id=1, source_target_pairs={{0,24},{8,16},{16,8},{24,0},{1,25},{9,17},{17,9},{25,1},{2,26},{10... | collective-permute-start | bytes 282632 | tf_op jit(solution)/shard_map/ppermute | solution.py:583
  17.8 3.0 %collective-permute-done.4.refs_1_ = f32[184,128]{1,0:T(8,128)S(1)} collective-permute-done((f32[184,128]{1,0:T(8,128)S(1)}, f32[184,128]{1,0:T(8,128)S(1)}, u32[]{:S(2)}, u32[]{:S(2)}) %collective-permute-start.4) | collective-permute-done | bytes 94240 | tf_op jit(solution)/shard_map/ppermute | solution.py:583
  20.8 3.8 %collective-permute-done.5.refs_2_ = f32[184,128]{1,0:T(8,128)S(1)} collective-permute-done((f32[184,128]{1,0:T(8,128)S(1)}, f32[184,128]{1,0:T(8,128)S(1)}, u32[]{:S(2)}, u32[]{:S(2)}) %collective-permute-start.5) | collective-permute-done | bytes 94240 | tf_op jit(solution)/shard_map/ppermute | solution.py:583
  24.6 2.7 %collective-permute-start.7 = (f32[184,128]{1,0:T(8,128)S(1)}, f32[184,128]{1,0:T(8,128)S(1)}, u32[]{:S(2)}, u32[]{:S(2)}) collective-permute-start(f32[184,128]{1,0:T(8,128)S(1)} %shard_map.63.refs_1_), channel_id=1, source_target_pairs={{0,24},{8,16},{16,8},{24,0},{1,25},{9,17},{17,9},{25,1},{2,26},{10... | collective-permute-start | bytes 282632 | tf_op jit(solution)/shard_map/ppermute | solution.py:583
  27.3 1.8 %collective-permute-start.9 = (f32[184,128]{1,0:T(8,128)S(1)}, f32[184,128]{1,0:T(8,128)S(1)}, u32[]{:S(2)}, u32[]{:S(2)}) collective-permute-start(f32[184,128]{1,0:T(8,128)S(1)} %shard_map.63.refs_1_), channel_id=1, source_target_pairs={{0,8},{8,0},{16,24},{24,16},{1,9},{9,1},{17,25},{25,17},{2,10},{10... | collective-permute-start | bytes 282632 | tf_op jit(solution)/shard_map/ppermute | solution.py:583
  29.1 3.1 %collective-permute-done.7.refs_2_ = f32[184,128]{1,0:T(8,128)S(1)} collective-permute-done((f32[184,128]{1,0:T(8,128)S(1)}, f32[184,128]{1,0:T(8,128)S(1)}, u32[]{:S(2)}, u32[]{:S(2)}) %collective-permute-start.7) | collective-permute-done | bytes 94240 | tf_op jit(solution)/shard_map/ppermute | solution.py:583
  32.1 3.0 %collective-permute-done.8.refs_3_ = f32[184,128]{1,0:T(8,128)S(1)} collective-permute-done((f32[184,128]{1,0:T(8,128)S(1)}, f32[184,128]{1,0:T(8,128)S(1)}, u32[]{:S(2)}, u32[]{:S(2)}) %collective-permute-start.8) | collective-permute-done | bytes 94240 | tf_op jit(solution)/shard_map/ppermute | solution.py:583
  35.1 1.4 %shard_map.64 = (f32[240,128]{1,0:T(8,128)S(1)}, f32[240,128]{1,0:T(8,128)S(1)}, f32[96,384]{1,0:T(8,128)S(1)}, f32[736,128]{1,0:T(8,128)S(1)}, f32[736,128]{1,0:T(8,128)S(1)}) custom-call(f32[32,3,24,1280]{3,2,1,0:T(8,128)S(1)} %shard_map.59.pert_ref.refs_0_, f32[184,128]{1,0:T(8,128)S(1)} %shard_map.63.refs_1_, ...), custom_call_target="tpu_custom_call" | custom-call | flops 503316480 | bytes 12541964 | tf_op jit(solution)/shard_map/pallas_call | solution.py:551
  38.1 1.2 %shard_map.65 = (f32[240,128]{1,0:T(8,128)S(1)}, f32[240,128]{1,0:T(8,128)S(1)}, f32[96,384]{1,0:T(8,128)S(1)}) custom-call(f32[32,3,24,1280]{3,2,1,0:T(8,128)S(1)} %shard_map.59.pert_ref.refs_0_, f32[736,128]{1,0:T(8,128)S(1)} %get-tuple-element.60.refs_1_), custom_call_target="tpu_custom_call" | custom-call | flops 503316480 | bytes 12173312 | tf_op jit(solution)/shard_map/pallas_call | solution.py:551
  41.2 1.7 %collective-permute-done.14.refs_1_ = f32[240,128]{1,0:T(8,128)S(1)} collective-permute-done((f32[240,128]{1,0:T(8,128)S(1)}, f32[240,128]{1,0:T(8,128)S(1)}, u32[]{:S(2)}, u32[]{:S(2)}) %collective-permute-start.14) | collective-permute-done | bytes 122912 | tf_op jit(solution)/shard_map/ppermute | solution.py:579
  44.2 1.6 %collective-permute-done.10.refs_1_ = f32[240,128]{1,0:T(8,128)S(1)} collective-permute-done((f32[240,128]{1,0:T(8,128)S(1)}, f32[240,128]{1,0:T(8,128)S(1)}, u32[]{:S(2)}, u32[]{:S(2)}) %collective-permute-start.10) | collective-permute-done | bytes 122912 | tf_op jit(solution)/shard_map/ppermute | solution.py:579
  45.9 1.2 %collective-permute-start.12 = (f32[240,128]{1,0:T(8,128)S(1)}, f32[240,128]{1,0:T(8,128)S(1)}, u32[]{:S(2)}, u32[]{:S(2)}) collective-permute-start(f32[240,128]{1,0:T(8,128)S(1)} %get-tuple-element.65.refs_5_), channel_id=1, source_target_pairs={{0,7},{1,2},{2,1},{3,4},{4,3},{5,6},{6,5},{7,0},{8,15},{9,10},{10,... | collective-permute-start | bytes 368648 | tf_op jit(solution)/shard_map/ppermute | solution.py:579
  47.2 1.8 %collective-permute-done.16.b_ref = f32[240,128]{1,0:T(8,128)S(1)} collective-permute-done((f32[240,128]{1,0:T(8,128)S(1)}, f32[240,128]{1,0:T(8,128)S(1)}, u32[]{:S(2)}, u32[]{:S(2)}) %collective-permute-start.16) | collective-permute-done | bytes 122912 | tf_op jit(solution)/shard_map/ppermute | solution.py:579
  50.1 2.0 %collective-permute-done.12.b_ref = f32[240,128]{1,0:T(8,128)S(1)} collective-permute-done((f32[240,128]{1,0:T(8,128)S(1)}, f32[240,128]{1,0:T(8,128)S(1)}, u32[]{:S(2)}, u32[]{:S(2)}) %collective-permute-start.12) | collective-permute-done | bytes 122912 | tf_op jit(solution)/shard_map/ppermute | solution.py:579
  53.3 2.9 %collective-permute-start.19 = (f32[184,128]{1,0:T(8,128)S(1)}, f32[184,128]{1,0:T(8,128)S(1)}, u32[]{:S(2)}, u32[]{:S(2)}) collective-permute-start(f32[184,128]{1,0:T(8,128)S(1)} %get-tuple-element.73), channel_id=1, source_target_pairs={{0,8},{8,0},{16,24},{24,16},{1,9},{9,1},{17,25},{25,17},{2,10},{10... | collective-permute-start | bytes 282632 | tf_op jit(solution)/shard_map/ppermute | solution.py:583
  56.2 1.4 %collective-permute-start.20 = (f32[184,128]{1,0:T(8,128)S(1)}, f32[184,128]{1,0:T(8,128)S(1)}, u32[]{:S(2)}, u32[]{:S(2)}) collective-permute-start(f32[184,128]{1,0:T(8,128)S(1)} %get-tuple-element.74), channel_id=1, source_target_pairs={{0,24},{8,16},{16,8},{24,0},{1,25},{9,17},{17,9},{25,1},{2,26},{10... | collective-permute-start | bytes 282632 | tf_op jit(solution)/shard_map/ppermute | solution.py:583
  57.7 3.3 %collective-permute-done.18.refs_1_ = f32[184,128]{1,0:T(8,128)S(1)} collective-permute-done((f32[184,128]{1,0:T(8,128)S(1)}, f32[184,128]{1,0:T(8,128)S(1)}, u32[]{:S(2)}, u32[]{:S(2)}) %collective-permute-start.18) | collective-permute-done | bytes 94240 | tf_op jit(solution)/shard_map/ppermute | solution.py:583
  61.0 1.7 %collective-permute-done.20.refs_3_ = f32[184,128]{1,0:T(8,128)S(1)} collective-permute-done((f32[184,128]{1,0:T(8,128)S(1)}, f32[184,128]{1,0:T(8,128)S(1)}, u32[]{:S(2)}, u32[]{:S(2)}) %collective-permute-start.20) | collective-permute-done | bytes 94240 | tf_op jit(solution)/shard_map/ppermute | solution.py:583
  62.9 1.5 %collective-permute-start.21 = (f32[184,128]{1,0:T(8,128)S(1)}, f32[184,128]{1,0:T(8,128)S(1)}, u32[]{:S(2)}, u32[]{:S(2)}) collective-permute-start(f32[184,128]{1,0:T(8,128)S(1)} %get-tuple-element.75.refs_1_), channel_id=1, source_target_pairs={{0,24},{8,16},{16,8},{24,0},{1,25},{9,17},{17,9},{25,1},{2,26},{10... | collective-permute-start | bytes 282632 | tf_op jit(solution)/shard_map/ppermute | solution.py:583
  65.3 2.1 %collective-permute-start.23 = (f32[184,128]{1,0:T(8,128)S(1)}, f32[184,128]{1,0:T(8,128)S(1)}, u32[]{:S(2)}, u32[]{:S(2)}) collective-permute-start(f32[184,128]{1,0:T(8,128)S(1)} %get-tuple-element.75.refs_1_), channel_id=1, source_target_pairs={{0,8},{8,0},{16,24},{24,16},{1,9},{9,1},{17,25},{25,17},{2,10},{10... | collective-permute-start | bytes 282632 | tf_op jit(solution)/shard_map/ppermute | solution.py:583
  67.3 9.3 %all_to_all.10 = f32[32,1,128]{2,1,0:T(1,128)S(1)} all-to-all(f32[32,1,128]{2,1,0:T(1,128)S(1)} %bitcast.21), channel_id=1, replica_groups=mesh['mem'=4,'lat'=8] {'mem','lat'}, dimensions={0} | all-to-all | bytes 32768 | tf_op jit(solution)/shard_map/all_to_all | solution.py:678
  76.6 1.3 %shard_map.71 = (f32[240,128]{1,0:T(8,128)S(1)}, f32[240,128]{1,0:T(8,128)S(1)}, f32[96,384]{1,0:T(8,128)S(1)}, f32[736,128]{1,0:T(8,128)S(1)}, f32[736,128]{1,0:T(8,128)S(1)}) custom-call(f32[32,3,24,1280]{3,2,1,0:T(8,128)S(1)} %shard_map.59.pert_ref.refs_0_, f32[184,128]{1,0:T(8,128)S(1)} %get-tuple-element.75.refs_1_, ...), custom_call_target="tpu_custom_call" | custom-call | flops 503316480 | bytes 12935180 | tf_op jit(solution)/shard_map/pallas_call | solution.py:551
  79.9 2.1 %collective-permute-start.26 = (f32[240,128]{1,0:T(8,128)S(1)}, f32[240,128]{1,0:T(8,128)S(1)}, u32[]{:S(2)}, u32[]{:S(2)}) collective-permute-start(f32[240,128]{1,0:T(8,128)S(1)} %get-tuple-element.84), channel_id=1, source_target_pairs={{0,7},{1,2},{2,1},{3,4},{4,3},{5,6},{6,5},{7,0},{8,15},{9,10},{10,... | collective-permute-start | bytes 368648 | tf_op jit(solution)/shard_map/ppermute | solution.py:579
  81.9 1.7 %collective-permute-done.24.refs_1_ = f32[240,128]{1,0:T(8,128)S(1)} collective-permute-done((f32[240,128]{1,0:T(8,128)S(1)}, f32[240,128]{1,0:T(8,128)S(1)}, u32[]{:S(2)}, u32[]{:S(2)}) %collective-permute-start.24) | collective-permute-done | bytes 122912 | tf_op jit(solution)/shard_map/ppermute | solution.py:579
  84.8 1.6 %collective-permute-done.26.refs_1_ = f32[240,128]{1,0:T(8,128)S(1)} collective-permute-done((f32[240,128]{1,0:T(8,128)S(1)}, f32[240,128]{1,0:T(8,128)S(1)}, u32[]{:S(2)}, u32[]{:S(2)}) %collective-permute-start.26) | collective-permute-done | bytes 122912 | tf_op jit(solution)/shard_map/ppermute | solution.py:579
  87.6 1.5 %collective-permute-done.28.b_ref = f32[240,128]{1,0:T(8,128)S(1)} collective-permute-done((f32[240,128]{1,0:T(8,128)S(1)}, f32[240,128]{1,0:T(8,128)S(1)}, u32[]{:S(2)}, u32[]{:S(2)}) %collective-permute-start.28) | collective-permute-done | bytes 122912 | tf_op jit(solution)/shard_map/ppermute | solution.py:579
  90.2 2.4 %collective-permute-done.30.b_ref = f32[240,128]{1,0:T(8,128)S(1)} collective-permute-done((f32[240,128]{1,0:T(8,128)S(1)}, f32[240,128]{1,0:T(8,128)S(1)}, u32[]{:S(2)}, u32[]{:S(2)}) %collective-permute-start.30) | collective-permute-done | bytes 122912 | tf_op jit(solution)/shard_map/ppermute | solution.py:579
  95.5 2.7 %collective-permute-start.34 = (f32[184,128]{1,0:T(8,128)S(1)}, f32[184,128]{1,0:T(8,128)S(1)}, u32[]{:S(2)}, u32[]{:S(2)}) collective-permute-start(f32[184,128]{1,0:T(8,128)S(1)} %get-tuple-element.97), channel_id=1, source_target_pairs={{0,24},{8,16},{16,8},{24,0},{1,25},{9,17},{17,9},{25,1},{2,26},{10... | collective-permute-start | bytes 282632 | tf_op jit(solution)/shard_map/ppermute | solution.py:583
  98.2 5.2 %collective-permute-done.32.refs_1_ = f32[184,128]{1,0:T(8,128)S(1)} collective-permute-done((f32[184,128]{1,0:T(8,128)S(1)}, f32[184,128]{1,0:T(8,128)S(1)}, u32[]{:S(2)}, u32[]{:S(2)}) %collective-permute-start.32) | collective-permute-done | bytes 94240 | tf_op jit(solution)/shard_map/ppermute | solution.py:583
  103.6 10.0 %all_to_all.11 = f32[32,1,128]{2,1,0:T(1,128)S(1)} all-to-all(f32[32,1,128]{2,1,0:T(1,128)S(1)} %bitcast.22), channel_id=1, replica_groups=mesh['mem'=4,'lat'=8] {'mem','lat'}, dimensions={0} | all-to-all | bytes 32768 | tf_op jit(solution)/shard_map/all_to_all | solution.py:678
  (66 shorter events, 24.2 us)
Async XLA Ops:
  1.8 7.7 %collective-permute-start.2 = (f32[240,128]{1,0:T(8,128)S(1)}, f32[240,128]{1,0:T(8,128)S(1)}, u32[]{:S(2)}, u32[]{:S(2)}) collective-permute-start(f32[240,128]{1,0:T(8,128)S(1)} %get-tuple-element.55), channel_id=1, source_target_pairs={{0,7},{1,2},{2,1},{3,4},{4,3},{5,6},{6,5},{7,0},{8,15},{9,10},{10,... | collective-permute-start | bytes 368648 | tf_op jit(solution)/shard_map/ppermute | solution.py:579
  5.2 6.5 %collective-permute-start = (f32[240,128]{1,0:T(8,128)S(1)}, f32[240,128]{1,0:T(8,128)S(1)}, u32[]{:S(2)}, u32[]{:S(2)}) collective-permute-start(f32[240,128]{1,0:T(8,128)S(1)} %get-tuple-element.53), channel_id=1, source_target_pairs={{0,7},{1,2},{2,1},{3,4},{4,3},{5,6},{6,5},{7,0},{8,15},{9,10},{10,... | collective-permute-start | bytes 368648 | tf_op jit(solution)/shard_map/ppermute | solution.py:579
  6.0 5.8 %collective-permute-start.1 = (f32[240,128]{1,0:T(8,128)S(1)}, f32[240,128]{1,0:T(8,128)S(1)}, u32[]{:S(2)}, u32[]{:S(2)}) collective-permute-start(f32[240,128]{1,0:T(8,128)S(1)} %get-tuple-element.53), channel_id=1, source_target_pairs={{0,1},{1,0},{2,3},{3,2},{4,5},{5,4},{6,7},{7,6},{8,9},{9,8},{10,11... | collective-permute-start | bytes 368648 | tf_op jit(solution)/shard_map/ppermute | solution.py:579
  12.9 7.9 %collective-permute-start.4 = (f32[184,128]{1,0:T(8,128)S(1)}, f32[184,128]{1,0:T(8,128)S(1)}, u32[]{:S(2)}, u32[]{:S(2)}) collective-permute-start(f32[184,128]{1,0:T(8,128)S(1)} %get-tuple-element.57), channel_id=1, source_target_pairs={{0,24},{8,16},{16,8},{24,0},{1,25},{9,17},{17,9},{25,1},{2,26},{10... | collective-permute-start | bytes 282632 | tf_op jit(solution)/shard_map/ppermute | solution.py:583
  17.2 7.4 %collective-permute-start.5 = (f32[184,128]{1,0:T(8,128)S(1)}, f32[184,128]{1,0:T(8,128)S(1)}, u32[]{:S(2)}, u32[]{:S(2)}) collective-permute-start(f32[184,128]{1,0:T(8,128)S(1)} %get-tuple-element.58), channel_id=1, source_target_pairs={{0,16},{8,24},{16,0},{24,8},{1,17},{9,25},{17,1},{25,9},{2,18},{10... | collective-permute-start | bytes 282632 | tf_op jit(solution)/shard_map/ppermute | solution.py:583
  17.2 7.4 %collective-permute-start.6 = (f32[184,128]{1,0:T(8,128)S(1)}, f32[184,128]{1,0:T(8,128)S(1)}, u32[]{:S(2)}, u32[]{:S(2)}) collective-permute-start(f32[184,128]{1,0:T(8,128)S(1)} %get-tuple-element.59), channel_id=1, source_target_pairs={{0,8},{8,0},{16,24},{24,16},{1,9},{9,1},{17,25},{25,17},{2,10},{10... | collective-permute-start | bytes 282632 | tf_op jit(solution)/shard_map/ppermute | solution.py:583
  24.6 7.5 %collective-permute-start.7 = (f32[184,128]{1,0:T(8,128)S(1)}, f32[184,128]{1,0:T(8,128)S(1)}, u32[]{:S(2)}, u32[]{:S(2)}) collective-permute-start(f32[184,128]{1,0:T(8,128)S(1)} %shard_map.63.refs_1_), channel_id=1, source_target_pairs={{0,24},{8,16},{16,8},{24,0},{1,25},{9,17},{17,9},{25,1},{2,26},{10... | collective-permute-start | bytes 282632 | tf_op jit(solution)/shard_map/ppermute | solution.py:583
  27.3 7.8 %collective-permute-start.8 = (f32[184,128]{1,0:T(8,128)S(1)}, f32[184,128]{1,0:T(8,128)S(1)}, u32[]{:S(2)}, u32[]{:S(2)}) collective-permute-start(f32[184,128]{1,0:T(8,128)S(1)} %shard_map.63.refs_1_), channel_id=1, source_target_pairs={{0,16},{8,24},{16,0},{24,8},{1,17},{9,25},{17,1},{25,9},{2,18},{10... | collective-permute-start | bytes 282632 | tf_op jit(solution)/shard_map/ppermute | solution.py:583
  27.3 7.8 %collective-permute-start.9 = (f32[184,128]{1,0:T(8,128)S(1)}, f32[184,128]{1,0:T(8,128)S(1)}, u32[]{:S(2)}, u32[]{:S(2)}) collective-permute-start(f32[184,128]{1,0:T(8,128)S(1)} %shard_map.63.refs_1_), channel_id=1, source_target_pairs={{0,8},{8,0},{16,24},{24,16},{1,9},{9,1},{17,25},{25,17},{2,10},{10... | collective-permute-start | bytes 282632 | tf_op jit(solution)/shard_map/ppermute | solution.py:583
  36.5 6.5 %collective-permute-start.14 = (f32[240,128]{1,0:T(8,128)S(1)}, f32[240,128]{1,0:T(8,128)S(1)}, u32[]{:S(2)}, u32[]{:S(2)}) collective-permute-start(f32[240,128]{1,0:T(8,128)S(1)} %get-tuple-element.67), channel_id=1, source_target_pairs={{0,7},{1,2},{2,1},{3,4},{4,3},{5,6},{6,5},{7,0},{8,15},{9,10},{10,... | collective-permute-start | bytes 368648 | tf_op jit(solution)/shard_map/ppermute | solution.py:579
  37.6 5.4 %collective-permute-start.15 = (f32[240,128]{1,0:T(8,128)S(1)}, f32[240,128]{1,0:T(8,128)S(1)}, u32[]{:S(2)}, u32[]{:S(2)}) collective-permute-start(f32[240,128]{1,0:T(8,128)S(1)} %get-tuple-element.68), channel_id=1, source_target_pairs={{0,1},{1,0},{2,3},{3,2},{4,5},{5,4},{6,7},{7,6},{8,9},{9,8},{10,11... | collective-permute-start | bytes 368648 | tf_op jit(solution)/shard_map/ppermute | solution.py:579
  39.4 6.4 %collective-permute-start.10 = (f32[240,128]{1,0:T(8,128)S(1)}, f32[240,128]{1,0:T(8,128)S(1)}, u32[]{:S(2)}, u32[]{:S(2)}) collective-permute-start(f32[240,128]{1,0:T(8,128)S(1)} %get-tuple-element.62), channel_id=1, source_target_pairs={{0,7},{1,2},{2,1},{3,4},{4,3},{5,6},{6,5},{7,0},{8,15},{9,10},{10,... | collective-permute-start | bytes 368648 | tf_op jit(solution)/shard_map/ppermute | solution.py:579
  40.5 5.3 %collective-permute-start.11 = (f32[240,128]{1,0:T(8,128)S(1)}, f32[240,128]{1,0:T(8,128)S(1)}, u32[]{:S(2)}, u32[]{:S(2)}) collective-permute-start(f32[240,128]{1,0:T(8,128)S(1)} %get-tuple-element.63), channel_id=1, source_target_pairs={{0,1},{1,0},{2,3},{3,2},{4,5},{5,4},{6,7},{7,6},{8,9},{9,8},{10,11... | collective-permute-start | bytes 368648 | tf_op jit(solution)/shard_map/ppermute | solution.py:579
  43.1 5.9 %collective-permute-start.16 = (f32[240,128]{1,0:T(8,128)S(1)}, f32[240,128]{1,0:T(8,128)S(1)}, u32[]{:S(2)}, u32[]{:S(2)}) collective-permute-start(f32[240,128]{1,0:T(8,128)S(1)} %get-tuple-element.70.refs_4_), channel_id=1, source_target_pairs={{0,7},{1,2},{2,1},{3,4},{4,3},{5,6},{6,5},{7,0},{8,15},{9,10},{10,... | collective-permute-start | bytes 368648 | tf_op jit(solution)/shard_map/ppermute | solution.py:579
  44.2 4.8 %collective-permute-start.17 = (f32[240,128]{1,0:T(8,128)S(1)}, f32[240,128]{1,0:T(8,128)S(1)}, u32[]{:S(2)}, u32[]{:S(2)}) collective-permute-start(f32[240,128]{1,0:T(8,128)S(1)} %get-tuple-element.70.refs_4_), channel_id=1, source_target_pairs={{0,1},{1,0},{2,3},{3,2},{4,5},{5,4},{6,7},{7,6},{8,9},{9,8},{10,11... | collective-permute-start | bytes 368648 | tf_op jit(solution)/shard_map/ppermute | solution.py:579
  45.9 6.2 %collective-permute-start.12 = (f32[240,128]{1,0:T(8,128)S(1)}, f32[240,128]{1,0:T(8,128)S(1)}, u32[]{:S(2)}, u32[]{:S(2)}) collective-permute-start(f32[240,128]{1,0:T(8,128)S(1)} %get-tuple-element.65.refs_5_), channel_id=1, source_target_pairs={{0,7},{1,2},{2,1},{3,4},{4,3},{5,6},{6,5},{7,0},{8,15},{9,10},{10,... | collective-permute-start | bytes 368648 | tf_op jit(solution)/shard_map/ppermute | solution.py:579
  47.2 4.9 %collective-permute-start.13 = (f32[240,128]{1,0:T(8,128)S(1)}, f32[240,128]{1,0:T(8,128)S(1)}, u32[]{:S(2)}, u32[]{:S(2)}) collective-permute-start(f32[240,128]{1,0:T(8,128)S(1)} %get-tuple-element.65.refs_5_), channel_id=1, source_target_pairs={{0,1},{1,0},{2,3},{3,2},{4,5},{5,4},{6,7},{7,6},{8,9},{9,8},{10,11... | collective-permute-start | bytes 368648 | tf_op jit(solution)/shard_map/ppermute | solution.py:579
  53.2 7.8 %collective-permute-start.18 = (f32[184,128]{1,0:T(8,128)S(1)}, f32[184,128]{1,0:T(8,128)S(1)}, u32[]{:S(2)}, u32[]{:S(2)}) collective-permute-start(f32[184,128]{1,0:T(8,128)S(1)} %get-tuple-element.72), channel_id=1, source_target_pairs={{0,16},{8,24},{16,0},{24,8},{1,17},{9,25},{17,1},{25,9},{2,18},{10... | collective-permute-start | bytes 282632 | tf_op jit(solution)/shard_map/ppermute | solution.py:583
  53.3 7.7 %collective-permute-start.19 = (f32[184,128]{1,0:T(8,128)S(1)}, f32[184,128]{1,0:T(8,128)S(1)}, u32[]{:S(2)}, u32[]{:S(2)}) collective-permute-start(f32[184,128]{1,0:T(8,128)S(1)} %get-tuple-element.73), channel_id=1, source_target_pairs={{0,8},{8,0},{16,24},{24,16},{1,9},{9,1},{17,25},{25,17},{2,10},{10... | collective-permute-start | bytes 282632 | tf_op jit(solution)/shard_map/ppermute | solution.py:583
  56.2 6.5 %collective-permute-start.20 = (f32[184,128]{1,0:T(8,128)S(1)}, f32[184,128]{1,0:T(8,128)S(1)}, u32[]{:S(2)}, u32[]{:S(2)}) collective-permute-start(f32[184,128]{1,0:T(8,128)S(1)} %get-tuple-element.74), channel_id=1, source_target_pairs={{0,24},{8,16},{16,8},{24,0},{1,25},{9,17},{17,9},{25,1},{2,26},{10... | collective-permute-start | bytes 282632 | tf_op jit(solution)/shard_map/ppermute | solution.py:583
  62.9 13.7 %collective-permute-start.21 = (f32[184,128]{1,0:T(8,128)S(1)}, f32[184,128]{1,0:T(8,128)S(1)}, u32[]{:S(2)}, u32[]{:S(2)}) collective-permute-start(f32[184,128]{1,0:T(8,128)S(1)} %get-tuple-element.75.refs_1_), channel_id=1, source_target_pairs={{0,24},{8,16},{16,8},{24,0},{1,25},{9,17},{17,9},{25,1},{2,26},{10... | collective-permute-start | bytes 282632 | tf_op jit(solution)/shard_map/ppermute | solution.py:583
  64.4 12.2 %collective-permute-start.22 = (f32[184,128]{1,0:T(8,128)S(1)}, f32[184,128]{1,0:T(8,128)S(1)}, u32[]{:S(2)}, u32[]{:S(2)}) collective-permute-start(f32[184,128]{1,0:T(8,128)S(1)} %get-tuple-element.75.refs_1_), channel_id=1, source_target_pairs={{0,16},{8,24},{16,0},{24,8},{1,17},{9,25},{17,1},{25,9},{2,18},{10... | collective-permute-start | bytes 282632 | tf_op jit(solution)/shard_map/ppermute | solution.py:583
  65.3 11.3 %collective-permute-start.23 = (f32[184,128]{1,0:T(8,128)S(1)}, f32[184,128]{1,0:T(8,128)S(1)}, u32[]{:S(2)}, u32[]{:S(2)}) collective-permute-start(f32[184,128]{1,0:T(8,128)S(1)} %get-tuple-element.75.refs_1_), channel_id=1, source_target_pairs={{0,8},{8,0},{16,24},{24,16},{1,9},{9,1},{17,25},{25,17},{2,10},{10... | collective-permute-start | bytes 282632 | tf_op jit(solution)/shard_map/ppermute | solution.py:583
  78.0 5.7 %collective-permute-start.24 = (f32[240,128]{1,0:T(8,128)S(1)}, f32[240,128]{1,0:T(8,128)S(1)}, u32[]{:S(2)}, u32[]{:S(2)}) collective-permute-start(f32[240,128]{1,0:T(8,128)S(1)} %get-tuple-element.79), channel_id=1, source_target_pairs={{0,7},{1,2},{2,1},{3,4},{4,3},{5,6},{6,5},{7,0},{8,15},{9,10},{10,... | collective-permute-start | bytes 368648 | tf_op jit(solution)/shard_map/ppermute | solution.py:579
  78.0 5.6 %collective-permute-start.25 = (f32[240,128]{1,0:T(8,128)S(1)}, f32[240,128]{1,0:T(8,128)S(1)}, u32[]{:S(2)}, u32[]{:S(2)}) collective-permute-start(f32[240,128]{1,0:T(8,128)S(1)} %get-tuple-element.80), channel_id=1, source_target_pairs={{0,1},{1,0},{2,3},{3,2},{4,5},{5,4},{6,7},{7,6},{8,9},{9,8},{10,11... | collective-permute-start | bytes 368648 | tf_op jit(solution)/shard_map/ppermute | solution.py:579
  79.9 6.5 %collective-permute-start.26 = (f32[240,128]{1,0:T(8,128)S(1)}, f32[240,128]{1,0:T(8,128)S(1)}, u32[]{:S(2)}, u32[]{:S(2)}) collective-permute-start(f32[240,128]{1,0:T(8,128)S(1)} %get-tuple-element.84), channel_id=1, source_target_pairs={{0,7},{1,2},{2,1},{3,4},{4,3},{5,6},{6,5},{7,0},{8,15},{9,10},{10,... | collective-permute-start | bytes 368648 | tf_op jit(solution)/shard_map/ppermute | solution.py:579
  83.8 5.3 %collective-permute-start.28 = (f32[240,128]{1,0:T(8,128)S(1)}, f32[240,128]{1,0:T(8,128)S(1)}, u32[]{:S(2)}, u32[]{:S(2)}) collective-permute-start(f32[240,128]{1,0:T(8,128)S(1)} %get-tuple-element.89.refs_4_), channel_id=1, source_target_pairs={{0,7},{1,2},{2,1},{3,4},{4,3},{5,6},{6,5},{7,0},{8,15},{9,10},{10,... | collective-permute-start | bytes 368648 | tf_op jit(solution)/shard_map/ppermute | solution.py:579
  86.6 6.0 %collective-permute-start.30 = (f32[240,128]{1,0:T(8,128)S(1)}, f32[240,128]{1,0:T(8,128)S(1)}, u32[]{:S(2)}, u32[]{:S(2)}) collective-permute-start(f32[240,128]{1,0:T(8,128)S(1)} %get-tuple-element.92.refs_5_), channel_id=1, source_target_pairs={{0,7},{1,2},{2,1},{3,4},{4,3},{5,6},{6,5},{7,0},{8,15},{9,10},{10,... | collective-permute-start | bytes 368648 | tf_op jit(solution)/shard_map/ppermute | solution.py:579
  87.6 5.0 %collective-permute-start.31 = (f32[240,128]{1,0:T(8,128)S(1)}, f32[240,128]{1,0:T(8,128)S(1)}, u32[]{:S(2)}, u32[]{:S(2)}) collective-permute-start(f32[240,128]{1,0:T(8,128)S(1)} %get-tuple-element.92.refs_5_), channel_id=1, source_target_pairs={{0,1},{1,0},{2,3},{3,2},{4,5},{5,4},{6,7},{7,6},{8,9},{9,8},{10,11... | collective-permute-start | bytes 368648 | tf_op jit(solution)/shard_map/ppermute | solution.py:579
  93.8 9.6 %collective-permute-start.32 = (f32[184,128]{1,0:T(8,128)S(1)}, f32[184,128]{1,0:T(8,128)S(1)}, u32[]{:S(2)}, u32[]{:S(2)}) collective-permute-start(f32[184,128]{1,0:T(8,128)S(1)} %get-tuple-element.95), channel_id=1, source_target_pairs={{0,16},{8,24},{16,0},{24,8},{1,17},{9,25},{17,1},{25,9},{2,18},{10... | collective-permute-start | bytes 282632 | tf_op jit(solution)/shard_map/ppermute | solution.py:583
  94.4 9.0 %collective-permute-start.33 = (f32[184,128]{1,0:T(8,128)S(1)}, f32[184,128]{1,0:T(8,128)S(1)}, u32[]{:S(2)}, u32[]{:S(2)}) collective-permute-start(f32[184,128]{1,0:T(8,128)S(1)} %get-tuple-element.96), channel_id=1, source_target_pairs={{0,8},{8,0},{16,24},{24,16},{1,9},{9,1},{17,25},{25,17},{2,10},{10... | collective-permute-start | bytes 282632 | tf_op jit(solution)/shard_map/ppermute | solution.py:583
  95.5 7.9 %collective-permute-start.34 = (f32[184,128]{1,0:T(8,128)S(1)}, f32[184,128]{1,0:T(8,128)S(1)}, u32[]{:S(2)}, u32[]{:S(2)}) collective-permute-start(f32[184,128]{1,0:T(8,128)S(1)} %get-tuple-element.97), channel_id=1, source_target_pairs={{0,24},{8,16},{16,8},{24,0},{1,25},{9,17},{17,9},{25,1},{2,26},{10... | collective-permute-start | bytes 282632 | tf_op jit(solution)/shard_map/ppermute | solution.py:583
  (6 other events, 65.2 us)

commit v5 on v4

--- a/solution.py
+++ b/solution.py
@@ -564,7 +564,11 @@
     n_mem, n_lat, members = size.n_mem, size.n_lat, size.members
     devices = n_mem * n_lat
     pairs = [(i, i ^ 1) for i in range(n_lat)]
-    cross = [(i, (i - 1 if i % 2 == 0 else i + 1) % n_lat) for i in range(n_lat)]
+    cross = []
+    for k in range(n_mem):
+        for i in range(n_lat):
+            to = (k ^ 1, i) if i in (0, n_lat - 1) else (k, i - 1 if i % 2 == 0 else i + 1)
+            cross.append((k * n_lat + i, to[0] * n_lat + to[1]))
     middle_first = sorted(range(1, n_mem), key=lambda d: (d != n_mem // 2, d))
     groups = range(GROUPS)
     slab = array(size.slab, size.ext)
@@ -576,7 +580,7 @@
     map_flops = 4 * size.group * size.fine_rows * size.fine_cols * 2 * LANES
 
     def swap(to_a, to_b):
-        return lax.ppermute(to_a, "lat", pairs), lax.ppermute(to_b, "lat", cross)
+        return lax.ppermute(to_a, "lat", pairs), lax.ppermute(to_b, ("mem", "lat"), cross)
 
     def exchange(parts, order):
         return [parts[0]] + [

time: 115 us -> 114 us (level)
  waiting for transfers between devices: 38.6 us -> 35.4 us
  blocking collectives: 19.2 us -> 20.7 us
    ppermute x20, waiting for transfers between devices: 15.5 us -> 8.92 us  [the longest x10 8.9 us: swap(): lax.ppermute(to_b, ('mem', 'lat'), cross)]
    ppermute x15, waiting for transfers between devices: 23.1 us -> 26.5 us  [exchange(): lax.ppermute(parts[d], 'mem', [(i, i ^ d) for i in range(n_mem)])]
    all_to_all x2, blocking collectives: 19.2 us -> 20.7 us  [everywhere(): lax.all_to_all(tile.reshape(devices, 1, LANES), ('mem', 'lat'), 0, 0)]
where the time goes in v5:
time: 114 us; the launch traced here: 113 us
  starting transfers between devices  38.5 us (34%)
  waiting for transfers between devices  35.4 us (31%)
  blocking collectives  20.7 us (18%)
  Pallas kernels  16.9 us (15%)
    ppermute x15, waiting for transfers between devices, exchange(): lax.ppermute(parts[d], 'mem', [(i, i ^ d) for i in range(n_mem)])  26.5 us
    ppermute x15, starting transfers between devices, exchange(): lax.ppermute(parts[d], 'mem', [(i, i ^ d) for i in range(n_mem)])  22.3 us
    all_to_all x2, blocking collectives, everywhere(): lax.all_to_all(tile.reshape(devices, 1, LANES), ('mem', 'lat'), 0, 0)  20.7 us
    pallas_call x20, Pallas kernels, call(): pl.pallas_call(kernel, out_shape=outs, in_specs=[pl.BlockSpec(memory_spac...  16.9 us
    ppermute x10, starting transfers between devices, swap(): lax.ppermute(to_b, ('mem', 'lat'), cross)  11.5 us
    ppermute x10, waiting for transfers between devices, swap(): lax.ppermute(to_b, ('mem', 'lat'), cross)  8.9 us
    ppermute x10, starting transfers between devices, swap(): lax.ppermute(to_a, 'lat', pairs)  4.72 us
  transfers between devices with their start and end apart: 35, of which 16 were waited for; matrix products, arithmetic and copies ran while one was open for 0% of the time, Pallas kernels for 8%

profile of v5, /device:TPU:0, one launch (start us, length us, event | category | flops | bytes accessed | tf_op | source)
XLA Modules:
  0.0 113.3 jit_solution(18292705614713760841)
XLA Ops:
  1.8 3.1 %collective-permute-start.2 = (f32[240,128]{1,0:T(8,128)S(1)}, f32[240,128]{1,0:T(8,128)S(1)}, u32[]{:S(2)}, u32[]{:S(2)}) collective-permute-start(f32[240,128]{1,0:T(8,128)S(1)} %get-tuple-element.55), channel_id=1, source_target_pairs={{0,8},{1,2},{2,1},{3,4},{4,3},{5,6},{6,5},{7,15},{8,0},{9,10},{10,... | collective-permute-start | bytes 368648 | tf_op jit(solution)/shard_map/ppermute | solution.py:583
  5.0 1.6 %collective-permute-start = (f32[240,128]{1,0:T(8,128)S(1)}, f32[240,128]{1,0:T(8,128)S(1)}, u32[]{:S(2)}, u32[]{:S(2)}) collective-permute-start(f32[240,128]{1,0:T(8,128)S(1)} %get-tuple-element.53), channel_id=1, source_target_pairs={{0,8},{1,2},{2,1},{3,4},{4,3},{5,6},{6,5},{7,15},{8,0},{9,10},{10,... | collective-permute-start | bytes 368648 | tf_op jit(solution)/shard_map/ppermute | solution.py:583
  6.6 2.9 %shard_map.59.pert_ref.refs_0_ = f32[32,3,24,1280]{3,2,1,0:T(8,128)S(1)} custom-call(bf16[32,3,24,1280]{3,2,1,0:T(8,128)(2,1)} %pert_ref.1), custom_call_target="tpu_custom_call" | custom-call | flops 1006632960 | bytes 5898240 | tf_op jit(solution)/shard_map/pallas_call | solution.py:551
  11.7 3.7 %collective-permute-start.4 = (f32[184,128]{1,0:T(8,128)S(1)}, f32[184,128]{1,0:T(8,128)S(1)}, u32[]{:S(2)}, u32[]{:S(2)}) collective-permute-start(f32[184,128]{1,0:T(8,128)S(1)} %get-tuple-element.57), channel_id=1, source_target_pairs={{0,24},{8,16},{16,8},{24,0},{1,25},{9,17},{17,9},{25,1},{2,26},{10... | collective-permute-start | bytes 282632 | tf_op jit(solution)/shard_map/ppermute | solution.py:587
  16.2 3.0 %collective-permute-done.4.refs_1_ = f32[184,128]{1,0:T(8,128)S(1)} collective-permute-done((f32[184,128]{1,0:T(8,128)S(1)}, f32[184,128]{1,0:T(8,128)S(1)}, u32[]{:S(2)}, u32[]{:S(2)}) %collective-permute-start.4) | collective-permute-done | bytes 94240 | tf_op jit(solution)/shard_map/ppermute | solution.py:587
  19.2 4.6 %collective-permute-done.5.refs_2_ = f32[184,128]{1,0:T(8,128)S(1)} collective-permute-done((f32[184,128]{1,0:T(8,128)S(1)}, f32[184,128]{1,0:T(8,128)S(1)}, u32[]{:S(2)}, u32[]{:S(2)}) %collective-permute-start.5) | collective-permute-done | bytes 94240 | tf_op jit(solution)/shard_map/ppermute | solution.py:587
  23.8 2.7 %collective-permute-start.7 = (f32[184,128]{1,0:T(8,128)S(1)}, f32[184,128]{1,0:T(8,128)S(1)}, u32[]{:S(2)}, u32[]{:S(2)}) collective-permute-start(f32[184,128]{1,0:T(8,128)S(1)} %shard_map.63.refs_1_), channel_id=1, source_target_pairs={{0,24},{8,16},{16,8},{24,0},{1,25},{9,17},{17,9},{25,1},{2,26},{10... | collective-permute-start | bytes 282632 | tf_op jit(solution)/shard_map/ppermute | solution.py:587
  26.5 1.7 %collective-permute-start.9 = (f32[184,128]{1,0:T(8,128)S(1)}, f32[184,128]{1,0:T(8,128)S(1)}, u32[]{:S(2)}, u32[]{:S(2)}) collective-permute-start(f32[184,128]{1,0:T(8,128)S(1)} %shard_map.63.refs_1_), channel_id=1, source_target_pairs={{0,8},{8,0},{16,24},{24,16},{1,9},{9,1},{17,25},{25,17},{2,10},{10... | collective-permute-start | bytes 282632 | tf_op jit(solution)/shard_map/ppermute | solution.py:587
  28.3 2.8 %collective-permute-done.7.refs_2_ = f32[184,128]{1,0:T(8,128)S(1)} collective-permute-done((f32[184,128]{1,0:T(8,128)S(1)}, f32[184,128]{1,0:T(8,128)S(1)}, u32[]{:S(2)}, u32[]{:S(2)}) %collective-permute-start.7) | collective-permute-done | bytes 94240 | tf_op jit(solution)/shard_map/ppermute | solution.py:587
  31.1 3.2 %collective-permute-done.8.refs_3_ = f32[184,128]{1,0:T(8,128)S(1)} collective-permute-done((f32[184,128]{1,0:T(8,128)S(1)}, f32[184,128]{1,0:T(8,128)S(1)}, u32[]{:S(2)}, u32[]{:S(2)}) %collective-permute-start.8) | collective-permute-done | bytes 94240 | tf_op jit(solution)/shard_map/ppermute | solution.py:587
  34.3 1.4 %shard_map.64 = (f32[240,128]{1,0:T(8,128)S(1)}, f32[240,128]{1,0:T(8,128)S(1)}, f32[96,384]{1,0:T(8,128)S(1)}, f32[736,128]{1,0:T(8,128)S(1)}, f32[736,128]{1,0:T(8,128)S(1)}) custom-call(f32[32,3,24,1280]{3,2,1,0:T(8,128)S(1)} %shard_map.59.pert_ref.refs_0_, f32[184,128]{1,0:T(8,128)S(1)} %shard_map.63.refs_1_, ...), custom_call_target="tpu_custom_call" | custom-call | flops 503316480 | bytes 12541964 | tf_op jit(solution)/shard_map/pallas_call | solution.py:551
  36.3 1.8 %collective-permute-start.15 = (f32[240,128]{1,0:T(8,128)S(1)}, f32[240,128]{1,0:T(8,128)S(1)}, u32[]{:S(2)}, u32[]{:S(2)}) collective-permute-start(f32[240,128]{1,0:T(8,128)S(1)} %get-tuple-element.68), channel_id=1, source_target_pairs={{0,1},{1,0},{2,3},{3,2},{4,5},{5,4},{6,7},{7,6},{8,9},{9,8},{10,11... | collective-permute-start | bytes 368648 | tf_op jit(solution)/shard_map/ppermute | solution.py:583
  38.1 1.2 %shard_map.65 = (f32[240,128]{1,0:T(8,128)S(1)}, f32[240,128]{1,0:T(8,128)S(1)}, f32[96,384]{1,0:T(8,128)S(1)}) custom-call(f32[32,3,24,1280]{3,2,1,0:T(8,128)S(1)} %shard_map.59.pert_ref.refs_0_, f32[736,128]{1,0:T(8,128)S(1)} %get-tuple-element.60.refs_1_), custom_call_target="tpu_custom_call" | custom-call | flops 503316480 | bytes 12173312 | tf_op jit(solution)/shard_map/pallas_call | solution.py:551
  42.7 1.6 %collective-permute-done.10.refs_1_ = f32[240,128]{1,0:T(8,128)S(1)} collective-permute-done((f32[240,128]{1,0:T(8,128)S(1)}, f32[240,128]{1,0:T(8,128)S(1)}, u32[]{:S(2)}, u32[]{:S(2)}) %collective-permute-start.10) | collective-permute-done | bytes 122912 | tf_op jit(solution)/shard_map/ppermute | solution.py:583
  46.7 2.7 %collective-permute-done.12.b_ref = f32[240,128]{1,0:T(8,128)S(1)} collective-permute-done((f32[240,128]{1,0:T(8,128)S(1)}, f32[240,128]{1,0:T(8,128)S(1)}, u32[]{:S(2)}, u32[]{:S(2)}) %collective-permute-start.12) | collective-permute-done | bytes 122912 | tf_op jit(solution)/shard_map/ppermute | solution.py:583
  51.3 2.0 %collective-permute-start.19 = (f32[184,128]{1,0:T(8,128)S(1)}, f32[184,128]{1,0:T(8,128)S(1)}, u32[]{:S(2)}, u32[]{:S(2)}) collective-permute-start(f32[184,128]{1,0:T(8,128)S(1)} %get-tuple-element.73), channel_id=1, source_target_pairs={{0,8},{8,0},{16,24},{24,16},{1,9},{9,1},{17,25},{25,17},{2,10},{10... | collective-permute-start | bytes 282632 | tf_op jit(solution)/shard_map/ppermute | solution.py:587
  53.4 1.6 %collective-permute-start.20 = (f32[184,128]{1,0:T(8,128)S(1)}, f32[184,128]{1,0:T(8,128)S(1)}, u32[]{:S(2)}, u32[]{:S(2)}) collective-permute-start(f32[184,128]{1,0:T(8,128)S(1)} %get-tuple-element.74), channel_id=1, source_target_pairs={{0,24},{8,16},{16,8},{24,0},{1,25},{9,17},{17,9},{25,1},{2,26},{10... | collective-permute-start | bytes 282632 | tf_op jit(solution)/shard_map/ppermute | solution.py:587
  55.0 4.2 %collective-permute-done.18.refs_1_ = f32[184,128]{1,0:T(8,128)S(1)} collective-permute-done((f32[184,128]{1,0:T(8,128)S(1)}, f32[184,128]{1,0:T(8,128)S(1)}, u32[]{:S(2)}, u32[]{:S(2)}) %collective-permute-start.18) | collective-permute-done | bytes 94240 | tf_op jit(solution)/shard_map/ppermute | solution.py:587
  59.2 1.7 %collective-permute-done.20.refs_3_ = f32[184,128]{1,0:T(8,128)S(1)} collective-permute-done((f32[184,128]{1,0:T(8,128)S(1)}, f32[184,128]{1,0:T(8,128)S(1)}, u32[]{:S(2)}, u32[]{:S(2)}) %collective-permute-start.20) | collective-permute-done | bytes 94240 | tf_op jit(solution)/shard_map/ppermute | solution.py:587
  61.1 1.9 %collective-permute-start.21 = (f32[184,128]{1,0:T(8,128)S(1)}, f32[184,128]{1,0:T(8,128)S(1)}, u32[]{:S(2)}, u32[]{:S(2)}) collective-permute-start(f32[184,128]{1,0:T(8,128)S(1)} %get-tuple-element.75.refs_1_), channel_id=1, source_target_pairs={{0,24},{8,16},{16,8},{24,0},{1,25},{9,17},{17,9},{25,1},{2,26},{10... | collective-permute-start | bytes 282632 | tf_op jit(solution)/shard_map/ppermute | solution.py:587
  63.0 1.9 %collective-permute-start.22 = (f32[184,128]{1,0:T(8,128)S(1)}, f32[184,128]{1,0:T(8,128)S(1)}, u32[]{:S(2)}, u32[]{:S(2)}) collective-permute-start(f32[184,128]{1,0:T(8,128)S(1)} %get-tuple-element.75.refs_1_), channel_id=1, source_target_pairs={{0,16},{8,24},{16,0},{24,8},{1,17},{9,25},{17,1},{25,9},{2,18},{10... | collective-permute-start | bytes 282632 | tf_op jit(solution)/shard_map/ppermute | solution.py:587
  65.5 10.5 %all_to_all.10 = f32[32,1,128]{2,1,0:T(1,128)S(1)} all-to-all(f32[32,1,128]{2,1,0:T(1,128)S(1)} %bitcast.21), channel_id=1, replica_groups=mesh['mem'=4,'lat'=8] {'mem','lat'}, dimensions={0} | all-to-all | bytes 32768 | tf_op jit(solution)/shard_map/all_to_all | solution.py:682
  76.1 1.3 %shard_map.71 = (f32[240,128]{1,0:T(8,128)S(1)}, f32[240,128]{1,0:T(8,128)S(1)}, f32[96,384]{1,0:T(8,128)S(1)}, f32[736,128]{1,0:T(8,128)S(1)}, f32[736,128]{1,0:T(8,128)S(1)}) custom-call(f32[32,3,24,1280]{3,2,1,0:T(8,128)S(1)} %shard_map.59.pert_ref.refs_0_, f32[184,128]{1,0:T(8,128)S(1)} %get-tuple-element.75.refs_1_, ...), custom_call_target="tpu_custom_call" | custom-call | flops 503316480 | bytes 12935180 | tf_op jit(solution)/shard_map/pallas_call | solution.py:551
  78.1 1.2 %shard_map.73 = (f32[240,128]{1,0:T(8,128)S(1)}, f32[240,128]{1,0:T(8,128)S(1)}, f32[96,384]{1,0:T(8,128)S(1)}) custom-call(f32[32,3,24,1280]{3,2,1,0:T(8,128)S(1)} %shard_map.59.pert_ref.refs_0_, f32[736,128]{1,0:T(8,128)S(1)} %get-tuple-element.82.refs_1_), custom_call_target="tpu_custom_call" | custom-call | flops 503316480 | bytes 12173312 | tf_op jit(solution)/shard_map/pallas_call | solution.py:551
  79.3 1.4 %collective-permute-start.26 = (f32[240,128]{1,0:T(8,128)S(1)}, f32[240,128]{1,0:T(8,128)S(1)}, u32[]{:S(2)}, u32[]{:S(2)}) collective-permute-start(f32[240,128]{1,0:T(8,128)S(1)} %get-tuple-element.84), channel_id=1, source_target_pairs={{0,8},{1,2},{2,1},{3,4},{4,3},{5,6},{6,5},{7,15},{8,0},{9,10},{10,... | collective-permute-start | bytes 368648 | tf_op jit(solution)/shard_map/ppermute | solution.py:583
  81.0 1.4 %collective-permute-done.24.refs_1_ = f32[240,128]{1,0:T(8,128)S(1)} collective-permute-done((f32[240,128]{1,0:T(8,128)S(1)}, f32[240,128]{1,0:T(8,128)S(1)}, u32[]{:S(2)}, u32[]{:S(2)}) %collective-permute-start.24) | collective-permute-done | bytes 122912 | tf_op jit(solution)/shard_map/ppermute | solution.py:583
  84.4 1.4 %collective-permute-start.30 = (f32[240,128]{1,0:T(8,128)S(1)}, f32[240,128]{1,0:T(8,128)S(1)}, u32[]{:S(2)}, u32[]{:S(2)}) collective-permute-start(f32[240,128]{1,0:T(8,128)S(1)} %get-tuple-element.92.refs_5_), channel_id=1, source_target_pairs={{0,8},{1,2},{2,1},{3,4},{4,3},{5,6},{6,5},{7,15},{8,0},{9,10},{10,... | collective-permute-start | bytes 368648 | tf_op jit(solution)/shard_map/ppermute | solution.py:583
  91.2 1.4 %collective-permute-start.33 = (f32[184,128]{1,0:T(8,128)S(1)}, f32[184,128]{1,0:T(8,128)S(1)}, u32[]{:S(2)}, u32[]{:S(2)}) collective-permute-start(f32[184,128]{1,0:T(8,128)S(1)} %get-tuple-element.96), channel_id=1, source_target_pairs={{0,8},{8,0},{16,24},{24,16},{1,9},{9,1},{17,25},{25,17},{2,10},{10... | collective-permute-start | bytes 282632 | tf_op jit(solution)/shard_map/ppermute | solution.py:587
  92.6 2.4 %collective-permute-start.34 = (f32[184,128]{1,0:T(8,128)S(1)}, f32[184,128]{1,0:T(8,128)S(1)}, u32[]{:S(2)}, u32[]{:S(2)}) collective-permute-start(f32[184,128]{1,0:T(8,128)S(1)} %get-tuple-element.97), channel_id=1, source_target_pairs={{0,24},{8,16},{16,8},{24,0},{1,25},{9,17},{17,9},{25,1},{2,26},{10... | collective-permute-start | bytes 282632 | tf_op jit(solution)/shard_map/ppermute | solution.py:587
  95.0 3.2 %collective-permute-done.32.refs_1_ = f32[184,128]{1,0:T(8,128)S(1)} collective-permute-done((f32[184,128]{1,0:T(8,128)S(1)}, f32[184,128]{1,0:T(8,128)S(1)}, u32[]{:S(2)}, u32[]{:S(2)}) %collective-permute-start.32) | collective-permute-done | bytes 94240 | tf_op jit(solution)/shard_map/ppermute | solution.py:587
  98.2 3.7 %collective-permute-done.34.refs_3_ = f32[184,128]{1,0:T(8,128)S(1)} collective-permute-done((f32[184,128]{1,0:T(8,128)S(1)}, f32[184,128]{1,0:T(8,128)S(1)}, u32[]{:S(2)}, u32[]{:S(2)}) %collective-permute-start.34) | collective-permute-done | bytes 94240 | tf_op jit(solution)/shard_map/ppermute | solution.py:587
  102.1 10.2 %all_to_all.11 = f32[32,1,128]{2,1,0:T(1,128)S(1)} all-to-all(f32[32,1,128]{2,1,0:T(1,128)S(1)} %bitcast.22), channel_id=1, replica_groups=mesh['mem'=4,'lat'=8] {'mem','lat'}, dimensions={0} | all-to-all | bytes 32768 | tf_op jit(solution)/shard_map/all_to_all | solution.py:682
  (66 shorter events, 22.8 us)
Async XLA Ops:
  1.8 7.7 %collective-permute-start.2 = (f32[240,128]{1,0:T(8,128)S(1)}, f32[240,128]{1,0:T(8,128)S(1)}, u32[]{:S(2)}, u32[]{:S(2)}) collective-permute-start(f32[240,128]{1,0:T(8,128)S(1)} %get-tuple-element.55), channel_id=1, source_target_pairs={{0,8},{1,2},{2,1},{3,4},{4,3},{5,6},{6,5},{7,15},{8,0},{9,10},{10,... | collective-permute-start | bytes 368648 | tf_op jit(solution)/shard_map/ppermute | solution.py:583
  4.9 4.6 %collective-permute-start.3 = (f32[240,128]{1,0:T(8,128)S(1)}, f32[240,128]{1,0:T(8,128)S(1)}, u32[]{:S(2)}, u32[]{:S(2)}) collective-permute-start(f32[240,128]{1,0:T(8,128)S(1)} %get-tuple-element.55), channel_id=1, source_target_pairs={{0,1},{1,0},{2,3},{3,2},{4,5},{5,4},{6,7},{7,6},{8,9},{9,8},{10,11... | collective-permute-start | bytes 368648 | tf_op jit(solution)/shard_map/ppermute | solution.py:583
  5.0 5.7 %collective-permute-start = (f32[240,128]{1,0:T(8,128)S(1)}, f32[240,128]{1,0:T(8,128)S(1)}, u32[]{:S(2)}, u32[]{:S(2)}) collective-permute-start(f32[240,128]{1,0:T(8,128)S(1)} %get-tuple-element.53), channel_id=1, source_target_pairs={{0,8},{1,2},{2,1},{3,4},{4,3},{5,6},{6,5},{7,15},{8,0},{9,10},{10,... | collective-permute-start | bytes 368648 | tf_op jit(solution)/shard_map/ppermute | solution.py:583
  6.5 4.1 %collective-permute-start.1 = (f32[240,128]{1,0:T(8,128)S(1)}, f32[240,128]{1,0:T(8,128)S(1)}, u32[]{:S(2)}, u32[]{:S(2)}) collective-permute-start(f32[240,128]{1,0:T(8,128)S(1)} %get-tuple-element.53), channel_id=1, source_target_pairs={{0,1},{1,0},{2,3},{3,2},{4,5},{5,4},{6,7},{7,6},{8,9},{9,8},{10,11... | collective-permute-start | bytes 368648 | tf_op jit(solution)/shard_map/ppermute | solution.py:583
  11.7 7.5 %collective-permute-start.4 = (f32[184,128]{1,0:T(8,128)S(1)}, f32[184,128]{1,0:T(8,128)S(1)}, u32[]{:S(2)}, u32[]{:S(2)}) collective-permute-start(f32[184,128]{1,0:T(8,128)S(1)} %get-tuple-element.57), channel_id=1, source_target_pairs={{0,24},{8,16},{16,8},{24,0},{1,25},{9,17},{17,9},{25,1},{2,26},{10... | collective-permute-start | bytes 282632 | tf_op jit(solution)/shard_map/ppermute | solution.py:587
  15.4 8.4 %collective-permute-start.5 = (f32[184,128]{1,0:T(8,128)S(1)}, f32[184,128]{1,0:T(8,128)S(1)}, u32[]{:S(2)}, u32[]{:S(2)}) collective-permute-start(f32[184,128]{1,0:T(8,128)S(1)} %get-tuple-element.58), channel_id=1, source_target_pairs={{0,16},{8,24},{16,0},{24,8},{1,17},{9,25},{17,1},{25,9},{2,18},{10... | collective-permute-start | bytes 282632 | tf_op jit(solution)/shard_map/ppermute | solution.py:587
  15.4 8.4 %collective-permute-start.6 = (f32[184,128]{1,0:T(8,128)S(1)}, f32[184,128]{1,0:T(8,128)S(1)}, u32[]{:S(2)}, u32[]{:S(2)}) collective-permute-start(f32[184,128]{1,0:T(8,128)S(1)} %get-tuple-element.59), channel_id=1, source_target_pairs={{0,8},{8,0},{16,24},{24,16},{1,9},{9,1},{17,25},{25,17},{2,10},{10... | collective-permute-start | bytes 282632 | tf_op jit(solution)/shard_map/ppermute | solution.py:587
  23.8 7.2 %collective-permute-start.7 = (f32[184,128]{1,0:T(8,128)S(1)}, f32[184,128]{1,0:T(8,128)S(1)}, u32[]{:S(2)}, u32[]{:S(2)}) collective-permute-start(f32[184,128]{1,0:T(8,128)S(1)} %shard_map.63.refs_1_), channel_id=1, source_target_pairs={{0,24},{8,16},{16,8},{24,0},{1,25},{9,17},{17,9},{25,1},{2,26},{10... | collective-permute-start | bytes 282632 | tf_op jit(solution)/shard_map/ppermute | solution.py:587
  26.5 7.7 %collective-permute-start.8 = (f32[184,128]{1,0:T(8,128)S(1)}, f32[184,128]{1,0:T(8,128)S(1)}, u32[]{:S(2)}, u32[]{:S(2)}) collective-permute-start(f32[184,128]{1,0:T(8,128)S(1)} %shard_map.63.refs_1_), channel_id=1, source_target_pairs={{0,16},{8,24},{16,0},{24,8},{1,17},{9,25},{17,1},{25,9},{2,18},{10... | collective-permute-start | bytes 282632 | tf_op jit(solution)/shard_map/ppermute | solution.py:587
  26.5 7.7 %collective-permute-start.9 = (f32[184,128]{1,0:T(8,128)S(1)}, f32[184,128]{1,0:T(8,128)S(1)}, u32[]{:S(2)}, u32[]{:S(2)}) collective-permute-start(f32[184,128]{1,0:T(8,128)S(1)} %shard_map.63.refs_1_), channel_id=1, source_target_pairs={{0,8},{8,0},{16,24},{24,16},{1,9},{9,1},{17,25},{25,17},{2,10},{10... | collective-permute-start | bytes 282632 | tf_op jit(solution)/shard_map/ppermute | solution.py:587
  35.6 4.9 %collective-permute-start.14 = (f32[240,128]{1,0:T(8,128)S(1)}, f32[240,128]{1,0:T(8,128)S(1)}, u32[]{:S(2)}, u32[]{:S(2)}) collective-permute-start(f32[240,128]{1,0:T(8,128)S(1)} %get-tuple-element.67), channel_id=1, source_target_pairs={{0,8},{1,2},{2,1},{3,4},{4,3},{5,6},{6,5},{7,15},{8,0},{9,10},{10,... | collective-permute-start | bytes 368648 | tf_op jit(solution)/shard_map/ppermute | solution.py:583
  36.3 4.2 %collective-permute-start.15 = (f32[240,128]{1,0:T(8,128)S(1)}, f32[240,128]{1,0:T(8,128)S(1)}, u32[]{:S(2)}, u32[]{:S(2)}) collective-permute-start(f32[240,128]{1,0:T(8,128)S(1)} %get-tuple-element.68), channel_id=1, source_target_pairs={{0,1},{1,0},{2,3},{3,2},{4,5},{5,4},{6,7},{7,6},{8,9},{9,8},{10,11... | collective-permute-start | bytes 368648 | tf_op jit(solution)/shard_map/ppermute | solution.py:583
  39.4 4.9 %collective-permute-start.10 = (f32[240,128]{1,0:T(8,128)S(1)}, f32[240,128]{1,0:T(8,128)S(1)}, u32[]{:S(2)}, u32[]{:S(2)}) collective-permute-start(f32[240,128]{1,0:T(8,128)S(1)} %get-tuple-element.62), channel_id=1, source_target_pairs={{0,8},{1,2},{2,1},{3,4},{4,3},{5,6},{6,5},{7,15},{8,0},{9,10},{10,... | collective-permute-start | bytes 368648 | tf_op jit(solution)/shard_map/ppermute | solution.py:583
  39.9 4.4 %collective-permute-start.11 = (f32[240,128]{1,0:T(8,128)S(1)}, f32[240,128]{1,0:T(8,128)S(1)}, u32[]{:S(2)}, u32[]{:S(2)}) collective-permute-start(f32[240,128]{1,0:T(8,128)S(1)} %get-tuple-element.63), channel_id=1, source_target_pairs={{0,1},{1,0},{2,3},{3,2},{4,5},{5,4},{6,7},{7,6},{8,9},{9,8},{10,11... | collective-permute-start | bytes 368648 | tf_op jit(solution)/shard_map/ppermute | solution.py:583
  40.8 4.9 %collective-permute-start.16 = (f32[240,128]{1,0:T(8,128)S(1)}, f32[240,128]{1,0:T(8,128)S(1)}, u32[]{:S(2)}, u32[]{:S(2)}) collective-permute-start(f32[240,128]{1,0:T(8,128)S(1)} %get-tuple-element.70.refs_4_), channel_id=1, source_target_pairs={{0,8},{1,2},{2,1},{3,4},{4,3},{5,6},{6,5},{7,15},{8,0},{9,10},{10,... | collective-permute-start | bytes 368648 | tf_op jit(solution)/shard_map/ppermute | solution.py:583
  44.5 4.9 %collective-permute-start.12 = (f32[240,128]{1,0:T(8,128)S(1)}, f32[240,128]{1,0:T(8,128)S(1)}, u32[]{:S(2)}, u32[]{:S(2)}) collective-permute-start(f32[240,128]{1,0:T(8,128)S(1)} %get-tuple-element.65.refs_5_), channel_id=1, source_target_pairs={{0,8},{1,2},{2,1},{3,4},{4,3},{5,6},{6,5},{7,15},{8,0},{9,10},{10,... | collective-permute-start | bytes 368648 | tf_op jit(solution)/shard_map/ppermute | solution.py:583
  45.0 4.4 %collective-permute-start.13 = (f32[240,128]{1,0:T(8,128)S(1)}, f32[240,128]{1,0:T(8,128)S(1)}, u32[]{:S(2)}, u32[]{:S(2)}) collective-permute-start(f32[240,128]{1,0:T(8,128)S(1)} %get-tuple-element.65.refs_5_), channel_id=1, source_target_pairs={{0,1},{1,0},{2,3},{3,2},{4,5},{5,4},{6,7},{7,6},{8,9},{9,8},{10,11... | collective-permute-start | bytes 368648 | tf_op jit(solution)/shard_map/ppermute | solution.py:583
  50.5 8.7 %collective-permute-start.18 = (f32[184,128]{1,0:T(8,128)S(1)}, f32[184,128]{1,0:T(8,128)S(1)}, u32[]{:S(2)}, u32[]{:S(2)}) collective-permute-start(f32[184,128]{1,0:T(8,128)S(1)} %get-tuple-element.72), channel_id=1, source_target_pairs={{0,16},{8,24},{16,0},{24,8},{1,17},{9,25},{17,1},{25,9},{2,18},{10... | collective-permute-start | bytes 282632 | tf_op jit(solution)/shard_map/ppermute | solution.py:587
  51.3 7.9 %collective-permute-start.19 = (f32[184,128]{1,0:T(8,128)S(1)}, f32[184,128]{1,0:T(8,128)S(1)}, u32[]{:S(2)}, u32[]{:S(2)}) collective-permute-start(f32[184,128]{1,0:T(8,128)S(1)} %get-tuple-element.73), channel_id=1, source_target_pairs={{0,8},{8,0},{16,24},{24,16},{1,9},{9,1},{17,25},{25,17},{2,10},{10... | collective-permute-start | bytes 282632 | tf_op jit(solution)/shard_map/ppermute | solution.py:587
  53.4 7.5 %collective-permute-start.20 = (f32[184,128]{1,0:T(8,128)S(1)}, f32[184,128]{1,0:T(8,128)S(1)}, u32[]{:S(2)}, u32[]{:S(2)}) collective-permute-start(f32[184,128]{1,0:T(8,128)S(1)} %get-tuple-element.74), channel_id=1, source_target_pairs={{0,24},{8,16},{16,8},{24,0},{1,25},{9,17},{17,9},{25,1},{2,26},{10... | collective-permute-start | bytes 282632 | tf_op jit(solution)/shard_map/ppermute | solution.py:587
  61.1 15.0 %collective-permute-start.21 = (f32[184,128]{1,0:T(8,128)S(1)}, f32[184,128]{1,0:T(8,128)S(1)}, u32[]{:S(2)}, u32[]{:S(2)}) collective-permute-start(f32[184,128]{1,0:T(8,128)S(1)} %get-tuple-element.75.refs_1_), channel_id=1, source_target_pairs={{0,24},{8,16},{16,8},{24,0},{1,25},{9,17},{17,9},{25,1},{2,26},{10... | collective-permute-start | bytes 282632 | tf_op jit(solution)/shard_map/ppermute | solution.py:587
  63.0 13.0 %collective-permute-start.22 = (f32[184,128]{1,0:T(8,128)S(1)}, f32[184,128]{1,0:T(8,128)S(1)}, u32[]{:S(2)}, u32[]{:S(2)}) collective-permute-start(f32[184,128]{1,0:T(8,128)S(1)} %get-tuple-element.75.refs_1_), channel_id=1, source_target_pairs={{0,16},{8,24},{16,0},{24,8},{1,17},{9,25},{17,1},{25,9},{2,18},{10... | collective-permute-start | bytes 282632 | tf_op jit(solution)/shard_map/ppermute | solution.py:587
  65.0 11.1 %collective-permute-start.23 = (f32[184,128]{1,0:T(8,128)S(1)}, f32[184,128]{1,0:T(8,128)S(1)}, u32[]{:S(2)}, u32[]{:S(2)}) collective-permute-start(f32[184,128]{1,0:T(8,128)S(1)} %get-tuple-element.75.refs_1_), channel_id=1, source_target_pairs={{0,8},{8,0},{16,24},{24,16},{1,9},{9,1},{17,25},{25,17},{2,10},{10... | collective-permute-start | bytes 282632 | tf_op jit(solution)/shard_map/ppermute | solution.py:587
  77.4 4.9 %collective-permute-start.24 = (f32[240,128]{1,0:T(8,128)S(1)}, f32[240,128]{1,0:T(8,128)S(1)}, u32[]{:S(2)}, u32[]{:S(2)}) collective-permute-start(f32[240,128]{1,0:T(8,128)S(1)} %get-tuple-element.79), channel_id=1, source_target_pairs={{0,8},{1,2},{2,1},{3,4},{4,3},{5,6},{6,5},{7,15},{8,0},{9,10},{10,... | collective-permute-start | bytes 368648 | tf_op jit(solution)/shard_map/ppermute | solution.py:583
  78.0 4.3 %collective-permute-start.25 = (f32[240,128]{1,0:T(8,128)S(1)}, f32[240,128]{1,0:T(8,128)S(1)}, u32[]{:S(2)}, u32[]{:S(2)}) collective-permute-start(f32[240,128]{1,0:T(8,128)S(1)} %get-tuple-element.80), channel_id=1, source_target_pairs={{0,1},{1,0},{2,3},{3,2},{4,5},{5,4},{6,7},{7,6},{8,9},{9,8},{10,11... | collective-permute-start | bytes 368648 | tf_op jit(solution)/shard_map/ppermute | solution.py:583
  79.3 4.9 %collective-permute-start.26 = (f32[240,128]{1,0:T(8,128)S(1)}, f32[240,128]{1,0:T(8,128)S(1)}, u32[]{:S(2)}, u32[]{:S(2)}) collective-permute-start(f32[240,128]{1,0:T(8,128)S(1)} %get-tuple-element.84), channel_id=1, source_target_pairs={{0,8},{1,2},{2,1},{3,4},{4,3},{5,6},{6,5},{7,15},{8,0},{9,10},{10,... | collective-permute-start | bytes 368648 | tf_op jit(solution)/shard_map/ppermute | solution.py:583
  82.5 4.9 %collective-permute-start.28 = (f32[240,128]{1,0:T(8,128)S(1)}, f32[240,128]{1,0:T(8,128)S(1)}, u32[]{:S(2)}, u32[]{:S(2)}) collective-permute-start(f32[240,128]{1,0:T(8,128)S(1)} %get-tuple-element.89.refs_4_), channel_id=1, source_target_pairs={{0,8},{1,2},{2,1},{3,4},{4,3},{5,6},{6,5},{7,15},{8,0},{9,10},{10,... | collective-permute-start | bytes 368648 | tf_op jit(solution)/shard_map/ppermute | solution.py:583
  83.2 4.3 %collective-permute-start.29 = (f32[240,128]{1,0:T(8,128)S(1)}, f32[240,128]{1,0:T(8,128)S(1)}, u32[]{:S(2)}, u32[]{:S(2)}) collective-permute-start(f32[240,128]{1,0:T(8,128)S(1)} %get-tuple-element.89.refs_4_), channel_id=1, source_target_pairs={{0,1},{1,0},{2,3},{3,2},{4,5},{5,4},{6,7},{7,6},{8,9},{9,8},{10,11... | collective-permute-start | bytes 368648 | tf_op jit(solution)/shard_map/ppermute | solution.py:583
  84.4 4.9 %collective-permute-start.30 = (f32[240,128]{1,0:T(8,128)S(1)}, f32[240,128]{1,0:T(8,128)S(1)}, u32[]{:S(2)}, u32[]{:S(2)}) collective-permute-start(f32[240,128]{1,0:T(8,128)S(1)} %get-tuple-element.92.refs_5_), channel_id=1, source_target_pairs={{0,8},{1,2},{2,1},{3,4},{4,3},{5,6},{6,5},{7,15},{8,0},{9,10},{10,... | collective-permute-start | bytes 368648 | tf_op jit(solution)/shard_map/ppermute | solution.py:583
  90.6 7.7 %collective-permute-start.32 = (f32[184,128]{1,0:T(8,128)S(1)}, f32[184,128]{1,0:T(8,128)S(1)}, u32[]{:S(2)}, u32[]{:S(2)}) collective-permute-start(f32[184,128]{1,0:T(8,128)S(1)} %get-tuple-element.95), channel_id=1, source_target_pairs={{0,16},{8,24},{16,0},{24,8},{1,17},{9,25},{17,1},{25,9},{2,18},{10... | collective-permute-start | bytes 282632 | tf_op jit(solution)/shard_map/ppermute | solution.py:587
  91.2 7.0 %collective-permute-start.33 = (f32[184,128]{1,0:T(8,128)S(1)}, f32[184,128]{1,0:T(8,128)S(1)}, u32[]{:S(2)}, u32[]{:S(2)}) collective-permute-start(f32[184,128]{1,0:T(8,128)S(1)} %get-tuple-element.96), channel_id=1, source_target_pairs={{0,8},{8,0},{16,24},{24,16},{1,9},{9,1},{17,25},{25,17},{2,10},{10... | collective-permute-start | bytes 282632 | tf_op jit(solution)/shard_map/ppermute | solution.py:587
  92.6 9.3 %collective-permute-start.34 = (f32[184,128]{1,0:T(8,128)S(1)}, f32[184,128]{1,0:T(8,128)S(1)}, u32[]{:S(2)}, u32[]{:S(2)}) collective-permute-start(f32[184,128]{1,0:T(8,128)S(1)} %get-tuple-element.97), channel_id=1, source_target_pairs={{0,24},{8,16},{16,8},{24,0},{1,25},{9,17},{17,9},{25,1},{2,26},{10... | collective-permute-start | bytes 282632 | tf_op jit(solution)/shard_map/ppermute | solution.py:587
  (6 other events, 61.4 us)

commit v6 on v5

--- a/solution.py
+++ b/solution.py
@@ -691,7 +691,7 @@
         control.transpose(1, 0, 2).reshape(size.rows * members, size.cols),
     )
     control_own, sent = entered[0::2], entered[1::2]
-    copies = min(4, members)
+    copies = min(8, members)
     resident = call(
         load_kernel,
         pltpu.VMEM(perturbations.shape, F32),

time: 114 us -> 113 us (level)
  no operation moved by 1% of the time
where the time goes in v6:
time: 113 us
  starting transfers between devices  38.5 us (34%)
  waiting for transfers between devices  35.5 us (31%)
  blocking collectives  20.7 us (18%)
  Pallas kernels  16.8 us (15%)
    ppermute x15, waiting for transfers between devices, exchange(): lax.ppermute(parts[d], 'mem', [(i, i ^ d) for i in range(n_mem)])  26.5 us
    ppermute x15, starting transfers between devices, exchange(): lax.ppermute(parts[d], 'mem', [(i, i ^ d) for i in range(n_mem)])  22.3 us
    all_to_all x2, blocking collectives, everywhere(): lax.all_to_all(tile.reshape(devices, 1, LANES), ('mem', 'lat'), 0, 0)  20.7 us
    pallas_call x20, Pallas kernels, call(): pl.pallas_call(kernel, out_shape=outs, in_specs=[pl.BlockSpec(memory_spac...  16.8 us
    ppermute x10, starting transfers between devices, swap(): lax.ppermute(to_b, ('mem', 'lat'), cross)  11.7 us
    ppermute x10, waiting for transfers between devices, swap(): lax.ppermute(to_b, ('mem', 'lat'), cross)  8.9 us
    ppermute x10, starting transfers between devices, swap(): lax.ppermute(to_a, 'lat', pairs)  4.54 us
  transfers between devices with their start and end apart: 35, of which 16 were waited for; matrix products, arithmetic and copies ran while one was open for 0% of the time, Pallas kernels for 8%

profile of v6, /device:TPU:0, one launch (start us, length us, event | category | flops | bytes accessed | tf_op | source)
XLA Modules:
  0.0 113.2 jit_solution(10838646939802390922)
XLA Ops:
  1.8 3.1 %collective-permute-start.2 = (f32[240,128]{1,0:T(8,128)S(1)}, f32[240,128]{1,0:T(8,128)S(1)}, u32[]{:S(2)}, u32[]{:S(2)}) collective-permute-start(f32[240,128]{1,0:T(8,128)S(1)} %get-tuple-element.55), channel_id=1, source_target_pairs={{0,8},{1,2},{2,1},{3,4},{4,3},{5,6},{6,5},{7,15},{8,0},{9,10},{10,... | collective-permute-start | bytes 368648 | tf_op jit(solution)/shard_map/ppermute | solution.py:583
  5.0 1.6 %collective-permute-start = (f32[240,128]{1,0:T(8,128)S(1)}, f32[240,128]{1,0:T(8,128)S(1)}, u32[]{:S(2)}, u32[]{:S(2)}) collective-permute-start(f32[240,128]{1,0:T(8,128)S(1)} %get-tuple-element.53), channel_id=1, source_target_pairs={{0,8},{1,2},{2,1},{3,4},{4,3},{5,6},{6,5},{7,15},{8,0},{9,10},{10,... | collective-permute-start | bytes 368648 | tf_op jit(solution)/shard_map/ppermute | solution.py:583
  6.6 2.8 %shard_map.59.pert_ref.refs_0_ = f32[32,3,24,1280]{3,2,1,0:T(8,128)S(1)} custom-call(bf16[32,3,24,1280]{3,2,1,0:T(8,128)(2,1)} %pert_ref.1), custom_call_target="tpu_custom_call" | custom-call | flops 1006632960 | bytes 5898240 | tf_op jit(solution)/shard_map/pallas_call | solution.py:551
  11.6 3.7 %collective-permute-start.4 = (f32[184,128]{1,0:T(8,128)S(1)}, f32[184,128]{1,0:T(8,128)S(1)}, u32[]{:S(2)}, u32[]{:S(2)}) collective-permute-start(f32[184,128]{1,0:T(8,128)S(1)} %get-tuple-element.57), channel_id=1, source_target_pairs={{0,24},{8,16},{16,8},{24,0},{1,25},{9,17},{17,9},{25,1},{2,26},{10... | collective-permute-start | bytes 282632 | tf_op jit(solution)/shard_map/ppermute | solution.py:587
  16.1 3.0 %collective-permute-done.4.refs_1_ = f32[184,128]{1,0:T(8,128)S(1)} collective-permute-done((f32[184,128]{1,0:T(8,128)S(1)}, f32[184,128]{1,0:T(8,128)S(1)}, u32[]{:S(2)}, u32[]{:S(2)}) %collective-permute-start.4) | collective-permute-done | bytes 94240 | tf_op jit(solution)/shard_map/ppermute | solution.py:587
  19.1 4.7 %collective-permute-done.5.refs_2_ = f32[184,128]{1,0:T(8,128)S(1)} collective-permute-done((f32[184,128]{1,0:T(8,128)S(1)}, f32[184,128]{1,0:T(8,128)S(1)}, u32[]{:S(2)}, u32[]{:S(2)}) %collective-permute-start.5) | collective-permute-done | bytes 94240 | tf_op jit(solution)/shard_map/ppermute | solution.py:587
  23.8 2.7 %collective-permute-start.7 = (f32[184,128]{1,0:T(8,128)S(1)}, f32[184,128]{1,0:T(8,128)S(1)}, u32[]{:S(2)}, u32[]{:S(2)}) collective-permute-start(f32[184,128]{1,0:T(8,128)S(1)} %shard_map.63.refs_1_), channel_id=1, source_target_pairs={{0,24},{8,16},{16,8},{24,0},{1,25},{9,17},{17,9},{25,1},{2,26},{10... | collective-permute-start | bytes 282632 | tf_op jit(solution)/shard_map/ppermute | solution.py:587
  26.5 1.7 %collective-permute-start.9 = (f32[184,128]{1,0:T(8,128)S(1)}, f32[184,128]{1,0:T(8,128)S(1)}, u32[]{:S(2)}, u32[]{:S(2)}) collective-permute-start(f32[184,128]{1,0:T(8,128)S(1)} %shard_map.63.refs_1_), channel_id=1, source_target_pairs={{0,8},{8,0},{16,24},{24,16},{1,9},{9,1},{17,25},{25,17},{2,10},{10... | collective-permute-start | bytes 282632 | tf_op jit(solution)/shard_map/ppermute | solution.py:587
  28.3 2.9 %collective-permute-done.7.refs_2_ = f32[184,128]{1,0:T(8,128)S(1)} collective-permute-done((f32[184,128]{1,0:T(8,128)S(1)}, f32[184,128]{1,0:T(8,128)S(1)}, u32[]{:S(2)}, u32[]{:S(2)}) %collective-permute-start.7) | collective-permute-done | bytes 94240 | tf_op jit(solution)/shard_map/ppermute | solution.py:587
  31.1 3.0 %collective-permute-done.8.refs_3_ = f32[184,128]{1,0:T(8,128)S(1)} collective-permute-done((f32[184,128]{1,0:T(8,128)S(1)}, f32[184,128]{1,0:T(8,128)S(1)}, u32[]{:S(2)}, u32[]{:S(2)}) %collective-permute-start.8) | collective-permute-done | bytes 94240 | tf_op jit(solution)/shard_map/ppermute | solution.py:587
  34.2 1.3 %shard_map.64 = (f32[240,128]{1,0:T(8,128)S(1)}, f32[240,128]{1,0:T(8,128)S(1)}, f32[96,384]{1,0:T(8,128)S(1)}, f32[736,128]{1,0:T(8,128)S(1)}, f32[736,128]{1,0:T(8,128)S(1)}) custom-call(f32[32,3,24,1280]{3,2,1,0:T(8,128)S(1)} %shard_map.59.pert_ref.refs_0_, f32[184,128]{1,0:T(8,128)S(1)} %shard_map.63.refs_1_, ...), custom_call_target="tpu_custom_call" | custom-call | flops 503316480 | bytes 12541964 | tf_op jit(solution)/shard_map/pallas_call | solution.py:551
  36.4 1.6 %collective-permute-start.15 = (f32[240,128]{1,0:T(8,128)S(1)}, f32[240,128]{1,0:T(8,128)S(1)}, u32[]{:S(2)}, u32[]{:S(2)}) collective-permute-start(f32[240,128]{1,0:T(8,128)S(1)} %get-tuple-element.68), channel_id=1, source_target_pairs={{0,1},{1,0},{2,3},{3,2},{4,5},{5,4},{6,7},{7,6},{8,9},{9,8},{10,11... | collective-permute-start | bytes 368648 | tf_op jit(solution)/shard_map/ppermute | solution.py:583
  38.0 1.2 %shard_map.65 = (f32[240,128]{1,0:T(8,128)S(1)}, f32[240,128]{1,0:T(8,128)S(1)}, f32[96,384]{1,0:T(8,128)S(1)}) custom-call(f32[32,3,24,1280]{3,2,1,0:T(8,128)S(1)} %shard_map.59.pert_ref.refs_0_, f32[736,128]{1,0:T(8,128)S(1)} %get-tuple-element.60.refs_1_), custom_call_target="tpu_custom_call" | custom-call | flops 503316480 | bytes 12173312 | tf_op jit(solution)/shard_map/pallas_call | solution.py:551
  42.6 1.6 %collective-permute-done.10.refs_1_ = f32[240,128]{1,0:T(8,128)S(1)} collective-permute-done((f32[240,128]{1,0:T(8,128)S(1)}, f32[240,128]{1,0:T(8,128)S(1)}, u32[]{:S(2)}, u32[]{:S(2)}) %collective-permute-start.10) | collective-permute-done | bytes 122912 | tf_op jit(solution)/shard_map/ppermute | solution.py:583
  46.6 2.7 %collective-permute-done.12.b_ref = f32[240,128]{1,0:T(8,128)S(1)} collective-permute-done((f32[240,128]{1,0:T(8,128)S(1)}, f32[240,128]{1,0:T(8,128)S(1)}, u32[]{:S(2)}, u32[]{:S(2)}) %collective-permute-start.12) | collective-permute-done | bytes 122912 | tf_op jit(solution)/shard_map/ppermute | solution.py:583
  51.2 2.1 %collective-permute-start.19 = (f32[184,128]{1,0:T(8,128)S(1)}, f32[184,128]{1,0:T(8,128)S(1)}, u32[]{:S(2)}, u32[]{:S(2)}) collective-permute-start(f32[184,128]{1,0:T(8,128)S(1)} %get-tuple-element.73), channel_id=1, source_target_pairs={{0,8},{8,0},{16,24},{24,16},{1,9},{9,1},{17,25},{25,17},{2,10},{10... | collective-permute-start | bytes 282632 | tf_op jit(solution)/shard_map/ppermute | solution.py:587
  53.3 1.6 %collective-permute-start.20 = (f32[184,128]{1,0:T(8,128)S(1)}, f32[184,128]{1,0:T(8,128)S(1)}, u32[]{:S(2)}, u32[]{:S(2)}) collective-permute-start(f32[184,128]{1,0:T(8,128)S(1)} %get-tuple-element.74), channel_id=1, source_target_pairs={{0,24},{8,16},{16,8},{24,0},{1,25},{9,17},{17,9},{25,1},{2,26},{10... | collective-permute-start | bytes 282632 | tf_op jit(solution)/shard_map/ppermute | solution.py:587
  54.9 4.2 %collective-permute-done.18.refs_1_ = f32[184,128]{1,0:T(8,128)S(1)} collective-permute-done((f32[184,128]{1,0:T(8,128)S(1)}, f32[184,128]{1,0:T(8,128)S(1)}, u32[]{:S(2)}, u32[]{:S(2)}) %collective-permute-start.18) | collective-permute-done | bytes 94240 | tf_op jit(solution)/shard_map/ppermute | solution.py:587
  59.0 1.8 %collective-permute-done.20.refs_3_ = f32[184,128]{1,0:T(8,128)S(1)} collective-permute-done((f32[184,128]{1,0:T(8,128)S(1)}, f32[184,128]{1,0:T(8,128)S(1)}, u32[]{:S(2)}, u32[]{:S(2)}) %collective-permute-start.20) | collective-permute-done | bytes 94240 | tf_op jit(solution)/shard_map/ppermute | solution.py:587
  61.0 2.0 %collective-permute-start.21 = (f32[184,128]{1,0:T(8,128)S(1)}, f32[184,128]{1,0:T(8,128)S(1)}, u32[]{:S(2)}, u32[]{:S(2)}) collective-permute-start(f32[184,128]{1,0:T(8,128)S(1)} %get-tuple-element.75.refs_1_), channel_id=1, source_target_pairs={{0,24},{8,16},{16,8},{24,0},{1,25},{9,17},{17,9},{25,1},{2,26},{10... | collective-permute-start | bytes 282632 | tf_op jit(solution)/shard_map/ppermute | solution.py:587
  63.0 1.8 %collective-permute-start.22 = (f32[184,128]{1,0:T(8,128)S(1)}, f32[184,128]{1,0:T(8,128)S(1)}, u32[]{:S(2)}, u32[]{:S(2)}) collective-permute-start(f32[184,128]{1,0:T(8,128)S(1)} %get-tuple-element.75.refs_1_), channel_id=1, source_target_pairs={{0,16},{8,24},{16,0},{24,8},{1,17},{9,25},{17,1},{25,9},{2,18},{10... | collective-permute-start | bytes 282632 | tf_op jit(solution)/shard_map/ppermute | solution.py:587
  65.5 10.4 %all_to_all.10 = f32[32,1,128]{2,1,0:T(1,128)S(1)} all-to-all(f32[32,1,128]{2,1,0:T(1,128)S(1)} %bitcast.21), channel_id=1, replica_groups=mesh['mem'=4,'lat'=8] {'mem','lat'}, dimensions={0} | all-to-all | bytes 32768 | tf_op jit(solution)/shard_map/all_to_all | solution.py:682
  75.9 1.3 %shard_map.71 = (f32[240,128]{1,0:T(8,128)S(1)}, f32[240,128]{1,0:T(8,128)S(1)}, f32[96,384]{1,0:T(8,128)S(1)}, f32[736,128]{1,0:T(8,128)S(1)}, f32[736,128]{1,0:T(8,128)S(1)}) custom-call(f32[32,3,24,1280]{3,2,1,0:T(8,128)S(1)} %shard_map.59.pert_ref.refs_0_, f32[184,128]{1,0:T(8,128)S(1)} %get-tuple-element.75.refs_1_, ...), custom_call_target="tpu_custom_call" | custom-call | flops 503316480 | bytes 12935180 | tf_op jit(solution)/shard_map/pallas_call | solution.py:551
  78.0 1.2 %shard_map.73 = (f32[240,128]{1,0:T(8,128)S(1)}, f32[240,128]{1,0:T(8,128)S(1)}, f32[96,384]{1,0:T(8,128)S(1)}) custom-call(f32[32,3,24,1280]{3,2,1,0:T(8,128)S(1)} %shard_map.59.pert_ref.refs_0_, f32[736,128]{1,0:T(8,128)S(1)} %get-tuple-element.82.refs_1_), custom_call_target="tpu_custom_call" | custom-call | flops 503316480 | bytes 12173312 | tf_op jit(solution)/shard_map/pallas_call | solution.py:551
  79.2 1.4 %collective-permute-start.26 = (f32[240,128]{1,0:T(8,128)S(1)}, f32[240,128]{1,0:T(8,128)S(1)}, u32[]{:S(2)}, u32[]{:S(2)}) collective-permute-start(f32[240,128]{1,0:T(8,128)S(1)} %get-tuple-element.84), channel_id=1, source_target_pairs={{0,8},{1,2},{2,1},{3,4},{4,3},{5,6},{6,5},{7,15},{8,0},{9,10},{10,... | collective-permute-start | bytes 368648 | tf_op jit(solution)/shard_map/ppermute | solution.py:583
  80.9 1.4 %collective-permute-done.24.refs_1_ = f32[240,128]{1,0:T(8,128)S(1)} collective-permute-done((f32[240,128]{1,0:T(8,128)S(1)}, f32[240,128]{1,0:T(8,128)S(1)}, u32[]{:S(2)}, u32[]{:S(2)}) %collective-permute-start.24) | collective-permute-done | bytes 122912 | tf_op jit(solution)/shard_map/ppermute | solution.py:583
  84.3 1.4 %collective-permute-start.30 = (f32[240,128]{1,0:T(8,128)S(1)}, f32[240,128]{1,0:T(8,128)S(1)}, u32[]{:S(2)}, u32[]{:S(2)}) collective-permute-start(f32[240,128]{1,0:T(8,128)S(1)} %get-tuple-element.92.refs_5_), channel_id=1, source_target_pairs={{0,8},{1,2},{2,1},{3,4},{4,3},{5,6},{6,5},{7,15},{8,0},{9,10},{10,... | collective-permute-start | bytes 368648 | tf_op jit(solution)/shard_map/ppermute | solution.py:583
  91.1 1.4 %collective-permute-start.33 = (f32[184,128]{1,0:T(8,128)S(1)}, f32[184,128]{1,0:T(8,128)S(1)}, u32[]{:S(2)}, u32[]{:S(2)}) collective-permute-start(f32[184,128]{1,0:T(8,128)S(1)} %get-tuple-element.96), channel_id=1, source_target_pairs={{0,8},{8,0},{16,24},{24,16},{1,9},{9,1},{17,25},{25,17},{2,10},{10... | collective-permute-start | bytes 282632 | tf_op jit(solution)/shard_map/ppermute | solution.py:587
  92.5 2.4 %collective-permute-start.34 = (f32[184,128]{1,0:T(8,128)S(1)}, f32[184,128]{1,0:T(8,128)S(1)}, u32[]{:S(2)}, u32[]{:S(2)}) collective-permute-start(f32[184,128]{1,0:T(8,128)S(1)} %get-tuple-element.97), channel_id=1, source_target_pairs={{0,24},{8,16},{16,8},{24,0},{1,25},{9,17},{17,9},{25,1},{2,26},{10... | collective-permute-start | bytes 282632 | tf_op jit(solution)/shard_map/ppermute | solution.py:587
  94.9 3.2 %collective-permute-done.32.refs_1_ = f32[184,128]{1,0:T(8,128)S(1)} collective-permute-done((f32[184,128]{1,0:T(8,128)S(1)}, f32[184,128]{1,0:T(8,128)S(1)}, u32[]{:S(2)}, u32[]{:S(2)}) %collective-permute-start.32) | collective-permute-done | bytes 94240 | tf_op jit(solution)/shard_map/ppermute | solution.py:587
  98.1 3.7 %collective-permute-done.34.refs_3_ = f32[184,128]{1,0:T(8,128)S(1)} collective-permute-done((f32[184,128]{1,0:T(8,128)S(1)}, f32[184,128]{1,0:T(8,128)S(1)}, u32[]{:S(2)}, u32[]{:S(2)}) %collective-permute-start.34) | collective-permute-done | bytes 94240 | tf_op jit(solution)/shard_map/ppermute | solution.py:587
  102.0 10.2 %all_to_all.11 = f32[32,1,128]{2,1,0:T(1,128)S(1)} all-to-all(f32[32,1,128]{2,1,0:T(1,128)S(1)} %bitcast.22), channel_id=1, replica_groups=mesh['mem'=4,'lat'=8] {'mem','lat'}, dimensions={0} | all-to-all | bytes 32768 | tf_op jit(solution)/shard_map/all_to_all | solution.py:682
  (66 shorter events, 23.1 us)
Async XLA Ops:
  1.8 7.6 %collective-permute-start.2 = (f32[240,128]{1,0:T(8,128)S(1)}, f32[240,128]{1,0:T(8,128)S(1)}, u32[]{:S(2)}, u32[]{:S(2)}) collective-permute-start(f32[240,128]{1,0:T(8,128)S(1)} %get-tuple-element.55), channel_id=1, source_target_pairs={{0,8},{1,2},{2,1},{3,4},{4,3},{5,6},{6,5},{7,15},{8,0},{9,10},{10,... | collective-permute-start | bytes 368648 | tf_op jit(solution)/shard_map/ppermute | solution.py:583
  4.9 4.5 %collective-permute-start.3 = (f32[240,128]{1,0:T(8,128)S(1)}, f32[240,128]{1,0:T(8,128)S(1)}, u32[]{:S(2)}, u32[]{:S(2)}) collective-permute-start(f32[240,128]{1,0:T(8,128)S(1)} %get-tuple-element.55), channel_id=1, source_target_pairs={{0,1},{1,0},{2,3},{3,2},{4,5},{5,4},{6,7},{7,6},{8,9},{9,8},{10,11... | collective-permute-start | bytes 368648 | tf_op jit(solution)/shard_map/ppermute | solution.py:583
  5.0 5.6 %collective-permute-start = (f32[240,128]{1,0:T(8,128)S(1)}, f32[240,128]{1,0:T(8,128)S(1)}, u32[]{:S(2)}, u32[]{:S(2)}) collective-permute-start(f32[240,128]{1,0:T(8,128)S(1)} %get-tuple-element.53), channel_id=1, source_target_pairs={{0,8},{1,2},{2,1},{3,4},{4,3},{5,6},{6,5},{7,15},{8,0},{9,10},{10,... | collective-permute-start | bytes 368648 | tf_op jit(solution)/shard_map/ppermute | solution.py:583
  11.6 7.5 %collective-permute-start.4 = (f32[184,128]{1,0:T(8,128)S(1)}, f32[184,128]{1,0:T(8,128)S(1)}, u32[]{:S(2)}, u32[]{:S(2)}) collective-permute-start(f32[184,128]{1,0:T(8,128)S(1)} %get-tuple-element.57), channel_id=1, source_target_pairs={{0,24},{8,16},{16,8},{24,0},{1,25},{9,17},{17,9},{25,1},{2,26},{10... | collective-permute-start | bytes 282632 | tf_op jit(solution)/shard_map/ppermute | solution.py:587
  15.3 8.5 %collective-permute-start.5 = (f32[184,128]{1,0:T(8,128)S(1)}, f32[184,128]{1,0:T(8,128)S(1)}, u32[]{:S(2)}, u32[]{:S(2)}) collective-permute-start(f32[184,128]{1,0:T(8,128)S(1)} %get-tuple-element.58), channel_id=1, source_target_pairs={{0,16},{8,24},{16,0},{24,8},{1,17},{9,25},{17,1},{25,9},{2,18},{10... | collective-permute-start | bytes 282632 | tf_op jit(solution)/shard_map/ppermute | solution.py:587
  15.3 8.5 %collective-permute-start.6 = (f32[184,128]{1,0:T(8,128)S(1)}, f32[184,128]{1,0:T(8,128)S(1)}, u32[]{:S(2)}, u32[]{:S(2)}) collective-permute-start(f32[184,128]{1,0:T(8,128)S(1)} %get-tuple-element.59), channel_id=1, source_target_pairs={{0,8},{8,0},{16,24},{24,16},{1,9},{9,1},{17,25},{25,17},{2,10},{10... | collective-permute-start | bytes 282632 | tf_op jit(solution)/shard_map/ppermute | solution.py:587
  23.8 7.3 %collective-permute-start.7 = (f32[184,128]{1,0:T(8,128)S(1)}, f32[184,128]{1,0:T(8,128)S(1)}, u32[]{:S(2)}, u32[]{:S(2)}) collective-permute-start(f32[184,128]{1,0:T(8,128)S(1)} %shard_map.63.refs_1_), channel_id=1, source_target_pairs={{0,24},{8,16},{16,8},{24,0},{1,25},{9,17},{17,9},{25,1},{2,26},{10... | collective-permute-start | bytes 282632 | tf_op jit(solution)/shard_map/ppermute | solution.py:587
  26.5 7.7 %collective-permute-start.8 = (f32[184,128]{1,0:T(8,128)S(1)}, f32[184,128]{1,0:T(8,128)S(1)}, u32[]{:S(2)}, u32[]{:S(2)}) collective-permute-start(f32[184,128]{1,0:T(8,128)S(1)} %shard_map.63.refs_1_), channel_id=1, source_target_pairs={{0,16},{8,24},{16,0},{24,8},{1,17},{9,25},{17,1},{25,9},{2,18},{10... | collective-permute-start | bytes 282632 | tf_op jit(solution)/shard_map/ppermute | solution.py:587
  26.5 7.7 %collective-permute-start.9 = (f32[184,128]{1,0:T(8,128)S(1)}, f32[184,128]{1,0:T(8,128)S(1)}, u32[]{:S(2)}, u32[]{:S(2)}) collective-permute-start(f32[184,128]{1,0:T(8,128)S(1)} %shard_map.63.refs_1_), channel_id=1, source_target_pairs={{0,8},{8,0},{16,24},{24,16},{1,9},{9,1},{17,25},{25,17},{2,10},{10... | collective-permute-start | bytes 282632 | tf_op jit(solution)/shard_map/ppermute | solution.py:587
  35.5 4.9 %collective-permute-start.14 = (f32[240,128]{1,0:T(8,128)S(1)}, f32[240,128]{1,0:T(8,128)S(1)}, u32[]{:S(2)}, u32[]{:S(2)}) collective-permute-start(f32[240,128]{1,0:T(8,128)S(1)} %get-tuple-element.67), channel_id=1, source_target_pairs={{0,8},{1,2},{2,1},{3,4},{4,3},{5,6},{6,5},{7,15},{8,0},{9,10},{10,... | collective-permute-start | bytes 368648 | tf_op jit(solution)/shard_map/ppermute | solution.py:583
  36.4 4.1 %collective-permute-start.15 = (f32[240,128]{1,0:T(8,128)S(1)}, f32[240,128]{1,0:T(8,128)S(1)}, u32[]{:S(2)}, u32[]{:S(2)}) collective-permute-start(f32[240,128]{1,0:T(8,128)S(1)} %get-tuple-element.68), channel_id=1, source_target_pairs={{0,1},{1,0},{2,3},{3,2},{4,5},{5,4},{6,7},{7,6},{8,9},{9,8},{10,11... | collective-permute-start | bytes 368648 | tf_op jit(solution)/shard_map/ppermute | solution.py:583
  39.3 4.9 %collective-permute-start.10 = (f32[240,128]{1,0:T(8,128)S(1)}, f32[240,128]{1,0:T(8,128)S(1)}, u32[]{:S(2)}, u32[]{:S(2)}) collective-permute-start(f32[240,128]{1,0:T(8,128)S(1)} %get-tuple-element.62), channel_id=1, source_target_pairs={{0,8},{1,2},{2,1},{3,4},{4,3},{5,6},{6,5},{7,15},{8,0},{9,10},{10,... | collective-permute-start | bytes 368648 | tf_op jit(solution)/shard_map/ppermute | solution.py:583
  39.8 4.4 %collective-permute-start.11 = (f32[240,128]{1,0:T(8,128)S(1)}, f32[240,128]{1,0:T(8,128)S(1)}, u32[]{:S(2)}, u32[]{:S(2)}) collective-permute-start(f32[240,128]{1,0:T(8,128)S(1)} %get-tuple-element.63), channel_id=1, source_target_pairs={{0,1},{1,0},{2,3},{3,2},{4,5},{5,4},{6,7},{7,6},{8,9},{9,8},{10,11... | collective-permute-start | bytes 368648 | tf_op jit(solution)/shard_map/ppermute | solution.py:583
  40.7 4.9 %collective-permute-start.16 = (f32[240,128]{1,0:T(8,128)S(1)}, f32[240,128]{1,0:T(8,128)S(1)}, u32[]{:S(2)}, u32[]{:S(2)}) collective-permute-start(f32[240,128]{1,0:T(8,128)S(1)} %get-tuple-element.70.refs_4_), channel_id=1, source_target_pairs={{0,8},{1,2},{2,1},{3,4},{4,3},{5,6},{6,5},{7,15},{8,0},{9,10},{10,... | collective-permute-start | bytes 368648 | tf_op jit(solution)/shard_map/ppermute | solution.py:583
  41.6 4.0 %collective-permute-start.17 = (f32[240,128]{1,0:T(8,128)S(1)}, f32[240,128]{1,0:T(8,128)S(1)}, u32[]{:S(2)}, u32[]{:S(2)}) collective-permute-start(f32[240,128]{1,0:T(8,128)S(1)} %get-tuple-element.70.refs_4_), channel_id=1, source_target_pairs={{0,1},{1,0},{2,3},{3,2},{4,5},{5,4},{6,7},{7,6},{8,9},{9,8},{10,11... | collective-permute-start | bytes 368648 | tf_op jit(solution)/shard_map/ppermute | solution.py:583
  44.4 4.9 %collective-permute-start.12 = (f32[240,128]{1,0:T(8,128)S(1)}, f32[240,128]{1,0:T(8,128)S(1)}, u32[]{:S(2)}, u32[]{:S(2)}) collective-permute-start(f32[240,128]{1,0:T(8,128)S(1)} %get-tuple-element.65.refs_5_), channel_id=1, source_target_pairs={{0,8},{1,2},{2,1},{3,4},{4,3},{5,6},{6,5},{7,15},{8,0},{9,10},{10,... | collective-permute-start | bytes 368648 | tf_op jit(solution)/shard_map/ppermute | solution.py:583
  44.9 4.4 %collective-permute-start.13 = (f32[240,128]{1,0:T(8,128)S(1)}, f32[240,128]{1,0:T(8,128)S(1)}, u32[]{:S(2)}, u32[]{:S(2)}) collective-permute-start(f32[240,128]{1,0:T(8,128)S(1)} %get-tuple-element.65.refs_5_), channel_id=1, source_target_pairs={{0,1},{1,0},{2,3},{3,2},{4,5},{5,4},{6,7},{7,6},{8,9},{9,8},{10,11... | collective-permute-start | bytes 368648 | tf_op jit(solution)/shard_map/ppermute | solution.py:583
  50.4 8.6 %collective-permute-start.18 = (f32[184,128]{1,0:T(8,128)S(1)}, f32[184,128]{1,0:T(8,128)S(1)}, u32[]{:S(2)}, u32[]{:S(2)}) collective-permute-start(f32[184,128]{1,0:T(8,128)S(1)} %get-tuple-element.72), channel_id=1, source_target_pairs={{0,16},{8,24},{16,0},{24,8},{1,17},{9,25},{17,1},{25,9},{2,18},{10... | collective-permute-start | bytes 282632 | tf_op jit(solution)/shard_map/ppermute | solution.py:587
  51.2 7.8 %collective-permute-start.19 = (f32[184,128]{1,0:T(8,128)S(1)}, f32[184,128]{1,0:T(8,128)S(1)}, u32[]{:S(2)}, u32[]{:S(2)}) collective-permute-start(f32[184,128]{1,0:T(8,128)S(1)} %get-tuple-element.73), channel_id=1, source_target_pairs={{0,8},{8,0},{16,24},{24,16},{1,9},{9,1},{17,25},{25,17},{2,10},{10... | collective-permute-start | bytes 282632 | tf_op jit(solution)/shard_map/ppermute | solution.py:587
  53.3 7.6 %collective-permute-start.20 = (f32[184,128]{1,0:T(8,128)S(1)}, f32[184,128]{1,0:T(8,128)S(1)}, u32[]{:S(2)}, u32[]{:S(2)}) collective-permute-start(f32[184,128]{1,0:T(8,128)S(1)} %get-tuple-element.74), channel_id=1, source_target_pairs={{0,24},{8,16},{16,8},{24,0},{1,25},{9,17},{17,9},{25,1},{2,26},{10... | collective-permute-start | bytes 282632 | tf_op jit(solution)/shard_map/ppermute | solution.py:587
  61.0 14.9 %collective-permute-start.21 = (f32[184,128]{1,0:T(8,128)S(1)}, f32[184,128]{1,0:T(8,128)S(1)}, u32[]{:S(2)}, u32[]{:S(2)}) collective-permute-start(f32[184,128]{1,0:T(8,128)S(1)} %get-tuple-element.75.refs_1_), channel_id=1, source_target_pairs={{0,24},{8,16},{16,8},{24,0},{1,25},{9,17},{17,9},{25,1},{2,26},{10... | collective-permute-start | bytes 282632 | tf_op jit(solution)/shard_map/ppermute | solution.py:587
  63.0 12.9 %collective-permute-start.22 = (f32[184,128]{1,0:T(8,128)S(1)}, f32[184,128]{1,0:T(8,128)S(1)}, u32[]{:S(2)}, u32[]{:S(2)}) collective-permute-start(f32[184,128]{1,0:T(8,128)S(1)} %get-tuple-element.75.refs_1_), channel_id=1, source_target_pairs={{0,16},{8,24},{16,0},{24,8},{1,17},{9,25},{17,1},{25,9},{2,18},{10... | collective-permute-start | bytes 282632 | tf_op jit(solution)/shard_map/ppermute | solution.py:587
  64.8 11.1 %collective-permute-start.23 = (f32[184,128]{1,0:T(8,128)S(1)}, f32[184,128]{1,0:T(8,128)S(1)}, u32[]{:S(2)}, u32[]{:S(2)}) collective-permute-start(f32[184,128]{1,0:T(8,128)S(1)} %get-tuple-element.75.refs_1_), channel_id=1, source_target_pairs={{0,8},{8,0},{16,24},{24,16},{1,9},{9,1},{17,25},{25,17},{2,10},{10... | collective-permute-start | bytes 282632 | tf_op jit(solution)/shard_map/ppermute | solution.py:587
  77.3 4.9 %collective-permute-start.24 = (f32[240,128]{1,0:T(8,128)S(1)}, f32[240,128]{1,0:T(8,128)S(1)}, u32[]{:S(2)}, u32[]{:S(2)}) collective-permute-start(f32[240,128]{1,0:T(8,128)S(1)} %get-tuple-element.79), channel_id=1, source_target_pairs={{0,8},{1,2},{2,1},{3,4},{4,3},{5,6},{6,5},{7,15},{8,0},{9,10},{10,... | collective-permute-start | bytes 368648 | tf_op jit(solution)/shard_map/ppermute | solution.py:583
  77.9 4.3 %collective-permute-start.25 = (f32[240,128]{1,0:T(8,128)S(1)}, f32[240,128]{1,0:T(8,128)S(1)}, u32[]{:S(2)}, u32[]{:S(2)}) collective-permute-start(f32[240,128]{1,0:T(8,128)S(1)} %get-tuple-element.80), channel_id=1, source_target_pairs={{0,1},{1,0},{2,3},{3,2},{4,5},{5,4},{6,7},{7,6},{8,9},{9,8},{10,11... | collective-permute-start | bytes 368648 | tf_op jit(solution)/shard_map/ppermute | solution.py:583
  79.2 4.9 %collective-permute-start.26 = (f32[240,128]{1,0:T(8,128)S(1)}, f32[240,128]{1,0:T(8,128)S(1)}, u32[]{:S(2)}, u32[]{:S(2)}) collective-permute-start(f32[240,128]{1,0:T(8,128)S(1)} %get-tuple-element.84), channel_id=1, source_target_pairs={{0,8},{1,2},{2,1},{3,4},{4,3},{5,6},{6,5},{7,15},{8,0},{9,10},{10,... | collective-permute-start | bytes 368648 | tf_op jit(solution)/shard_map/ppermute | solution.py:583
  82.4 4.9 %collective-permute-start.28 = (f32[240,128]{1,0:T(8,128)S(1)}, f32[240,128]{1,0:T(8,128)S(1)}, u32[]{:S(2)}, u32[]{:S(2)}) collective-permute-start(f32[240,128]{1,0:T(8,128)S(1)} %get-tuple-element.89.refs_4_), channel_id=1, source_target_pairs={{0,8},{1,2},{2,1},{3,4},{4,3},{5,6},{6,5},{7,15},{8,0},{9,10},{10,... | collective-permute-start | bytes 368648 | tf_op jit(solution)/shard_map/ppermute | solution.py:583
  83.1 4.3 %collective-permute-start.29 = (f32[240,128]{1,0:T(8,128)S(1)}, f32[240,128]{1,0:T(8,128)S(1)}, u32[]{:S(2)}, u32[]{:S(2)}) collective-permute-start(f32[240,128]{1,0:T(8,128)S(1)} %get-tuple-element.89.refs_4_), channel_id=1, source_target_pairs={{0,1},{1,0},{2,3},{3,2},{4,5},{5,4},{6,7},{7,6},{8,9},{9,8},{10,11... | collective-permute-start | bytes 368648 | tf_op jit(solution)/shard_map/ppermute | solution.py:583
  84.3 4.9 %collective-permute-start.30 = (f32[240,128]{1,0:T(8,128)S(1)}, f32[240,128]{1,0:T(8,128)S(1)}, u32[]{:S(2)}, u32[]{:S(2)}) collective-permute-start(f32[240,128]{1,0:T(8,128)S(1)} %get-tuple-element.92.refs_5_), channel_id=1, source_target_pairs={{0,8},{1,2},{2,1},{3,4},{4,3},{5,6},{6,5},{7,15},{8,0},{9,10},{10,... | collective-permute-start | bytes 368648 | tf_op jit(solution)/shard_map/ppermute | solution.py:583
  90.4 7.7 %collective-permute-start.32 = (f32[184,128]{1,0:T(8,128)S(1)}, f32[184,128]{1,0:T(8,128)S(1)}, u32[]{:S(2)}, u32[]{:S(2)}) collective-permute-start(f32[184,128]{1,0:T(8,128)S(1)} %get-tuple-element.95), channel_id=1, source_target_pairs={{0,16},{8,24},{16,0},{24,8},{1,17},{9,25},{17,1},{25,9},{2,18},{10... | collective-permute-start | bytes 282632 | tf_op jit(solution)/shard_map/ppermute | solution.py:587
  91.1 7.0 %collective-permute-start.33 = (f32[184,128]{1,0:T(8,128)S(1)}, f32[184,128]{1,0:T(8,128)S(1)}, u32[]{:S(2)}, u32[]{:S(2)}) collective-permute-start(f32[184,128]{1,0:T(8,128)S(1)} %get-tuple-element.96), channel_id=1, source_target_pairs={{0,8},{8,0},{16,24},{24,16},{1,9},{9,1},{17,25},{25,17},{2,10},{10... | collective-permute-start | bytes 282632 | tf_op jit(solution)/shard_map/ppermute | solution.py:587
  92.5 9.3 %collective-permute-start.34 = (f32[184,128]{1,0:T(8,128)S(1)}, f32[184,128]{1,0:T(8,128)S(1)}, u32[]{:S(2)}, u32[]{:S(2)}) collective-permute-start(f32[184,128]{1,0:T(8,128)S(1)} %get-tuple-element.97), channel_id=1, source_target_pairs={{0,24},{8,16},{16,8},{24,0},{1,25},{9,17},{17,9},{25,1},{2,26},{10... | collective-permute-start | bytes 282632 | tf_op jit(solution)/shard_map/ppermute | solution.py:587
  (6 other events, 61.4 us)
